TPU v7x, 32 devices: a whole 2x2x4 slice. The times are simulated.
32 devices in a mesh: dp: 16 (over z, y, core), tensor: 2 (over x).
Axes of the slice: x: 2, y: 2, z: 4, core: 2. Of those that a mesh axis runs over, the one named last changes fastest.
Arguments:
- tokens: bfloat16 [21760, 1024], P(('dp', 'tensor')), may hold values from -6 to 6
- condition: bfloat16 [32, 1024], P('dp'), may hold values from -6 to 6
- scale_lens: int32 [32, 10], P('dp'), may hold values from 1 to 256, 680 in all within a row
- qkv_weight: bfloat16 [1024, 3, 1024], P('dp', None, 'tensor'), may hold values from -0.1875 to 0.1875
- qv_bias: bfloat16 [2, 1024], P(None, 'tensor'), may hold values from -3 to 3
- head_scale: float32 [16], P('tensor'), may hold values from 8 to 24
- proj_weight: bfloat16 [1024, 1024], P('tensor', 'dp'), may hold values from -0.75 to 0.75
- proj_bias: bfloat16 [1024], P('dp'), may hold values from -3 to 3
- fc1_weight: bfloat16 [1024, 4096], P('dp', 'tensor'), may hold values from -0.1875 to 0.1875
- fc1_bias: bfloat16 [4096], P('tensor'), may hold values from -3 to 3
- fc2_weight: bfloat16 [4096, 1024], P('tensor', 'dp'), may hold values from -0.09375 to 0.09375
- fc2_bias: bfloat16 [1024], P('dp'), may hold values from -3 to 3
- ada_weight: bfloat16 [1024, 6, 1024], P('dp', None, 'tensor'), may hold values from -0.1875 to 0.1875
- ada_bias: bfloat16 [6, 1024], P(None, 'tensor'), may hold values from -2 to 2
- cotangent: bfloat16 [21760, 1024], P(('dp', 'tensor')), may hold values from -6 to 6
Outputs:
- mixed: bfloat16 [21760, 1024], P(('dp', 'tensor'))
- grad_tokens: bfloat16 [21760, 1024], P(('dp', 'tensor'))
- grad_condition: float32 [32, 1024], P(('dp', 'tensor'))
- grad_qkv_weight: float32 [1024, 3, 1024], P('dp', None, 'tensor')
- grad_qv_bias: float32 [2, 1024], P(None, 'tensor')
- grad_head_scale: float32 [16], P('tensor')
- grad_proj_weight: float32 [1024, 1024], P('tensor', 'dp')
- grad_proj_bias: float32 [1024], P('dp')
- grad_fc1_weight: float32 [1024, 4096], P('dp', 'tensor')
- grad_fc1_bias: float32 [4096], P('tensor')
- grad_fc2_weight: float32 [4096, 1024], P('tensor', 'dp')
- grad_fc2_bias: float32 [1024], P('dp')
- grad_ada_weight: float32 [1024, 6, 1024], P('dp', None, 'tensor')
- grad_ada_bias: float32 [6, 1024], P(None, 'tensor')
Inputs may be any that keep to these rules, and one draw needn't show every extreme that they name: `scale_lens`: the 10 lengths of each image sum to 680.
All inputs are finite; a program needn't handle non-finite values.
Results may differ from a plain program's by a relative error of at most 0.019.
Values may be sent and summed in bfloat16 or wider, within the bound.
No kernel may reach another device: no remote copies, remote signals or barrier semaphores. Data moves between devices by JAX's collectives and lax.ppermute only.
A program may use at most 256 MiB of HBM per device.

v0:
```python
import jax
import jax.numpy as jnp
from jax import lax
from jax.sharding import PartitionSpec as P

SEQ = 680


NORM_EPS = 1e-06
HEAD_EPS = 1e-06
MASKED = -1e30


def layer_norm(row_data):
    average = jnp.mean(row_data, axis=-1, keepdims=True)
    centred = row_data - average
    variance = jnp.mean(centred * centred, axis=-1, keepdims=True)
    return centred * lax.rsqrt(variance + NORM_EPS)


def modulate(row_data, scale_row, shift_row):
    return layer_norm(row_data) * (1.0 + scale_row) + shift_row


def unit_norm(values):
    return values * lax.rsqrt(jnp.sum(values * values, axis=-1, keepdims=True) + HEAD_EPS)


def head_inputs(query_raw, key_raw, scales):
    return (unit_norm(query_raw) * scales[:, None], unit_norm(key_raw))


def gelu_tanh(values):
    return jax.nn.gelu(values, approximate=True)


def scale_ids(lengths, seq_len):
    bounds = jnp.cumsum(lengths)
    places = jnp.arange(seq_len, dtype=jnp.int32)
    return jnp.sum((places[:, None] >= bounds[None, :]).astype(jnp.int32), axis=1)


def masked_scores(queries, key_rows, lengths):
    scale_of = scale_ids(lengths, queries.shape[0])
    allowed = scale_of[None, :] <= scale_of[:, None]
    scores = jnp.einsum("qhd,khd->hqk", queries, key_rows, preferred_element_type=jnp.float32)
    return jnp.where(allowed[None], scores, MASKED)


def attend_image(operands):
    queries, key_rows, value_rows, lengths = operands
    scores = masked_scores(queries, key_rows, lengths)
    row_max = jnp.max(scores, axis=-1, keepdims=True)
    expo_terms = jnp.exp(scores - row_max)
    row_sum = jnp.sum(expo_terms, axis=-1, keepdims=True)
    probability = (expo_terms / row_sum).astype(jnp.bfloat16)
    attended = jnp.einsum(
        "hqk,khd->qhd", probability, value_rows, preferred_element_type=jnp.float32
    )
    return (attended, (row_max + jnp.log(row_sum))[..., 0])


def attend_back(operands):
    queries, key_rows, value_rows, grad_out, log_total, lengths = operands
    scores = masked_scores(queries, key_rows, lengths)
    probability = jnp.exp(scores - log_total[..., None])
    grad_value = jnp.einsum(
        "hqk,qhd->khd",
        probability.astype(jnp.bfloat16),
        grad_out,
        preferred_element_type=jnp.float32,
    )
    grad_prob = jnp.einsum("qhd,khd->hqk", grad_out, value_rows, preferred_element_type=jnp.float32)
    inner_sum = jnp.sum(probability * grad_prob, axis=-1, keepdims=True)
    grad_score = (probability * (grad_prob - inner_sum)).astype(jnp.bfloat16)
    grad_query = jnp.einsum(
        "hqk,khd->qhd", grad_score, key_rows, preferred_element_type=jnp.float32
    )
    grad_key = jnp.einsum("hqk,qhd->khd", grad_score, queries, preferred_element_type=jnp.float32)
    return (grad_query, grad_key, grad_value)


def share_rows(local_rows):
    return lax.all_gather(local_rows, "tensor", axis=0, tiled=True)


def sum_rows(inputs, weight, own_rows):

    def row_term(first_row, row_count):
        return jnp.dot(inputs, weight, preferred_element_type=jnp.float32)

    return lax.psum_scatter(
        row_term(jnp.int32(0), lax.axis_size("tensor") * own_rows),
        "tensor",
        scatter_dimension=0,
        tiled=True,
    )


def share_grads(local_rows):
    return lax.all_gather(local_rows, "tensor", axis=0, tiled=True)


def sum_grads(inputs, weight, own_rows):

    def row_term(first_row, row_count):
        return jnp.einsum("rk,dk->rd", inputs, weight, preferred_element_type=jnp.float32)

    return lax.psum_scatter(
        row_term(jnp.int32(0), lax.axis_size("tensor") * own_rows),
        "tensor",
        scatter_dimension=0,
        tiled=True,
    )


def local(
    tokens,
    condition,
    scale_lens,
    qkv_weight,
    qv_bias,
    head_scale,
    proj_weight,
    proj_bias,
    fc1_weight,
    fc1_bias,
    fc2_weight,
    fc2_bias,
    ada_weight,
    ada_bias,
    cotangent,
):
    own_rows, model_width = tokens.shape
    own_images = own_rows // SEQ
    group_images = condition.shape[0]
    group_rows = group_images * SEQ
    local_width = qkv_weight.shape[2]
    local_heads = head_scale.shape[0]
    head_width = local_width // local_heads
    per_image = (group_images, SEQ, local_heads, head_width)
    per_row = (group_rows, local_heads, head_width)
    own_shape = (own_images, SEQ, model_width)
    gathered = (
        lax.all_gather(qkv_weight, "dp", axis=0, tiled=True),
        lax.all_gather(proj_weight, "dp", axis=1, tiled=True),
        lax.all_gather(fc1_weight, "dp", axis=0, tiled=True),
        lax.all_gather(fc2_weight, "dp", axis=1, tiled=True),
        lax.all_gather(ada_weight, "dp", axis=0, tiled=True),
        lax.all_gather(proj_bias, "dp", axis=0, tiled=True),
        lax.all_gather(fc2_bias, "dp", axis=0, tiled=True),
    )
    qkv_full, proj_full, fc1_full, fc2_full, ada_full, proj_bias_full, fc2_bias_full = gathered
    cond_float = condition.astype(jnp.float32)
    cond_low = jax.nn.silu(cond_float).astype(jnp.bfloat16)
    modul_part = jnp.einsum("ic,csd->isd", cond_low, ada_full, preferred_element_type=jnp.float32)
    modul_part = modul_part + ada_bias.astype(jnp.float32)
    modulation = lax.all_to_all(modul_part, "tensor", split_axis=0, concat_axis=2, tiled=True)
    rows_float = tokens.astype(jnp.float32).reshape(own_shape)
    mixed_one = modulate(rows_float, modulation[:, 2:3], modulation[:, 4:5])
    inputs_one = share_rows(mixed_one.astype(jnp.bfloat16).reshape(own_rows, model_width))
    qkv_raw = jnp.einsum("rd,dsk->rsk", inputs_one, qkv_full, preferred_element_type=jnp.float32)
    bias_float = qv_bias.astype(jnp.float32)
    query_raw = (qkv_raw[:, 0] + bias_float[0]).reshape(per_row)
    key_raw = qkv_raw[:, 1].reshape(per_row)
    value_raw = qkv_raw[:, 2] + bias_float[1]
    query_norm, key_norm = head_inputs(query_raw, key_raw, head_scale)
    query_low = query_norm.astype(jnp.bfloat16).reshape(per_image)
    key_low = key_norm.astype(jnp.bfloat16).reshape(per_image)
    value_low = value_raw.astype(jnp.bfloat16).reshape(per_image)
    attended, log_total = lax.map(attend_image, (query_low, key_low, value_low, scale_lens))
    heads_low = attended.reshape(group_rows, local_width).astype(jnp.bfloat16)
    branch_one = sum_rows(heads_low, proj_full, own_rows)
    branch_one = (branch_one + proj_bias_full.astype(jnp.float32)).reshape(own_shape)
    middle = rows_float + modulation[:, 0:1] * branch_one
    mixed_two = modulate(middle, modulation[:, 3:4], modulation[:, 5:6])
    inputs_two = share_rows(mixed_two.astype(jnp.bfloat16).reshape(own_rows, model_width))
    hidden_pre = jnp.dot(
        inputs_two, fc1_full, preferred_element_type=jnp.float32
    ) + fc1_bias.astype(jnp.float32)
    hidden_low = gelu_tanh(hidden_pre).astype(jnp.bfloat16)
    branch_two = sum_rows(hidden_low, fc2_full, own_rows)
    branch_two = (branch_two + fc2_bias_full.astype(jnp.float32)).reshape(own_shape)
    output = middle + modulation[:, 1:2] * branch_two
    grad_out = cotangent.astype(jnp.float32).reshape(own_shape)
    grad_gamma_two = jnp.sum(grad_out * branch_two, axis=1)
    grad_branch_two = (
        (grad_out * modulation[:, 1:2]).astype(jnp.bfloat16).reshape(own_rows, model_width)
    )
    grads_two = share_grads(grad_branch_two)
    grad_fc2_bias = jnp.sum(grads_two, axis=0, dtype=jnp.float32)
    grad_fc2 = jnp.einsum("rf,rd->fd", hidden_low, grads_two, preferred_element_type=jnp.float32)
    grad_hidden = jnp.einsum("rd,fd->rf", grads_two, fc2_full, preferred_element_type=jnp.float32)
    unused, gelu_back = jax.vjp(gelu_tanh, hidden_pre)
    grad_pre = gelu_back(grad_hidden)[0].astype(jnp.bfloat16)
    grad_fc1_bias = jnp.sum(grad_pre, axis=0, dtype=jnp.float32)
    grad_fc1 = jnp.einsum("rd,rf->df", inputs_two, grad_pre, preferred_element_type=jnp.float32)
    grad_mixed_two = sum_grads(grad_pre, fc1_full, own_rows)
    grad_mixed_two = grad_mixed_two.reshape(own_shape)
    unused, norm_two_back = jax.vjp(modulate, middle, modulation[:, 3:4], modulation[:, 5:6])
    grad_middle_norm, grad_scale_two, grad_shift_two = norm_two_back(grad_mixed_two)
    grad_middle = grad_out + grad_middle_norm
    grad_gamma_one = jnp.sum(grad_middle * branch_one, axis=1)
    grad_branch_one = (
        (grad_middle * modulation[:, 0:1]).astype(jnp.bfloat16).reshape(own_rows, model_width)
    )
    grads_one = share_grads(grad_branch_one)
    grad_proj_bias = jnp.sum(grads_one, axis=0, dtype=jnp.float32)
    grad_proj = jnp.einsum("rk,rd->kd", heads_low, grads_one, preferred_element_type=jnp.float32)
    grad_heads = jnp.einsum("rd,kd->rk", grads_one, proj_full, preferred_element_type=jnp.float32)
    grad_heads = grad_heads.astype(jnp.bfloat16).reshape(per_image)
    grad_query, grad_key, grad_value = lax.map(
        attend_back, (query_low, key_low, value_low, grad_heads, log_total, scale_lens)
    )
    unused, head_back = jax.vjp(head_inputs, query_raw, key_raw, head_scale)
    grad_query_raw, grad_key_raw, grad_head_scale = head_back(
        (grad_query.reshape(per_row), grad_key.reshape(per_row))
    )
    grad_qkv = jnp.stack(
        [
            grad_query_raw.reshape(group_rows, local_width),
            grad_key_raw.reshape(group_rows, local_width),
            grad_value.reshape(group_rows, local_width),
        ],
        axis=1,
    ).astype(jnp.bfloat16)
    grad_qv_bias = jnp.stack(
        [
            jnp.sum(grad_qkv[:, 0], axis=0, dtype=jnp.float32),
            jnp.sum(grad_qkv[:, 2], axis=0, dtype=jnp.float32),
        ]
    )
    grad_qkv_weight = jnp.einsum(
        "rd,rsk->dsk", inputs_one, grad_qkv, preferred_element_type=jnp.float32
    )
    grad_qkv_flat = grad_qkv.reshape(group_rows, 3 * local_width)
    grad_mixed_one = sum_grads(
        grad_qkv_flat, qkv_full.reshape(model_width, 3 * local_width), own_rows
    )
    grad_mixed_one = grad_mixed_one.reshape(own_shape)
    unused, norm_one_back = jax.vjp(modulate, rows_float, modulation[:, 2:3], modulation[:, 4:5])
    grad_rows_norm, grad_scale_one, grad_shift_one = norm_one_back(grad_mixed_one)
    grad_tokens = (grad_middle + grad_rows_norm).astype(jnp.bfloat16).reshape(own_rows, model_width)
    grad_modul = jnp.stack(
        [
            grad_gamma_one,
            grad_gamma_two,
            grad_scale_one[:, 0],
            grad_scale_two[:, 0],
            grad_shift_one[:, 0],
            grad_shift_two[:, 0],
        ],
        axis=1,
    ).astype(jnp.bfloat16)
    grad_modul_part = lax.all_to_all(grad_modul, "tensor", split_axis=2, concat_axis=0, tiled=True)
    grad_ada = jnp.einsum(
        "ic,isd->csd", cond_low, grad_modul_part, preferred_element_type=jnp.float32
    )
    grad_ada_bias = jnp.sum(grad_modul_part, axis=0, dtype=jnp.float32)
    unused, silu_back = jax.vjp(jax.nn.silu, cond_float)
    grad_cond_part = silu_back(
        jnp.einsum("isd,csd->ic", grad_modul_part, ada_full, preferred_element_type=jnp.float32)
    )[0]
    grad_condition = lax.psum_scatter(
        grad_cond_part.astype(jnp.bfloat16), "tensor", scatter_dimension=0, tiled=True
    ).astype(jnp.float32)
    weight_grads = (
        lax.psum_scatter(
            grad_qkv_weight.astype(jnp.bfloat16), "dp", scatter_dimension=0, tiled=True
        ).astype(jnp.float32),
        lax.psum_scatter(
            grad_proj.astype(jnp.bfloat16), "dp", scatter_dimension=1, tiled=True
        ).astype(jnp.float32),
        lax.psum_scatter(
            grad_fc1.astype(jnp.bfloat16), "dp", scatter_dimension=0, tiled=True
        ).astype(jnp.float32),
        lax.psum_scatter(
            grad_fc2.astype(jnp.bfloat16), "dp", scatter_dimension=1, tiled=True
        ).astype(jnp.float32),
        lax.psum_scatter(
            grad_ada.astype(jnp.bfloat16), "dp", scatter_dimension=0, tiled=True
        ).astype(jnp.float32),
        lax.psum_scatter(
            grad_proj_bias.astype(jnp.bfloat16), "dp", scatter_dimension=0, tiled=True
        ).astype(jnp.float32),
        lax.psum_scatter(
            grad_fc2_bias.astype(jnp.bfloat16), "dp", scatter_dimension=0, tiled=True
        ).astype(jnp.float32),
    )
    small_grads = lax.psum((grad_qv_bias, grad_head_scale, grad_fc1_bias, grad_ada_bias), "dp")
    return (
        output.astype(jnp.bfloat16).reshape(own_rows, model_width),
        grad_tokens,
        grad_condition,
        weight_grads[0],
        small_grads[0],
        small_grads[1],
        weight_grads[1],
        weight_grads[5],
        weight_grads[2],
        small_grads[2],
        weight_grads[3],
        weight_grads[6],
        weight_grads[4],
        small_grads[3],
    )


def solution(mesh):
    return jax.shard_map(
        local,
        mesh=mesh,
        in_specs=(
            P(("dp", "tensor"), None),
            P("dp", None),
            P("dp", None),
            P("dp", None, "tensor"),
            P(None, "tensor"),
            P("tensor"),
            P("tensor", "dp"),
            P("dp"),
            P("dp", "tensor"),
            P("tensor"),
            P("tensor", "dp"),
            P("dp"),
            P("dp", None, "tensor"),
            P(None, "tensor"),
            P(("dp", "tensor"), None),
        ),
        out_specs=(
            P(("dp", "tensor"), None),
            P(("dp", "tensor"), None),
            P(("dp", "tensor"), None),
            P("dp", None, "tensor"),
            P(None, "tensor"),
            P("tensor"),
            P("tensor", "dp"),
            P("dp"),
            P("dp", "tensor"),
            P("tensor"),
            P("tensor", "dp"),
            P("dp"),
            P("dp", None, "tensor"),
            P(None, "tensor"),
        ),
        check_vma=False,
    )
```

profile of v0, /device:TPU:0, one launch (start us, length us, event | category | flops | bytes accessed | tf_op | source)
XLA Modules:
  0.0 1390.0 jit_solution(8071925931883333469)
XLA Ops:
  11.5 63.4 %all-gather.10.cloned.1.call-done = bf16[1024,6,512]{2,0,1:T(8,128)(2,1)} async-done(((bf16[64,6,512]{2,0,1:T(8,128)(2,1)}), bf16[1024,6,512]{2,0,1:T(8,128)(2,1)}) %all-gather.10.cloned.1.call-update) | async-done | bytes 6291472 | tf_op jit(solution)/shard_map/all_gather | solution.py:149
  94.3 26.6 %all-gather.14.cloned.1.call-done = bf16[1024,3,512]{2,0,1:T(8,128)(2,1)} async-done(((bf16[64,3,512]{2,0,1:T(8,128)(2,1)}), bf16[1024,3,512]{2,0,1:T(8,128)(2,1)}) %all-gather.14.cloned.1.call-update) | async-done | bytes 3145744 | tf_op jit(solution)/shard_map/all_gather | solution.py:145
  120.9 41.8 %all-gather.12.cloned.1.call-done = bf16[1360,1024]{1,0:T(8,128)(2,1)} async-done(((bf16[680,1024]{1,0:T(8,128)(2,1)}), bf16[1360,1024]{1,0:T(8,128)(2,1)}) %all-gather.12.cloned.1.call-update) | async-done | bytes 2785296 | tf_op jit(solution)/shard_map/all_gather | solution.py:84
  207.9 56.2 %while.28 = (s32[]{:T(128)}, bf16[2,680,8,64]{1,3,2,0:T(8,128)(2,1)}, f32[2,8,680]{2,1,0:T(8,128)S(1)}, bf16[2,680,8,64]{1,3,2,0:T(8,128)(2,1)}, s32[2,10]{1,0:T...) while((s32[]{:T(128)}, bf16[2,680,8,64]{1,3,2,0:T(8,128)(2,1)}, ...), condition=%wide.region_9.10_spmd.clone, body=%wide.region_4.9_spmd.sunk.clone | while | flops 980764736 | bytes 52156968 | solution.py:171
  280.8 33.2 %all-reduce = bf16[1024]{0:T(1024)(128)(2,1)S(1)} all-reduce(bf16[1024]{0:T(1024)(128)(2,1)S(1)} %dynamic-update-slice), channel_id=1, replica_groups=mesh['dp'=16,'tensor'=2] {'dp'}, use_global_device_ids=true, to_apply=%add | all-reduce | flops 1024 | bytes 4096
  313.9 34.1 %reduce-scatter.10.cloned.1.call-done = f32[680,1024]{1,0:T(8,128)} async-done(((f32[1360,1024]{1,0:T(8,128)}), f32[680,1024]{1,0:T(8,128)}) %reduce-scatter.10.cloned.1.call-update) | async-done | bytes 2785296 | tf_op jit(solution)/shard_map/reduce_scatter | solution.py:92
  355.9 44.7 %all-gather.20.cloned.1.call-done = bf16[1024,2048]{1,0:T(8,128)(2,1)} async-done(((bf16[64,2048]{1,0:T(8,128)(2,1)}), bf16[1024,2048]{1,0:T(8,128)(2,1)}) %all-gather.20.cloned.1.call-update) | async-done | bytes 4194320 | tf_op jit(solution)/shard_map/all_gather | solution.py:147
  400.6 41.5 %all-gather.18.cloned.1.call-done = bf16[1360,1024]{1,0:T(8,128)(2,1)} async-done(((bf16[680,1024]{1,0:T(8,128)(2,1)}), bf16[1360,1024]{1,0:T(8,128)(2,1)}) %all-gather.18.cloned.1.call-update) | async-done | bytes 2785296 | tf_op jit(solution)/shard_map/all_gather | solution.py:84
  453.6 41.3 %all-gather.22.cloned.1.call-done = bf16[2048,1024]{0,1:T(8,128)(2,1)} async-done(((bf16[2048,64]{0,1:T(8,128)(2,1)}), bf16[2048,1024]{0,1:T(8,128)(2,1)}) %all-gather.22.cloned.1.call-update) | async-done | bytes 4194320 | tf_op jit(solution)/shard_map/all_gather | solution.py:148
  494.9 41.5 %all-gather.24.cloned.1.call-done = bf16[1360,1024]{1,0:T(8,128)(2,1)} async-done(((bf16[680,1024]{1,0:T(8,128)(2,1)}), bf16[1360,1024]{1,0:T(8,128)(2,1)}) %all-gather.24.cloned.1.call-update) | async-done | bytes 2785296 | tf_op jit(solution)/shard_map/all_gather | solution.py:101
  536.4 19.9 %convert_reduce_fusion.2 = (f32[2048]{0:T(1024)}, bf16[1360,2048]{1,0:T(8,128)(2,1)S(1)}, bf16[1360,2048]{1,0:T(8,128)(2,1)}) fusion(f32[1360,2048]{1,0:T(8,128)} %fusion.104, f32[2048]{0:T(1024)S(1)} %convert_element_type.176, bf16[1360,1024]{1,0:T(8,128)(2,1)} %all-gather.24.cloned.1.call-done, bf16[2048,1024]{0,1:T(8,128)(2,1)} %all-gather.22.cloned.1.call-done), kind=kOutput, calls=%fused_computation.70 | convolution fusion | flops 5773883392 | bytes 29278208 | tf_op jit(solution)/shard_map/rd,fd->rf/dot_general | solution.py:193
  567.2 68.9 %reduce-scatter.14.cloned.1.call-done = f32[680,1024]{1,0:T(8,128)} async-done(((f32[1360,1024]{1,0:T(8,128)}), f32[680,1024]{1,0:T(8,128)}) %reduce-scatter.14.cloned.1.call-update) | async-done | bytes 2785296 | tf_op jit(solution)/shard_map/reduce_scatter | solution.py:109
  656.4 29.2 %all-gather.26.cloned.1.call-done = bf16[1360,1024]{1,0:T(8,128)(2,1)} async-done(((bf16[680,1024]{1,0:T(8,128)(2,1)}), bf16[1360,1024]{1,0:T(8,128)(2,1)}) %all-gather.26.cloned.1.call-update) | async-done | bytes 2785296 | tf_op jit(solution)/shard_map/all_gather | solution.py:101
  696.2 98.0 %while.29 = (s32[]{:T(128)}, f32[2,680,8,64]{1,3,2,0:T(8,128)}, f32[2,680,8,64]{1,3,2,0:T(8,128)}, bf16[2,680,8,64]{1,3,2,0:T(8,128)(2,1)}, bf16[2,680,8,64]{1,3...) while((s32[]{:T(128)}, f32[2,680,8,64]{1,3,2,0:T(8,128)}, ...), condition=%wide.region_21.22_spmd.clone, body=%wide.region_17.21_spmd.sunk.clone | while | flops 2412355072 | bytes 217011264 | solution.py:212
  715.5 13.2 multiply_reduce_fusion.12
  764.5 13.2 multiply_reduce_fusion.12
  928.2 33.9 %all-reduce.6 = (bf16[1024]{0:T(1024)(128)(2,1)S(1)}, bf16[1024]{0:T(1024)(128)(2,1)S(1)}, bf16[1024]{0:T(1024)(128)(2,1)S(1)}) all-reduce(bf16[1024]{0:T(1024)(128)(2,1)S(1)} %dynamic-update-slice.1, bf16[1024]{0:T(1024)(128)(2,1)S(1)} %reduce_sum.344, bf16[1024]{0:T(1024)(128)(2,1)S(1)} %reduce_sum.346), channel_id=1, replica_groups=mesh['dp'=16,'tensor'=2] {'dp'}, use_global_device_ids=true, to_apply=%add.1 | all-reduce | flops 3072 | bytes 12288
  967.8 43.4 %reduce-scatter.12.cloned.1.call-done = f32[680,1024]{1,0:T(8,128)} async-done(((f32[1360,1024]{1,0:T(8,128)}), f32[680,1024]{1,0:T(8,128)}) %reduce-scatter.12.cloned.1.call-update) | async-done | bytes 2785296 | tf_op jit(solution)/shard_map/reduce_scatter | solution.py:92
  1035.8 51.5 %reduce-scatter.22.cloned.1.call-done = bf16[64,2048]{1,0:T(8,128)(2,1)} async-done(((bf16[1024,2048]{1,0:T(8,128)(2,1)}), bf16[64,2048]{1,0:T(8,128)(2,1)}) %reduce-scatter.22.cloned.1.call-update) | async-done | bytes 262160 | tf_op jit(solution)/shard_map/reduce_scatter | solution.py:274
  1089.1 73.9 %reduce-scatter.24.cloned.1.call-done = bf16[2048,64]{0,1:T(8,128)(2,1)} async-done(((bf16[2048,1024]{0,1:T(8,128)(2,1)}), bf16[2048,64]{0,1:T(8,128)(2,1)}) %reduce-scatter.24.cloned.1.call-update) | async-done | bytes 262160 | tf_op jit(solution)/shard_map/reduce_scatter | solution.py:277
  1165.6 57.3 %reduce-scatter.20.cloned.1.call-done = bf16[512,64]{0,1:T(8,128)(2,1)} async-done(((bf16[512,1024]{0,1:T(8,128)(2,1)}), bf16[512,64]{0,1:T(8,128)(2,1)}) %reduce-scatter.20.cloned.1.call-update) | async-done | bytes 65552 | tf_op jit(solution)/shard_map/reduce_scatter | solution.py:271
  1224.4 67.8 %reduce-scatter.18.cloned.1.call-done = bf16[64,3,512]{2,0,1:T(8,128)(2,1)} async-done(((bf16[1024,3,512]{2,0,1:T(8,128)(2,1)}), bf16[64,3,512]{2,0,1:T(8,128)(2,1)}) %reduce-scatter.18.cloned.1.call-update) | async-done | bytes 196624 | tf_op jit(solution)/shard_map/reduce_scatter | solution.py:268
  1294.0 59.5 %all-reduce.5 = (f32[2,512]{1,0:T(2,128)}, f32[8]{0:T(128)}, f32[2048]{0:T(1024)}, f32[6,512]{1,0:T(8,128)}) all-reduce(f32[2,512]{1,0:T(2,128)S(1)} %pad_maximum_fusion.3, f32[8]{0:T(128)S(1)} %get-tuple-element.259, f32[2048]{0:T(1024)S(1)} %copy-done.68, ...), channel_id=1, replica_groups=mesh['dp'=16,'tensor'=2] {'dp'}, use_global_device_ids=true, to_apply=%region_37.38 | all-reduce | flops 6152 | bytes 49216 | tf_op jit(solution)/shard_map/psum | solution.py:290
  1364.2 16.8 %reduce-scatter.26.cloned.1.call-done = bf16[64,6,512]{2,0,1:T(8,128)(2,1)} async-done(((bf16[1024,6,512]{2,0,1:T(8,128)(2,1)}), bf16[64,6,512]{2,0,1:T(8,128)(2,1)}) %reduce-scatter.26.cloned.1.call-update) | async-done | bytes 393232 | tf_op jit(solution)/shard_map/reduce_scatter | solution.py:280
  (408 shorter events, 455.6 us)
Async XLA Ops:
  7.2 67.7 %all-gather.10.cloned.1.call-start = ((), (), s32[]{:S(2)}) async-start(), calls=%async_computation.11 | async-start | bytes 6684672 | tf_op jit(solution)/shard_map/all_gather | solution.py:149
  7.9 113.0 %all-gather.14.cloned.1.call-start = ((), (), s32[]{:S(2)}) async-start(), calls=%async_computation.13 | async-start | bytes 3342336 | tf_op jit(solution)/shard_map/all_gather | solution.py:145
  79.2 7.2 all-to-all-start
  82.5 80.3 %all-gather.12.cloned.1.call-start = ((), (), s32[]{:S(2)}) async-start(), calls=%async_computation.12 | async-start | bytes 4177920 | tf_op jit(solution)/shard_map/all_gather | solution.py:84
  89.4 183.3 %all-gather.16.cloned.1.call-start = ((), (), s32[]{:S(2)}) async-start(), calls=%async_computation.14 | async-start | bytes 1114112 | tf_op jit(solution)/shard_map/all_gather | solution.py:146
  90.0 258.1 %reduce-scatter.10.cloned.1.call-start = ((), (), s32[]{:S(2)}) async-start(), calls=%async_computation.15 | async-start | bytes 8355840 | tf_op jit(solution)/shard_map/reduce_scatter | solution.py:92
  91.5 111.3 %copy-start.47 = (f32[8,64]{1,0:T(8,128)}, f32[8,64]{1,0:T(8,128)S(1)}, u32[]{:S(2)}) copy-start(f32[8,64]{1,0:T(8,128)S(1)} %add.248) | copy-start | bytes 6148
  278.6 122.0 %all-gather.20.cloned.1.call-start = ((), (), s32[]{:S(2)}) async-start(), calls=%async_computation.17 | async-start | bytes 4456448 | tf_op jit(solution)/shard_map/all_gather | solution.py:147
  279.2 163.0 %all-gather.18.cloned.1.call-start = ((), (), s32[]{:S(2)}) async-start(), calls=%async_computation.16 | async-start | bytes 4177920 | tf_op jit(solution)/shard_map/all_gather | solution.py:84
  353.6 141.4 %all-gather.22.cloned.1.call-start = ((), (), s32[]{:S(2)}) async-start(), calls=%async_computation.18 | async-start | bytes 4456448 | tf_op jit(solution)/shard_map/all_gather | solution.py:148
  354.3 182.1 %all-gather.24.cloned.1.call-start = ((), (), s32[]{:S(2)}) async-start(), calls=%async_computation.20 | async-start | bytes 4177920 | tf_op jit(solution)/shard_map/all_gather | solution.py:101
  355.8 280.3 %reduce-scatter.14.cloned.1.call-start = ((), (), s32[]{:S(2)}) async-start(), calls=%async_computation.21 | async-start | bytes 8355840 | tf_op jit(solution)/shard_map/reduce_scatter | solution.py:109
  566.7 118.8 %all-gather.26.cloned.1.call-start = ((), (), s32[]{:S(2)}) async-start(), calls=%async_computation.22 | async-start | bytes 4177920 | tf_op jit(solution)/shard_map/all_gather | solution.py:101
  644.6 317.6 %reduce-scatter.16.cloned.1.call-start = ((), (), s32[]{:S(2)}) async-start(), calls=%async_computation.23 | async-start | bytes 8355840 | tf_op jit(solution)/shard_map/reduce_scatter | solution.py:109
  696.2 98.0 %copy-start.32 = (f32[2,680,8]{1,0,2:T(2,128)S(1)}, f32[2,680,8]{1,0,2:T(2,128)}, u32[]{:S(2)}) copy-start(f32[2,680,8]{1,0,2:T(2,128)} %copy-done.31) | copy-start | bytes 130564
  696.2 98.0 %copy-start.48 = (f32[8,64]{1,0:T(8,128)S(1)}, f32[8,64]{1,0:T(8,128)}, u32[]{:S(2)}) copy-start(f32[8,64]{1,0:T(8,128)} %copy-done.47) | copy-start | bytes 6148
  870.2 141.0 %reduce-scatter.12.cloned.1.call-start = ((), (), s32[]{:S(2)}) async-start(), calls=%async_computation.19 | async-start | bytes 8355840 | tf_op jit(solution)/shard_map/reduce_scatter | solution.py:92
  881.0 206.3 %reduce-scatter.22.cloned.1.call-start = ((), (), s32[]{:S(2)}) async-start(), calls=%async_computation.26 | async-start | bytes 4456448 | tf_op jit(solution)/shard_map/reduce_scatter | solution.py:274
  893.7 269.2 %reduce-scatter.24.cloned.1.call-start = ((), (), s32[]{:S(2)}) async-start(), calls=%async_computation.27 | async-start | bytes 4456448 | tf_op jit(solution)/shard_map/reduce_scatter | solution.py:277
  907.1 315.8 %reduce-scatter.20.cloned.1.call-start = ((), (), s32[]{:S(2)}) async-start(), calls=%async_computation.25 | async-start | bytes 1114112 | tf_op jit(solution)/shard_map/reduce_scatter | solution.py:271
  913.2 379.0 %reduce-scatter.18.cloned.1.call-start = ((), (), s32[]{:S(2)}) async-start(), calls=%async_computation.24 | async-start | bytes 3342336 | tf_op jit(solution)/shard_map/reduce_scatter | solution.py:268
  922.6 458.4 %reduce-scatter.26.cloned.1.call-start = ((), (), s32[]{:S(2)}) async-start(), calls=%async_computation.28 | async-start | bytes 6684672 | tf_op jit(solution)/shard_map/reduce_scatter | solution.py:280
  1033.9 131.4 %copy-start.18 = (bf16[1360,1,512]{0,2,1:T(8,128)(2,1)S(1)}, bf16[1360,1,512]{0,2,1:T(8,128)(2,1)}, u32[]{:S(2)}) copy-start(bf16[1360,1,512]{0,2,1:T(8,128)(2,1)} %copy-done.17) | copy-start | bytes 4177924
  1034.6 259.4 %copy-start.68 = (f32[2048]{0:T(1024)S(1)}, f32[2048]{0:T(1024)}, u32[]{:S(2)}) copy-start(f32[2048]{0:T(1024)} %get-tuple-element.241) | copy-start | bytes 24580
  (92 other events, 1168.5 us)
Sparse Core Ops, SparseCore 0:
  10.2 64.6 all-gather.9
  77.1 43.7 all-gather.13
  123.0 39.6 all-gather.11
  164.8 37.9 all-gather.15
  278.7 69.2 reduce-scatter.9
  350.0 50.5 all-gather.19
  402.8 39.3 all-gather.17
  444.3 50.5 all-gather.21
  497.0 39.3 all-gather.23
  566.9 69.2 reduce-scatter.13
  644.7 40.8 all-gather.25
  870.3 69.2 reduce-scatter.15
  941.9 69.2 reduce-scatter.11
  1014.9 72.3 reduce-scatter.21
  1091.5 71.4 reduce-scatter.23
  1166.4 56.3 reduce-scatter.19
  1227.0 65.1 reduce-scatter.17
  1296.5 84.4 reduce-scatter.25
where the time goes:
time: 1400 us; the launch traced here: 1390 us
  waiting for transfers between devices  751 us (54%)
  matrix products  235 us (17%)
  blocking collectives  138 us (10%)
  local copies, waits for them, and re-layouts  132 us (9%)
  other arithmetic  113 us (8%)
  between operations  16.8 us (1%)
    all_gather x2, waiting for transfers between devices, share_rows(): return lax.all_gather(local_rows, 'tensor', axis=0, tiled=True)  83.3 us
    reduce_scatter x2, waiting for transfers between devices, sum_rows(): lax.psum_scatter(row_term(jnp.int32(0), lax.axis_size('tensor') * own_row...  77.4 us
    reduce_scatter x1, waiting for transfers between devices, local(): lax.psum_scatter(grad_fc2.astype(jnp.bfloat16), 'dp', scatter_dimension=1...  73.9 us
    unnamed x3, blocking collectives  72.1 us
    all_gather x2, waiting for transfers between devices, share_grads(): return lax.all_gather(local_rows, 'tensor', axis=0, tiled=True)  70.7 us
    reduce_scatter x2, waiting for transfers between devices, sum_grads(): lax.psum_scatter(row_term(jnp.int32(0), lax.axis_size('tensor') * own_row...  69 us
    reduce_scatter x1, waiting for transfers between devices, local(): lax.psum_scatter(grad_qkv_weight.astype(jnp.bfloat16), 'dp', scatter_dime...  67.8 us
    all_gather x1, waiting for transfers between devices, local(): lax.all_gather(ada_weight, 'dp', axis=0, tiled=True)  63.4 us
  transfers between devices with their start and end apart: 19, of which 17 were waited for; matrix products, arithmetic and copies ran while one was open for 17% of the time, Pallas kernels for 0%

commit v1 on v0

v1 whole, which is shorter than its diff:
```python
import functools

import jax
import jax.numpy as jnp
from jax import lax
from jax.experimental import pallas as pl
from jax.experimental.pallas import tpu as pltpu
from jax.sharding import PartitionSpec as P

SEQ = 680
NORM_EPS = 1e-06
HEAD_EPS = 1e-06
MASKED = -1e30
HEAD = 64
LANES = 128
GELU_C = 0.7978845608
GELU_A = 0.044715
AXES = ("dp", "tensor")
BACK_AXES = ("tensor", "dp")
VMEM_BYTES = 56 * 1024 * 1024

F32 = jnp.float32
BF16 = jnp.bfloat16
VMEM = pl.BlockSpec(memory_space=pltpu.VMEM)
SMEM = pl.BlockSpec(memory_space=pltpu.SMEM)
ANY = pl.BlockSpec(memory_space=pl.ANY)


def dot(left, right):
    return lax.dot_general(left, right, (((1,), (0,)), ((), ())), preferred_element_type=F32)


def dot_nt(left, right):
    return lax.dot_general(left, right, (((1,), (1,)), ((), ())), preferred_element_type=F32)


def row_chunks(rows, size):
    return [(first, min(size, rows - first)) for first in range(0, rows, size)]


def call(kernel, out_shape, in_specs, out_specs, scratch, cost, name, grid=None, after=()):
    extra = {} if grid is None else {"grid": grid}
    count = len(in_specs)

    def body(*refs):
        kernel(*refs[:count], *refs[count + len(after) :])

    run = pl.pallas_call(
        body,
        out_shape=out_shape,
        in_specs=list(in_specs) + [ANY] * len(after),
        out_specs=out_specs,
        scratch_shapes=scratch,
        cost_estimate=pl.CostEstimate(
            flops=int(cost * 1e9), bytes_accessed=1 << 20, transcendentals=0
        ),
        compiler_params=pltpu.CompilerParams(vmem_limit_bytes=VMEM_BYTES),
        name=name,
        **extra,
    )
    return lambda *operands: run(*operands, *after)


def shape(*dims, dtype=F32):
    return jax.ShapeDtypeStruct(dims, dtype)


class Cube:
    def __init__(self, dp_size, tensor_size):
        self.dp_size, self.tensor_size = dp_size, tensor_size
        dp_bits = dp_size.bit_length() - 1
        tensor_bits = tensor_size.bit_length() - 1
        far = [("dp", 1 << bit) for bit in range(2, dp_bits)]
        near = [("dp", 2)]
        side = [("tensor", 1 << bit) for bit in reversed(range(tensor_bits))]
        core = [("dp", 1)]
        self.orders = (core + side + near + far, core + near + side + far)
        self.sum_orders = (side + near + far, near + side + far)
        self.near_hops = len(side) + 1
        self.core = core[0]
        self.devices = dp_size * tensor_size

    def hop(self, values, hop):
        axis, mask = hop
        size = self.dp_size if axis == "dp" else self.tensor_size
        return lax.ppermute(values, axis, [(i, i ^ mask) for i in range(size)])

    def masks(self, order, index):
        dp_mask, tensor_mask = 0, 0
        for place, (axis, mask) in enumerate(order):
            if (index >> (len(order) - 1 - place)) & 1:
                if axis == "dp":
                    dp_mask |= mask
                else:
                    tensor_mask |= mask
        return dp_mask, tensor_mask

    def index(self, order, dp_rel, tensor_rel):
        total = 0
        for place, (axis, mask) in enumerate(order):
            rel = dp_rel if axis == "dp" else tensor_rel
            bit = (rel // mask) % 2
            total = total + bit * (1 << (len(order) - 1 - place))
        return total

    @property
    def hops(self):
        return len(self.orders[0])


def behind(values, others):
    kept, unused = lax.optimization_barrier((values, others))
    return kept


class Gather:
    def __init__(self, cube, shard):
        self.cube = cube
        rows = shard.shape[0] // 2
        self.step = 0
        self.held = [shard[None, :rows], shard[None, rows:]]
        self.launch()

    def launch(self):
        hops = [order[len(order) - 1 - self.step] for order in self.cube.orders]
        self.received = [self.cube.hop(held, hop) for held, hop in zip(self.held, hops)]

    def advance(self, others=None):
        if others is not None:
            self.received = behind(self.received, others)
        self.step += 1
        self.held = [jnp.concatenate(pair, axis=0) for pair in zip(self.held, self.received)]
        self.launch()

    def sides(self):
        while self.step < self.cube.hops - 1:
            self.advance()
        return [self.held[0], self.received[0], self.held[1], self.received[1]]


class Scatter:
    def __init__(self, cube, groups):
        self.cube, self.step = cube, 0
        self.kept, self.received = [], []
        for group in groups:
            self.add(group)

    def add(self, pairs):
        self.kept.append([keep for keep, send in pairs])
        self.received.append(self.launch([send for keep, send in pairs]))

    def launch(self, outgoing):
        return [
            self.cube.hop(values, order[self.step])
            for values, order in zip(outgoing, self.cube.sum_orders)
        ]

    def advance(self, others=None):
        if self.step == self.cube.hops - 2:
            return []
        if others is not None:
            self.received = behind(self.received, others)
        self.step += 1
        merge = self.step >= self.cube.near_hops
        outs = add_pieces(self.kept, self.received, merge)
        self.kept = [list(outs[0::2])]
        if merge:
            self.received = [[self.cube.hop(outs[1], self.cube.sum_orders[0][self.step])]]
        else:
            self.received = [self.launch(outs[1::2])]
        return list(outs)

    def finish(self, others=None):
        while self.step < self.cube.hops - 2:
            self.advance()
        received = self.received if others is None else behind(self.received, others)
        return self.kept[0][0][0].astype(F32) + received[0][0][0].astype(F32)


def start_pieces(cube, place, held, columns, target, sem):
    copies = make_pieces(cube, place, held, columns, target, sem)
    for copy in copies:
        copy.start()
    return copies


def make_pieces(cube, place, held, columns, target, sem):
    dp_at, tensor_at = place[0], place[1]
    first, count = columns
    half = cube.devices // 2
    copies = []
    for part, order in enumerate(cube.orders):
        for side in range(2):
            source = held[2 * part + side]
            rows = source.shape[1]
            for item in range(half):
                dp_mask, tensor_mask = cube.masks(order, side * half + item)
                owner = jnp.bitwise_xor(dp_at, dp_mask)
                tensor_owner = jnp.bitwise_xor(tensor_at, tensor_mask)
                row = pl.multiple_of(owner * (2 * rows) + part * rows, 16)
                copies.append(
                    pltpu.make_async_copy(
                        source.at[item, :, pl.ds(first, count)],
                        target.at[tensor_owner, pl.ds(row, rows), :],
                        sem,
                    )
                )
    return copies


def moments(values):
    average = jnp.mean(values, axis=-1, keepdims=True)
    centred = values - average
    variance = jnp.mean(centred * centred, axis=-1, keepdims=True)
    return centred, lax.rsqrt(variance + NORM_EPS)


def head_ones():
    row = lax.broadcasted_iota(jnp.int32, (LANES, LANES), 0) // HEAD
    col = lax.broadcasted_iota(jnp.int32, (LANES, LANES), 1) // HEAD
    return (row == col).astype(BF16)


def head_sums(values, ones):
    high = values.astype(BF16)
    low = (values - high.astype(F32)).astype(BF16)
    return dot(high, ones) + dot(low, ones)


def front_kernel(
    cube, pieces, place, tokens, parts, h0, h1, h2, h3,
    mixed, query, key, value, r_query, r_key, modul, fc1_bias, head_scale,
    weight, sem, qv_bias,
):
    copies = start_pieces(cube, place, (h0, h1, h2, h3), (0, weight.shape[2]), weight, sem)
    rows, width = tokens.shape
    local = width // cube.tensor_size
    wide = fc1_bias.shape[1] // cube.tensor_size
    share = (3 * local + wide) // pieces
    last = parts.shape[2] - share
    for item in range(cube.tensor_size):
        for kind in range(6):
            at = slice(kind * local, (kind + 1) * local)
            total = parts[0, item : item + 1, at]
            for source in range(1, cube.dp_size):
                total = total + parts[source, item : item + 1, at]
            modul[kind : kind + 1, item * local : (item + 1) * local] = total
        for piece in range(pieces):
            for step in range(0, share, LANES):
                at = piece * share + step
                got = parts[piece, item : item + 1, last + step : last + step + LANES]
                kind, inner = at // local, at % local
                if kind < 2:
                    qv_bias[kind : kind + 1, pl.ds(item * local + inner, LANES)] = got
                elif kind == 2:
                    head_scale[0:1, pl.ds(item * local + inner, LANES)] = got
                else:
                    fc1_bias[0:1, pl.ds(item * wide + at - 3 * local, LANES)] = got
    modul[6:8, :] = jnp.zeros((2, width), F32)
    gain = 1.0 + modul[2:3, :]
    shift = modul[4:5, :]
    for first, count in row_chunks(rows, 64):
        centred, scale = moments(tokens[first : first + count, :].astype(F32))
        mixed[first : first + count, :] = (centred * scale * gain + shift).astype(BF16)
    for copy in copies:
        copy.wait()
    ones = head_ones()
    for item in range(cube.tensor_size):
        for kind in range(3):
            out = dot(mixed[...], weight[item, :, kind * local : (kind + 1) * local])
            for slab in range(local // LANES):
                at = item * local + slab * LANES
                cols = slice(at, at + LANES)
                part = out[:, slab * LANES : (slab + 1) * LANES]
                if kind == 0:
                    part = part + qv_bias[0:1, cols]
                if kind == 2:
                    value[:, cols] = (part + qv_bias[1:2, cols]).astype(BF16)
                    continue
                inverse = lax.rsqrt(head_sums(part * part, ones) + HEAD_EPS)
                unit = part * inverse
                if kind == 0:
                    query[:, cols] = (unit * head_scale[0:1, cols]).astype(BF16)
                    r_query[:, cols] = inverse
                else:
                    key[:, cols] = unit.astype(BF16)
                    r_key[:, cols] = inverse


def lane_index(rows):
    return lax.broadcasted_iota(jnp.int32, (rows, LANES), 1)


def attend_kernel(query, key, value, query_code, key_code, heads, log_sum):
    rows = query.shape[0]
    low = lane_index(rows) < HEAD
    q, k, v = query[...], key[...], value[...]
    qc, kc = query_code[...], key_code[...]
    zero = jnp.zeros_like(v)
    keys = (jnp.where(low, k, kc), jnp.where(low, kc, k))
    queries = (jnp.where(low, q, qc), jnp.where(low, qc, q))
    values = (jnp.where(low, v, zero), jnp.where(low, zero, v))
    for first, count in row_chunks(rows, 352):
        at = slice(first, first + count)
        out, logs = jnp.zeros((count, LANES), F32), []
        for head in range(2):
            expo = jnp.exp(dot_nt(queries[head][at], keys[head]))
            total = jnp.sum(expo, axis=1, keepdims=True)
            out = out + dot((expo * (1.0 / total)).astype(BF16), values[head])
            logs.append(jnp.log(total))
        heads[at, :] = out.astype(BF16)
        log_sum[at, :] = jnp.where(lane_index(count) < HEAD, logs[1], logs[0])


def middle_kernel(
    cube, place, heads, tokens, cotangent, modul, proj_bias, h0, h1, h2, h3,
    branch, middle, mixed, gated_sum, weight, sem,
):
    rows, width = tokens.shape
    local = width // cube.tensor_size
    copies = start_pieces(cube, place, (h0, h1, h2, h3), (3 * local, local), weight, sem)
    for copy in copies:
        copy.wait()
    gain = 1.0 + modul[3:4, :]
    shift = modul[5:6, :]
    gamma = modul[0:1, :]
    gamma_two = modul[1:2, :]
    total = jnp.zeros((1, width), F32)
    for first, count in row_chunks(rows, 176):
        at = slice(first, first + count)
        out = proj_bias[0:1, :] + jnp.zeros((count, width), F32)
        for item in range(cube.tensor_size):
            out = out + dot_nt(
                heads[at, item * local : (item + 1) * local], weight[item]
            )
        branch[at, :] = out
        mid = tokens[at, :].astype(F32) + gamma * out
        middle[at, :] = mid
        centred, scale = moments(mid)
        mixed[0, at, :] = (centred * scale * gain + shift).astype(BF16)
        gated = (cotangent[at, :].astype(F32) * gamma_two).astype(BF16)
        mixed[1, at, :] = gated
        total += jnp.sum(gated.astype(F32), axis=0, keepdims=True)
    gated_sum[...] = total


def hidden_kernel(mixed, bias, matrix, hidden, slope):
    rows = mixed.shape[0]
    weight = matrix[...].reshape(mixed.shape[1], matrix.shape[2])
    for first, count in row_chunks(rows, 352):
        at = slice(first, first + count)
        pre = dot(mixed[at, :], weight) + bias[...]
        square = pre * pre
        bent = jnp.tanh(pre * (GELU_C + (GELU_C * GELU_A) * square))
        half = 0.5 * pre
        hidden[at, :] = (half + half * bent).astype(BF16)
        slope[at, :] = (
            0.5
            + 0.5 * bent
            + half * (1.0 - bent * bent) * (GELU_C + (3.0 * GELU_C * GELU_A) * square)
        )


def pre_back_kernel(slope, gated, matrix, grad_pre, bias_sums):
    weight = matrix[...].reshape(gated.shape[1], matrix.shape[2])
    low = (dot(gated[...], weight) * slope[...]).astype(BF16)
    grad_pre[...] = low
    bias_sums[...] = jnp.sum(low.astype(F32), axis=0, keepdims=True)


def add_products(total, left, matrix):
    weight = matrix[...].reshape(total.shape[1], matrix.shape[2])

    @pl.when(pl.program_id(0) == 0)
    def _():
        total[...] = dot_nt(left[...], weight)

    @pl.when(pl.program_id(0) > 0)
    def _():
        total[...] += dot_nt(left[...], weight)


def output_kernel(
    steps, hidden, matrix, cotangent, middle, modul, fc2_bias, output, sums,
    total, cotangent_here, middle_here, sem,
):
    step = pl.program_id(0)
    copies = [
        pltpu.make_async_copy(cotangent, cotangent_here, sem.at[0]),
        pltpu.make_async_copy(middle, middle_here, sem.at[1]),
    ]

    @pl.when(step == 0)
    def _():
        for copy in copies:
            copy.start()

    add_products(total, hidden, matrix)

    @pl.when(step == steps - 1)
    def _():
        for copy in copies:
            copy.wait()
        rows, width = total.shape
        gamma = modul[1:2, :]
        gamma_sum = jnp.zeros((1, width), F32)
        for first, count in row_chunks(rows, 64):
            at = slice(first, first + count)
            out = total[at, :] + fc2_bias[...]
            output[at, :] = (middle_here[at, :] + gamma * out).astype(BF16)
            gamma_sum += jnp.sum(
                cotangent_here[at, :].astype(F32) * out, axis=0, keepdims=True
            )
        sums[...] = gamma_sum


def first_back_kernel(
    cube, steps, place, grad_pre, matrix, middle, branch, cotangent, modul, h0, h1, h2, h3,
    g_middle, gated, g_heads, sums,
    total, middle_here, branch_here, cotangent_here, gated_here, small, sem, small_sem,
):
    step = pl.program_id(0)
    rows, width = total.shape
    narrow = small.shape[2]
    copies = [
        pltpu.make_async_copy(middle, middle_here, sem.at[0]),
        pltpu.make_async_copy(branch, branch_here, sem.at[1]),
        pltpu.make_async_copy(cotangent, cotangent_here, sem.at[2]),
    ]
    small_copies = make_pieces(
        cube, place, (h0, h1, h2, h3), (3 * narrow, narrow), small, small_sem
    )
    outs = [
        pltpu.make_async_copy(total, g_middle, sem.at[0]),
        pltpu.make_async_copy(gated_here, gated, sem.at[1]),
    ]

    @pl.when(step == 0)
    def _():
        for copy in copies + small_copies:
            copy.start()

    add_products(total, grad_pre, matrix)

    @pl.when(step == steps - 1)
    def _():
        for copy in copies:
            copy.wait()
        gain = 1.0 + modul[3:4, :]
        gamma = modul[0:1, :]
        totals = [jnp.zeros((1, width), F32) for _ in range(4)]
        for first, count in row_chunks(rows, 64):
            at = slice(first, first + count)
            grad = total[at, :]
            centred, scale = moments(middle_here[at, :])
            normed = centred * scale
            totals[0] += jnp.sum(grad * normed, axis=0, keepdims=True)
            totals[1] += jnp.sum(grad, axis=0, keepdims=True)
            lifted = grad * gain
            back = cotangent_here[at, :].astype(F32) + scale * (
                lifted
                - jnp.mean(lifted, axis=-1, keepdims=True)
                - normed * jnp.mean(lifted * normed, axis=-1, keepdims=True)
            )
            total[at, :] = back
            totals[2] += jnp.sum(back * branch_here[at, :], axis=0, keepdims=True)
            low = (back * gamma).astype(BF16)
            gated_here[at, :] = low
            totals[3] += jnp.sum(low.astype(F32), axis=0, keepdims=True)
        for place_at in range(4):
            sums[place_at : place_at + 1, :] = totals[place_at]
        for copy in outs:
            copy.start()
        for copy in small_copies:
            copy.wait()
        for item in range(cube.tensor_size):
            g_heads[:, item * narrow : (item + 1) * narrow] = dot(
                gated_here[...], small[item]
            ).astype(BF16)
        for copy in outs:
            copy.wait()


def core_rows(cube, place, target, source):
    rows, width = source.shape
    piece = width // cube.dp_size
    here = place[0] % 2 == 0
    for slab in range(width // LANES):
        flipped = source[:, slab * LANES : (slab + 1) * LANES].T
        for pair in range(LANES // (2 * piece)):
            at = 2 * pair * piece
            at_target = slab * LANES // 2 + pair * piece
            target[at_target : at_target + piece, :] = jnp.where(
                here, flipped[at : at + piece], flipped[at + piece : at + 2 * piece]
            )


def pieces_out(cube, place, item, table, outs, sem, first, count):
    dp_at, tensor_at = place[0], place[1]
    tensor_rel = jnp.bitwise_xor(tensor_at, item)
    piece = table.shape[1] * 2 // cube.dp_size
    for pair in range(cube.dp_size // 2):
        dp_rel = jnp.bitwise_xor(dp_at - dp_at % 2, 2 * pair)
        for part, order in enumerate(cube.sum_orders):
            keep, send = outs[2 * part], outs[2 * part + 1]
            half, rows = keep.shape[0], keep.shape[1]
            index = cube.index(order, dp_rel, tensor_rel)
            source = table.at[item, pl.ds(pair * piece + part * rows, rows), :]
            away = index >= half

            @pl.when(away)
            def _():
                pltpu.make_async_copy(
                    source, send.at[index - half, :, pl.ds(first, count)], sem
                ).start()

            @pl.when(jnp.logical_not(away))
            def _():
                pltpu.make_async_copy(
                    source, keep.at[index, :, pl.ds(first, count)], sem
                ).start()


def wait_pieces(cube, item, table, outs, sem, first, count):
    for pair in range(cube.dp_size // 2):
        for part in range(2):
            keep = outs[2 * part]
            rows = keep.shape[1]
            pltpu.make_async_copy(
                table.at[item, pl.ds(0, rows), :], keep.at[0, :, pl.ds(first, count)], sem
            ).wait()


def wide_grad_kernel(cube, per, place, left, left_far, right, right_far, *refs):
    outs, (flip, table, sem) = refs[:-3], refs[-3:]
    step = pl.program_id(0)
    local, block = table.shape[2], right.shape[1]

    @pl.when(step == 0)
    def _():
        core_rows(cube, place, flip.at[0], left)
        core_rows(cube, place, flip.at[1], left_far)

    got = (dot(flip[0], right[...]) + dot(flip[1], right_far[...])).astype(BF16)
    for item in range(cube.tensor_size):
        for part in range(per):

            @pl.when(step == item * per + part)
            def _():
                table[item, :, part * block : (part + 1) * block] = got
                if part == per - 1:
                    pieces_out(cube, place, item, table, outs, sem, 0, local)

    @pl.when(step == cube.tensor_size * per - 1)
    def _():
        for item in range(cube.tensor_size):
            wait_pieces(cube, item, table, outs, sem, 0, local)


def qkv_grad_kernel(cube, with_proj, place, mixed, mixed_far, grads, grads_far, *refs):
    if with_proj:
        gated, gated_far, heads, heads_far = refs[:4]
        outs, refs = refs[4:8], refs[8:]
        flip, table, mat, mat_far, own, far, sem, in_sem, small, sides, sides_far = refs
    else:
        outs, refs = refs[:4], refs[4:]
        flip, table, mat, mat_far, own, far, sem, in_sem = refs
    copies = [
        pltpu.make_async_copy(source, target, in_sem.at[place_at])
        for place_at, (source, target) in enumerate(
            ((mixed, mat), (mixed_far, mat_far), (grads, own), (grads_far, far))
        )
    ]
    if with_proj:
        copies += [
            pltpu.make_async_copy(source, target, in_sem.at[4 + place_at])
            for place_at, (source, target) in enumerate(((heads, sides), (heads_far, sides_far)))
        ]
    for copy in copies:
        copy.start()
    local = table.shape[2] // 3
    for copy in copies[:2]:
        copy.wait()
    core_rows(cube, place, flip.at[0], mat)
    core_rows(cube, place, flip.at[1], mat_far)
    if with_proj:
        late = [
            pltpu.make_async_copy(source, target, in_sem.at[place_at])
            for place_at, (source, target) in enumerate(((gated, mat), (gated_far, mat_far)))
        ]
        for copy in late:
            copy.start()
    for copy in copies[2:4]:
        copy.wait()
    for item in range(cube.tensor_size):
        cols = slice(item * local, (item + 1) * local)
        for kind in range(3):
            table[item, :, kind * local : (kind + 1) * local] = (
                dot(flip[0], own[kind, :, cols]) + dot(flip[1], far[kind, :, cols])
            ).astype(BF16)
        pieces_out(cube, place, item, table, outs, sem, 0, 3 * local)
    if with_proj:
        narrow = small.shape[2]
        for copy in late + copies[4:]:
            copy.wait()
        core_rows(cube, place, flip.at[0], mat)
        core_rows(cube, place, flip.at[1], mat_far)
        for item in range(cube.tensor_size):
            cols = slice(item * narrow, (item + 1) * narrow)
            small[item] = (dot(flip[0], sides[:, cols]) + dot(flip[1], sides_far[:, cols])).astype(
                BF16
            )
            pieces_out(cube, place, item, small, outs, sem, 3 * local, narrow)
        for item in range(cube.tensor_size):
            wait_pieces(cube, item, small, outs, sem, 3 * local, narrow)
    for item in range(cube.tensor_size):
        wait_pieces(cube, item, table, outs, sem, 0, 3 * local)


def split_into(base, lanes, start, values):
    high = values.astype(BF16)
    rest = (values - high.astype(F32)).astype(BF16)
    base = jnp.where(lanes == start, high, base)
    return jnp.where(lanes == start + 1, rest, base)


def attend_back_kernel(
    query, key, value, grad, log_sum, r_query, r_key, head_scale, query_code, key_code,
    grads, sums, flat_query, sides, pairs,
):
    rows = query.shape[0]
    step = pairs.shape[1] // 2
    lanes = lane_index(rows)
    low = lanes < HEAD
    inner = lanes % HEAD
    q, k, v, g = query[...], key[...], value[...], grad[...]
    ones = head_ones()
    spare = 16
    zero = jnp.zeros((rows, LANES), BF16)
    one = jnp.ones((rows, LANES), BF16)
    marks = (inner == spare) | (inner == spare + 1)

    @pl.when(pl.program_id(0) == 0)
    def _():
        pairs[...] = jnp.zeros_like(pairs)
        sides[...] = jnp.zeros_like(sides)

    qc = split_into(query_code[...], inner, spare, -log_sum[...])
    high = jnp.logical_not(low)
    q_wide = jnp.concatenate([q, qc], axis=1)
    for head in range(2):
        side = low if head == 0 else high
        k_code = jnp.where(marks & (high if head == 0 else low), one, key_code[...])
        k_side = jnp.where(side, k, zero)
        k_wide = jnp.concatenate([k_side, k_code], axis=1)
        v_side = jnp.where(side, v, zero)
        at = slice(head * step, head * step + rows)
        sides[0, at, :] = jnp.where(side, g, zero)
        sides[1, at, :] = jnp.where(side, q, zero)
        probs = jnp.exp(dot_nt(k_wide, q_wide))
        pairs[0:rows, at] = probs.astype(BF16)
        weighted = probs * dot_nt(v_side, g)
        change = (weighted - probs * jnp.sum(weighted, axis=0, keepdims=True)).astype(BF16)
        pairs[step : step + rows, at] = change
        flat = dot(k_side.T, change)
        if head == 0:
            flat_query[...] = flat
        else:
            flat_query[...] += flat
    d_value = dot(pairs[0:rows, :], sides[0]).astype(BF16)
    d_key = dot(pairs[step : step + rows, :], sides[1])
    d_query = flat_query[...].T
    scale = head_scale[0:1, :]
    unit = q.astype(F32) / scale
    along = head_sums(unit * d_query, ones)
    out = (r_query[...] * scale * (d_query - unit * along)).astype(BF16)
    grads[0] = out
    sums[0:1, :] = jnp.sum(out.astype(F32), axis=0, keepdims=True)
    sums[2:3, :] = jnp.sum(along, axis=0, keepdims=True)
    unit_key = k.astype(F32)
    along_key = head_sums(unit_key * d_key, ones)
    grads[1] = (r_key[...] * (d_key - unit_key * along_key)).astype(BF16)
    grads[2] = d_value
    sums[1:2, :] = jnp.sum(d_value.astype(F32), axis=0, keepdims=True)


def last_kernel(cube, splits, place, modul, tokens, g_middle, h0, h1, h2, h3, *refs):
    grads, refs = refs[: len(splits)], refs[len(splits) :]
    grad_tokens, sums, weight, left, tokens_here, middle_here, sem, in_sem = refs[:8]
    grads_here = refs[8:]
    rows, width = tokens_here.shape
    local = width // cube.tensor_size
    copies = [
        pltpu.make_async_copy(source, target, in_sem.at[place_at])
        for place_at, (source, target) in enumerate(
            list(zip(grads, grads_here)) + [(tokens, tokens_here), (g_middle, middle_here)]
        )
    ]
    for copy in copies:
        copy.start()
    pieces = make_pieces(cube, place, (h0, h1, h2, h3), (0, weight.shape[2]), weight, sem)
    for copy in pieces:
        copy.start()
    for which, (start, size) in enumerate(splits):
        copies[which].wait()
        for item in range(cube.tensor_size):
            for kind in range(3):
                at = kind * local + start
                left[item, :, at : at + size] = grads_here[which][
                    kind, :, item * size : (item + 1) * size
                ]
    for copy in copies[len(splits) :] + pieces:
        copy.wait()
    gain = 1.0 + modul[2:3, :]
    totals = [jnp.zeros((1, width), F32) for _ in range(2)]
    for first, count in row_chunks(rows, 352):
        out = dot_nt(left[0, first : first + count, :], weight[0])
        for item in range(1, cube.tensor_size):
            out = out + dot_nt(left[item, first : first + count, :], weight[item])
        for inner, inner_count in row_chunks(count, 64):
            at = slice(first + inner, first + inner + inner_count)
            grad = out[inner : inner + inner_count]
            centred, scale = moments(tokens_here[at, :].astype(F32))
            normed = centred * scale
            totals[0] += jnp.sum(grad * normed, axis=0, keepdims=True)
            totals[1] += jnp.sum(grad, axis=0, keepdims=True)
            lifted = grad * gain
            back = middle_here[at, :] + scale * (
                lifted
                - jnp.mean(lifted, axis=-1, keepdims=True)
                - normed * jnp.mean(lifted * normed, axis=-1, keepdims=True)
            )
            grad_tokens[at, :] = back.astype(BF16)
    for place_at in range(2):
        sums[place_at : place_at + 1, :] = totals[place_at]


def pack_kernel(splits, sums_one, gamma_sum, sums_zero, fc1_bias_sum, gated_sum, *refs):
    parts, (out, side) = refs[: len(splits)], refs[len(splits) :]
    dp_size = side.shape[0]
    tensor_size = out.shape[0] // dp_size
    width = gamma_sum.shape[1]
    local, wide = width // tensor_size, fc1_bias_sum.shape[1] // tensor_size
    owners = LANES * dp_size // width
    for slab in range(width // LANES):
        cols = slice(slab * LANES, (slab + 1) * LANES)
        rows = slice(slab * owners, (slab + 1) * owners)
        side[rows, 0:LANES] = jnp.broadcast_to(gated_sum[:, cols], (owners, LANES))
        side[rows, LANES : 2 * LANES] = jnp.broadcast_to(sums_one[3:4, cols], (owners, LANES))
    modul = (
        sums_one[2:3, :], gamma_sum[...], sums_zero[0:1, :],
        sums_one[0:1, :], sums_zero[1:2, :], sums_one[1:2, :],
    )
    for item in range(tensor_size):
        rows = slice(item * dp_size, (item + 1) * dp_size)

        def put(at, values):
            count = values.shape[1]
            out[rows, at : at + count] = jnp.broadcast_to(values, (dp_size, count)).astype(BF16)

        for kind, values in enumerate(modul):
            put(kind * local, values[:, item * local : (item + 1) * local])
        for kind in range(3):
            for part, (start, size) in zip(parts, splits):
                at = (6 + kind) * local + start
                values = part[kind : kind + 1, item * size : (item + 1) * size]
                put(at, values)
                if kind == 2:
                    put(at + local, values - values.astype(BF16).astype(F32))
        put(10 * local, fc1_bias_sum[:, item * wide : (item + 1) * wide])
        out[rows, 10 * local + wide :] = side[...].astype(BF16)


def add_kernel(parts, groups, merge, *refs):
    outs = refs[4 * parts * groups :]
    at = 0
    for part in range(parts):
        first = 0
        for group in range(groups):
            for side in range(2):
                kept, received = refs[at], refs[at + 1]
                at += 2
                rows, count = kept.shape[1:]
                total = (kept[...].astype(F32) + received[...].astype(F32)).astype(BF16)
                base = part * rows if merge else 0
                out = outs[side] if merge else outs[2 * part + side]
                out[:, base : base + rows, first : first + count] = total
            first += count


def add_pieces(kept, received, merge):
    groups, parts = len(kept), len(kept[0])
    items, rows = kept[0][0].shape[0], kept[0][0].shape[1]
    half = items // 2
    per = max(1, half // 2)
    columns = sum(group[0].shape[2] for group in kept)
    operands, specs = [], []
    for part in range(parts):
        for group in range(groups):
            block = (per, rows, kept[group][part].shape[2])
            for side in range(2):
                spec = pl.BlockSpec(block, lambda i, side=side: (i + side * (half // per), 0, 0))
                operands += [kept[group][part], received[group][part]]
                specs += [spec, spec]
    out_rows, out_parts = (parts * rows, 1) if merge else (rows, parts)
    return pl.pallas_call(
        functools.partial(add_kernel, parts, groups, merge),
        out_shape=[jax.ShapeDtypeStruct((half, out_rows, columns), BF16)] * (2 * out_parts),
        grid=(half // per,),
        in_specs=specs,
        out_specs=[pl.BlockSpec((per, out_rows, columns), lambda i: (i, 0, 0))] * (2 * out_parts),
        cost_estimate=pl.CostEstimate(flops=1 << 20, bytes_accessed=1 << 20, transcendentals=0),
        compiler_params=pltpu.CompilerParams(vmem_limit_bytes=VMEM_BYTES),
        name="add",
    )(*operands)


def scale_codes(lengths, rows):
    count = lengths.shape[0]
    bounds = jnp.cumsum(lengths)
    places = jnp.arange(rows, dtype=jnp.int32)
    scale_of = jnp.sum((places[:, None] >= bounds[None, :]).astype(jnp.int32), axis=1)
    lane = jnp.arange(HEAD, dtype=jnp.int32)
    query_code = (scale_of[:, None] == lane[None, :]).astype(BF16)
    blocked = (scale_of[:, None] > lane[None, :]) & (lane[None, :] < count)
    key_code = jnp.where(blocked, MASKED, 0.0).astype(BF16)
    return jnp.tile(query_code, (1, 2)), jnp.tile(key_code, (1, 2))


def to_all(values, axes=AXES):
    return lax.all_to_all(values, axes, split_axis=0, concat_axis=0, tiled=True)


def local(
    tokens, condition, scale_lens, qkv_weight, qv_bias, head_scale, proj_weight, proj_bias,
    fc1_weight, fc1_bias, fc2_weight, fc2_bias, ada_weight, ada_bias, cotangent,
):
    dp_size, tensor_size = lax.axis_size("dp"), lax.axis_size("tensor")
    devices = dp_size * tensor_size
    cube = Cube(dp_size, tensor_size)
    dp_at, tensor_at = lax.axis_index("dp"), lax.axis_index("tensor")
    place = jnp.stack([dp_at, tensor_at]).astype(jnp.int32)
    rows, width = tokens.shape
    piece_rows = qkv_weight.shape[0]
    narrow = qkv_weight.shape[2]
    wide = fc1_weight.shape[1]
    hidden_width = wide * tensor_size

    cond_float = condition.astype(F32)
    cond_low = jax.nn.silu(cond_float).astype(BF16)
    cond_parts = cond_low.reshape(tensor_size, dp_size, piece_rows).transpose(1, 0, 2)
    cond_own = lax.all_to_all(cond_parts, "dp", split_axis=0, concat_axis=0, tiled=True)
    cond_back = cond_own.reshape(dp_size, tensor_size, piece_rows).transpose(1, 0, 2)
    cond_back = cond_back.reshape(devices, piece_rows)
    cond_own = cond_own.reshape(devices, piece_rows)
    ada_flat = ada_weight.reshape(piece_rows, 6 * narrow)

    narrow_gather = Gather(
        cube,
        jnp.concatenate([qkv_weight.reshape(piece_rows, 3 * narrow), proj_weight.T], axis=1),
    )
    narrow_gather.advance(cond_own)
    while narrow_gather.step < cube.hops - 4:
        narrow_gather.advance()
    wide_shard = jnp.concatenate([fc1_weight, fc2_weight.T], axis=1)
    wide_all = lax.all_gather(
        behind(wide_shard, narrow_gather.held), AXES, axis=0, tiled=True
    ).reshape(dp_size, tensor_size, piece_rows, 2 * wide)
    while narrow_gather.step < cube.hops - 2:
        narrow_gather.advance()

    modul_part = jnp.dot(cond_own, ada_flat, preferred_element_type=F32)
    bias_part = jnp.where(dp_at == 0, ada_bias.astype(F32).reshape(1, 6 * narrow), 0.0)
    dp_part = jnp.concatenate([proj_bias, fc2_bias]).astype(F32)
    tensor_part = jnp.concatenate(
        [qv_bias.astype(F32).reshape(-1), jnp.repeat(head_scale, HEAD), fc1_bias.astype(F32)]
    )
    share = -(-tensor_part.shape[0] // (dp_size * LANES)) * LANES
    pieces = tensor_part.shape[0] // share
    tensor_share = lax.dynamic_index_in_dim(
        tensor_part.reshape(pieces, share), jnp.minimum(dp_at, pieces - 1), 0, keepdims=False
    )
    rest = jnp.concatenate([dp_part, tensor_share])[None]
    parts = to_all(
        jnp.concatenate(
            [modul_part + bias_part, jnp.broadcast_to(rest, (devices, rest.shape[1]))], axis=1
        )
    ).reshape(dp_size, tensor_size, -1)
    narrow_gather.advance(parts)
    held = narrow_gather.sides()
    rest = parts[:, 0, 6 * narrow :]
    proj_bias_full = rest[:, :piece_rows].reshape(1, width)
    fc2_bias_full = rest[:, piece_rows : 2 * piece_rows].reshape(1, width)

    own_lens = lax.dynamic_index_in_dim(scale_lens, tensor_at, 0, keepdims=False)
    query_code, key_code = scale_codes(own_lens, rows)

    dma = pltpu.SemaphoreType.DMA

    def half_shape(*dims):
        return shape(*dims, dtype=BF16)

    mixed_one, query, key, value, r_query, r_key, modul, fc1_bias_full, head_scale_full = call(
        functools.partial(front_kernel, cube, pieces),
        [half_shape(rows, width)] * 4
        + [shape(rows, width)] * 2
        + [shape(8, width), shape(1, hidden_width), shape(1, width)],
        [SMEM, VMEM, VMEM] + [ANY] * 4,
        [VMEM] * 9,
        [
            pltpu.VMEM((tensor_size, width, 3 * narrow), BF16),
            dma,
            pltpu.VMEM((2, width), F32),
        ],
        16, "front",
    )(place, tokens, parts, *held)
    mixed_one_far = cube.hop(mixed_one, cube.core)

    slab = pl.BlockSpec((rows, LANES), lambda i: (0, i))
    whole = pl.BlockSpec((rows, LANES), lambda i: (0, 0))
    heads, log_sum = call(
        attend_kernel,
        [half_shape(rows, width), shape(rows, width)],
        [slab] * 3 + [whole] * 2,
        [slab] * 2,
        [],
        20, "attend", grid=(width // LANES,),
    )(query, key, value, query_code, key_code)
    heads_far = cube.hop(heads, cube.core)

    branch, middle, mixed_two, gated_sum = call(
        functools.partial(middle_kernel, cube),
        [shape(rows, width)] * 2 + [half_shape(2, rows, width), shape(1, width)],
        [SMEM] + [VMEM] * 5 + [ANY] * 4,
        [VMEM] * 4,
        [pltpu.VMEM((tensor_size, width, narrow), BF16), dma],
        10, "middle", after=[mixed_one_far],
    )(place, heads, tokens, cotangent, modul, proj_bias_full, *held)
    mixed_two_far = cube.hop(mixed_two, cube.core)

    block = min(1024, wide)
    per = wide // block
    wide_steps = tensor_size * per

    def wide_block(first):
        return pl.BlockSpec(
            (dp_size, None, piece_rows, block), lambda i: (0, i // per, 0, first * per + i % per)
        )

    side = pl.BlockSpec((rows, block), lambda i: (0, i))
    side_row = pl.BlockSpec((1, block), lambda i: (0, i))

    def mixed_part(which):
        return pl.BlockSpec((None, rows, width), lambda i: (which, 0, 0))

    hidden, slope = call(
        hidden_kernel,
        [half_shape(rows, hidden_width), shape(rows, hidden_width)],
        [mixed_part(0), side_row, wide_block(0)],
        [side] * 2,
        [],
        20, "hidden", grid=(wide_steps,), after=[heads_far],
    )(mixed_two, fc1_bias_full, wide_all)
    hidden_far = cube.hop(hidden, cube.core)

    grad_pre, fc1_bias_sum = call(
        pre_back_kernel,
        [half_shape(rows, hidden_width), shape(1, hidden_width)],
        [side, mixed_part(1), wide_block(1)],
        [side, side_row],
        [],
        300, "pre_back", grid=(wide_steps,), after=[mixed_two_far],
    )(slope, mixed_two, wide_all)
    grad_pre_far = cube.hop(grad_pre, cube.core)

    def piece_shapes(columns):
        return [half_shape(devices // 4, piece_rows // 2, columns)] * 4

    def pairs(outs):
        return list(zip(outs[0::2], outs[1::2]))

    flip_scratch = pltpu.VMEM((2, width // 2, rows), BF16)
    grad_scratch = [flip_scratch, pltpu.VMEM((tensor_size, width // 2, wide), BF16), dma]

    def wide_grad(which, right, right_far, name, after):
        return call(
            functools.partial(wide_grad_kernel, cube, per),
            piece_shapes(wide),
            [SMEM] + [mixed_part(which)] * 2 + [side] * 2,
            [ANY] * 4,
            grad_scratch,
            300, name, grid=(wide_steps,), after=after,
        )(place, mixed_two, mixed_two_far, right, right_far)

    outs = wide_grad(1, hidden, hidden_far, "fc2_grad", [grad_pre])
    fc2_sum = Scatter(cube, [pairs(outs)])
    outs = wide_grad(0, grad_pre, grad_pre_far, "fc1_grad", [outs[0]])
    fc1_sum = Scatter(cube, [pairs(outs)])

    full = pltpu.VMEM((rows, width), F32)
    full_half = pltpu.VMEM((rows, width), BF16)
    whole_row = pl.BlockSpec((1, width), lambda i: (0, 0))
    eight_rows = pl.BlockSpec((8, width), lambda i: (0, 0))
    whole_half = pl.BlockSpec((rows, width), lambda i: (0, 0))
    g_middle, gated_one, g_heads, sums_one = call(
        functools.partial(first_back_kernel, cube, wide_steps),
        [
            shape(rows, width),
            half_shape(rows, width),
            half_shape(rows, width),
            shape(8, width),
        ],
        [SMEM, side, wide_block(0)] + [ANY] * 3 + [eight_rows] + [ANY] * 4,
        [ANY, ANY, whole_half, eight_rows],
        [
            full, full, full, full_half, full_half,
            pltpu.VMEM((tensor_size, width, narrow), BF16),
            dma((3,)), dma,
        ],
        500, "first_back", grid=(wide_steps,), after=[outs[0]],
    )(place, grad_pre, wide_all, middle, branch, cotangent, modul, *held)
    gated_one_far = cube.hop(gated_one, cube.core)

    splits = [(0, narrow // 2), (narrow // 2, narrow // 2)]
    if narrow < 2 * LANES:
        splits = [(0, narrow)]
    steps = narrow // LANES
    padded = -(-rows // LANES) * LANES

    def attend_back(start, size, after):
        per, base = size // LANES, start // LANES

        def column(i):
            return (i // per) * steps + base + i % per

        picked = pl.BlockSpec((rows, LANES), lambda i: (0, column(i)))
        picked_row = pl.BlockSpec((1, LANES), lambda i: (0, column(i)))
        count = tensor_size * per
        return call(
            attend_back_kernel,
            [half_shape(3, rows, count * LANES), shape(8, count * LANES)],
            [picked] * 7 + [picked_row] + [whole] * 2,
            [
                pl.BlockSpec((3, rows, LANES), lambda i: (0, 0, i)),
                pl.BlockSpec((8, LANES), lambda i: (0, i)),
            ],
            [
                pltpu.VMEM((LANES, rows), F32),
                pltpu.VMEM((2, 2 * padded, LANES), BF16),
                pltpu.VMEM((2 * padded, 2 * padded), BF16),
            ],
            400, "attend_back", grid=(count,), after=after,
        )(query, key, value, g_heads, log_sum, r_query, r_key, head_scale_full,
          query_code, key_code)

    def qkv_grad(size, with_proj, grads, grads_far, after):
        extra = [gated_one, gated_one_far, heads, heads_far] if with_proj else []
        cut = pltpu.VMEM((3, rows, tensor_size * size), BF16)
        proj_scratch = [pltpu.VMEM((tensor_size, width // 2, narrow), BF16), full_half, full_half]
        return call(
            functools.partial(qkv_grad_kernel, cube, with_proj),
            piece_shapes(3 * size + (narrow if with_proj else 0)),
            [SMEM] + [ANY] * (4 + len(extra)),
            [ANY] * 4,
            [
                flip_scratch,
                pltpu.VMEM((tensor_size, width // 2, 3 * size), BF16),
                full_half, full_half, cut, cut,
                dma, dma((6,)),
            ] + (proj_scratch if with_proj else []),
            200, "qkv_grad", after=after,
        )(place, mixed_one, mixed_one_far, grads, grads_far, *extra)

    after = fc2_sum.advance(sums_one)
    qkv_grads, qkv_grads_far, all_sums = [], [], []
    for start, size in splits:
        grads, part_sums = attend_back(start, size, after)
        qkv_grads.append(grads)
        all_sums.append(part_sums)
        qkv_grads_far.append(cube.hop(grads, cube.core))
        after = [grads] + fc2_sum.advance(part_sums) + fc1_sum.advance(part_sums)
        if len(all_sums) == 1:
            after += [gated_one_far]
    qkv_sum = Scatter(cube, [])
    for which, (start, size) in enumerate(splits):
        outs = qkv_grad(size, which == 0, qkv_grads[which], qkv_grads_far[which], after)
        qkv_sum.add(pairs(outs))
        after = [outs[0]]
    fc2_received = fc2_sum.received
    after += fc1_sum.advance(outs[0])
    output, gamma_sum = call(
        functools.partial(output_kernel, wide_steps),
        [half_shape(rows, width), shape(1, width)],
        [side, wide_block(1)] + [ANY] * 2 + [eight_rows, whole_row],
        [whole_half, whole_row],
        [full, full_half, full, dma((2,))],
        400, "output", grid=(wide_steps,), after=after + [fc2_received[0][0]],
    )(hidden, wide_all, cotangent, middle, modul, fc2_bias_full)
    fc1_received = fc1_sum.received
    after = qkv_sum.advance(gamma_sum) + [fc1_received[0][0]]
    grad_tokens, sums_zero = call(
        functools.partial(last_kernel, cube, splits),
        [half_shape(rows, width), shape(8, width)],
        [SMEM, VMEM] + [ANY] * (6 + len(splits)),
        [VMEM] * 2,
        [
            pltpu.VMEM((tensor_size, width, 3 * narrow), BF16),
            pltpu.VMEM((tensor_size, rows, 3 * narrow), BF16),
            full_half, full, dma, dma((2 + len(splits),)),
        ]
        + [pltpu.VMEM((3, rows, tensor_size * size), BF16) for start, size in splits],
        400, "last", after=after,
    )(place, modul, tokens, g_middle, *held, *qkv_grads)

    landed = qkv_sum.received
    qkv_sum.advance(sums_zero)
    fc2_own = fc2_sum.finish(sums_zero)
    fc1_own = fc1_sum.finish(sums_zero)

    late = call(
        functools.partial(pack_kernel, splits),
        half_shape(devices, 10 * narrow + wide + 2 * LANES),
        [VMEM] * (5 + len(splits)),
        VMEM,
        [pltpu.VMEM((dp_size, 2 * LANES), F32)],
        1, "pack",
    )(sums_one, gamma_sum, sums_zero, fc1_bias_sum, gated_sum, *all_sums)
    late = to_all(behind(late, landed), BACK_AXES)
    grad_modul_all = late[:, : 6 * narrow]
    late_sum = jnp.sum(late.astype(F32), axis=0)
    grad_ada_bias = late_sum[: 6 * narrow].reshape(6, narrow)
    grad_qv_bias = late_sum[6 * narrow : 8 * narrow].reshape(2, narrow)
    head_sum = late_sum[8 * narrow : 9 * narrow] + late_sum[9 * narrow : 10 * narrow]
    grad_head_scale = head_sum.reshape(-1, HEAD)[:, 0]
    rest = late_sum[10 * narrow :]
    grad_fc1_bias = rest[:wide]
    first_own = (dp_at % (LANES // piece_rows)) * piece_rows
    own_rows = lax.dynamic_slice_in_dim(rest[wide:].reshape(2, LANES), first_own, piece_rows, axis=1)
    grad_fc2_bias, grad_proj_bias = own_rows[0], own_rows[1]
    grad_ada = lax.dot_general(
        cond_back, grad_modul_all, (((0,), (0,)), ((), ())), preferred_element_type=F32
    ).reshape(piece_rows, 6, narrow)
    cond_part = dot_nt(grad_modul_all, ada_flat)
    qkv_sum.advance(cond_part)
    own = qkv_sum.finish()
    parts_own, first = [], 0
    for which, (start, size) in enumerate(splits):
        parts_own.append(own[:, first : first + 3 * size].reshape(piece_rows, 3, size))
        first += 3 * size
        if which == 0:
            proj_own = own[:, first : first + narrow].T
            first += narrow
    qkv_own = jnp.concatenate(parts_own, axis=2)

    cond_all = to_all(cond_part, BACK_AXES).reshape(tensor_size, dp_size, piece_rows)
    cond_image = lax.dynamic_slice_in_dim(cond_float, tensor_at, 1, axis=0)
    unused, silu_back = jax.vjp(jax.nn.silu, cond_image)
    grad_condition = silu_back(jnp.sum(cond_all, axis=0).reshape(1, width))[0]

    return (
        output,
        grad_tokens,
        grad_condition,
        qkv_own,
        grad_qv_bias,
        grad_head_scale,
        proj_own,
        grad_proj_bias,
        fc1_own,
        grad_fc1_bias,
        fc2_own.T,
        grad_fc2_bias,
        grad_ada,
        grad_ada_bias,
    )


def solution(mesh):
    return jax.shard_map(
        local,
        mesh=mesh,
        in_specs=(
            P(("dp", "tensor"), None),
            P("dp", None),
            P("dp", None),
            P("dp", None, "tensor"),
            P(None, "tensor"),
            P("tensor"),
            P("tensor", "dp"),
            P("dp"),
            P("dp", "tensor"),
            P("tensor"),
            P("tensor", "dp"),
            P("dp"),
            P("dp", None, "tensor"),
            P(None, "tensor"),
            P(("dp", "tensor"), None),
        ),
        out_specs=(
            P(("dp", "tensor"), None),
            P(("dp", "tensor"), None),
            P(("dp", "tensor"), None),
            P("dp", None, "tensor"),
            P(None, "tensor"),
            P("tensor"),
            P("tensor", "dp"),
            P("dp"),
            P("dp", "tensor"),
            P("tensor"),
            P("tensor", "dp"),
            P("dp"),
            P("dp", None, "tensor"),
            P(None, "tensor"),
        ),
        check_vma=False,
    )
```

time: 1400 us -> 421 us (0.30)
  waiting for transfers between devices: 751 us -> 82.6 us
  matrix products: 235 us -> 2.19 us
  Pallas kernels: 0 us -> 217 us
  blocking collectives: 138 us -> 0 us
  local copies, waits for them, and re-layouts: 132 us -> 26.1 us
  other arithmetic: 113 us -> 17.5 us
  starting transfers between devices: 4.39 us -> 57 us
    reduce_scatter x9 -> x0, waiting for transfers between devices: 414 us -> none  [the longest x2 77.4 us: sum_rows(): lax.psum_scatter(row_term(jnp.int32(0), lax.axis_size('tensor') * own_row...]
    all_gather x9 -> x1, waiting for transfers between devices: 330 us -> 7.03 us  [local(): lax.all_gather(behind(wide_shard, narrow_gather.held), AXES, axis=0, tile...]
    dot_general x29 -> x3, matrix products: 235 us -> 2.19 us  [the longest x1 1.16 us: local(): lax.dot_general(cond_back, grad_modul_all, (((0,), (0,)), ((), ())), pref...]
    pallas_call x0 -> x24, Pallas kernels: none -> 217 us  [the longest x15 193 us: call(): return lambda *operands: run(*operands, *after)]
    unnamed x3 -> x0, blocking collectives: 72.1 us -> none
    reduce_sum x25 -> x3, other arithmetic: 68.2 us -> 0.22 us  [the longest x1 0.13 us: local(): late_sum = jnp.sum(late.astype(F32), axis=0)]
    psum x1 -> x0, blocking collectives: 59.5 us -> none  [local(): lax.psum((grad_qv_bias, grad_head_scale, grad_fc1_bias, grad_ada_bias), '...]
    ppermute x0 -> x38, waiting for transfers between devices: none -> 42.1 us  [hop(): return lax.ppermute(values, axis, [(i, i ^ mask) for i in range(size)])]
  transfers between devices with their start and end apart: 19 -> 43, of which waited for: 17 -> 11; matrix products, arithmetic and copies ran while one was open for 17% -> 8% of each run, Pallas kernels for 0% -> 52%
where the time goes in v1:
time: 421 us; the launch traced here: 417 us
  Pallas kernels  217 us (52%)
  waiting for transfers between devices  82.6 us (20%)
  starting transfers between devices  57 us (14%)
  local copies, waits for them, and re-layouts  26.1 us (6%)
  other arithmetic  17.5 us (4%)
  between operations  15 us (4%)
    pallas_call x15, Pallas kernels, call(): return lambda *operands: run(*operands, *after)  193 us
    ppermute x38, waiting for transfers between devices, hop(): return lax.ppermute(values, axis, [(i, i ^ mask) for i in range(size)])  42.1 us
    ppermute x38, starting transfers between devices, hop(): return lax.ppermute(values, axis, [(i, i ^ mask) for i in range(size)])  36.1 us
    all_to_all x3, waiting for transfers between devices, to_all(): return lax.all_to_all(values, axes, split_axis=0, concat_axis=0, tiled=True)  29 us
    pallas_call x9, Pallas kernels, add_pieces(): pl.pallas_call(functools.partial(add_kernel, parts, groups, merge), out_s...  24.1 us
    all_to_all x3, starting transfers between devices, to_all(): return lax.all_to_all(values, axes, split_axis=0, concat_axis=0, tiled=True)  14.6 us
    unnamed x52, local copies, waits for them, and re-layouts  9.82 us
  transfers between devices with their start and end apart: 43, of which 11 were waited for; matrix products, arithmetic and copies ran while one was open for 8% of the time, Pallas kernels for 52%

profile of v1, /device:TPU:0, one launch (start us, length us, event | category | flops | bytes accessed | tf_op | source)
XLA Modules:
  0.0 417.5 jit_solution(798275988403354405)
XLA Ops:
  30.7 6.8 %collective-permute-done.5 = bf16[2,32,2048]{2,1,0:T(8,128)(2,1)S(1)} collective-permute-done((bf16[2,32,2048]{2,1,0:T(8,128)(2,1)S(1)}, bf16[2,32,2048]{2,1,0:T(8,128)(2,1)S(1)}, u32[]{:S(2)}, u32[]{:S(2)}) %collective-permute-start.5) | collective-permute-done | bytes 262176 | tf_op jit(solution)/shard_map/ppermute | solution.py:86
  39.9 8.8 %collective-permute-done.2 = bf16[2,32,2048]{2,1,0:T(8,128)(2,1)S(1)} collective-permute-done((bf16[2,32,2048]{2,1,0:T(8,128)(2,1)S(1)}, bf16[2,32,2048]{2,1,0:T(8,128)(2,1)S(1)}, u32[]{:S(2)}, u32[]{:S(2)}) %collective-permute-start.2) | collective-permute-done | bytes 262176 | tf_op jit(solution)/shard_map/ppermute | solution.py:86
  50.1 7.3 %all-to-all-start.1 = ((f32[32,1,3456]{2,1,0:T(1,128)}), f32[32,1,3456]{2,1,0:T(1,128)S(1)}, u32[]{:S(2)}, u32[]{:S(2)}) async-start(f32[32,1,3456]{2,1,0:T(1,128)} %copy.89), calls=%async_computation.1 | async-start | bytes 884736 | tf_op jit(solution)/shard_map/all_to_all | solution.py:831
  65.1 15.7 %all-to-all-done.1 = f32[32,1,3456]{2,1,0:T(1,128)S(1)} async-done(((f32[32,1,3456]{2,1,0:T(1,128)}), f32[32,1,3456]{2,1,0:T(1,128)S(1)}, u32[]{:S(2)}, u32[]{:S(2)}) %all-to-all-start.1) | async-done | bytes 442400 | tf_op jit(solution)/shard_map/all_to_all | solution.py:831
  83.9 11.5 %collective-permute-done.7 = bf16[8,32,2048]{2,1,0:T(8,128)(2,1)} collective-permute-done((bf16[8,32,2048]{2,1,0:T(8,128)(2,1)}, bf16[8,32,2048]{2,1,0:T(8,128)(2,1)}, u32[]{:S(2)}, u32[]{:S(2)}) %collective-permute-start.7) | collective-permute-done | bytes 1048608 | tf_op jit(solution)/shard_map/ppermute | solution.py:86
  95.4 7.1 %collective-permute-done.4 = bf16[8,32,2048]{2,1,0:T(8,128)(2,1)} collective-permute-done((bf16[8,32,2048]{2,1,0:T(8,128)(2,1)}, bf16[8,32,2048]{2,1,0:T(8,128)(2,1)}, u32[]{:S(2)}, u32[]{:S(2)}) %collective-permute-start.4) | collective-permute-done | bytes 1048608 | tf_op jit(solution)/shard_map/ppermute | solution.py:86
  112.4 14.6 %front.1 = (bf16[680,1024]{1,0:T(8,128)(2,1)}, bf16[680,1024]{1,0:T(8,128)(2,1)}, bf16[680,1024]{1,0:T(8,128)(2,1)}, bf16[680,1024]{1,0:T(8,128)(2,1)}, f32[680,...) custom-call(s32[2]{0:T(128)} %pad_add_fusion.refs_0_, ...), custom_call_target="tpu_custom_call" | custom-call | flops 16000000000 | bytes 1048576 | tf_op jit(solution)/shard_map/front/pallas_call | solution.py:61
  127.1 14.7 %attend.1 = (bf16[680,1024]{1,0:T(8,128)(2,1)}, f32[680,1024]{1,0:T(8,128)}) custom-call(bf16[680,1024]{1,0:T(8,128)(2,1)} %get-tuple-element.114.refs_0_, bf16[680,1024]{1,0:T(8,128)(2,1)} %get-tuple-element.115.refs_1_, bf16[680,1024]{1,0:T(8,128)(2,1)} %get-tuple-element.116.refs_2_, bf16[680,128]{1,0:T(8,128)(2,1)} %copy.91.refs_3_.refs_8_, ...), custom_call_target="tpu_custom_call" | custom-call | flops 20000000000 | bytes 1048576 | tf_op jit(solution)/shard_map/attend/pallas_call | solution.py:61
  143.4 10.0 %middle.1 = (f32[680,1024]{1,0:T(8,128)}, f32[680,1024]{1,0:T(8,128)}, bf16[2,680,1024]{2,1,0:T(8,128)(2,1)}, f32[1,1024]{1,0:T(1,128)}) custom-call(s32[2]{0:T(128)} %pad_add_fusion.refs_0_, bf16[680,1024]{1,0:T(8,128)(2,1)} %get-tuple-element.117.refs_1_.refs_7_, bf16[680,1024]{1,0:T(8,128)(2,1)} %refs_2_.5, bf16[680,1024]{1,0:T(8,128)(2,1)} %refs_2_.4, ...), custom_call_target="tpu_custom_call" | custom-call | flops 10000000000 | bytes 1048576 | tf_op jit(solution)/shard_map/middle/pallas_call | solution.py:61
  155.5 7.0 %all-gather.2.cloned.1.call-done = bf16[2048,4096]{1,0:T(8,128)(2,1)} async-done(((bf16[64,4096]{1,0:T(8,128)(2,1)}), bf16[2048,4096]{1,0:T(8,128)(2,1)}) %all-gather.2.cloned.1.call-update) | async-done | bytes 16777232 | tf_op jit(solution)/shard_map/all_gather | solution.py:866
  162.6 15.5 %hidden.1 = (bf16[680,4096]{1,0:T(8,128)(2,1)}, f32[680,4096]{1,0:T(8,128)}) custom-call(bf16[2,680,1024]{2,1,0:T(8,128)(2,1)} %get-tuple-element.120.refs_0_.refs_1_, f32[1,4096]{1,0:T(1,128)} %get-tuple-element.121.refs_1_, bf16[16,2,64,4096]{3,2,1,0:T(8,128)(2,1)} %bitcast.91, bf16[680,1024]{1,0:T(8,128)(2,1)} %collective-permute-done.11.refs_3_.refs_8_), custom_call_target="tpu_custom_call" | custom-call | flops 20000000000 | bytes 1048576 | tf_op jit(solution)/shard_map/hidden/pallas_call | solution.py:61
  179.9 12.4 %pre_back.1 = (bf16[680,4096]{1,0:T(8,128)(2,1)}, f32[1,4096]{1,0:T(1,128)}) custom-call(f32[680,4096]{1,0:T(8,128)} %get-tuple-element.125.refs_0_, bf16[2,680,1024]{2,1,0:T(8,128)(2,1)} %get-tuple-element.120.refs_0_.refs_1_, bf16[16,2,64,4096]{3,2,1,0:T(8,128)(2,1)} %bitcast.92, bf16[2,680,1024]{2,1,0:T(8,128)(2,1)} %copy-done.16), custom_call_target="tpu_custom_call" | custom-call | flops 299999985664 | bytes 1048576 | tf_op jit(solution)/shard_map/pre_back/pallas_call | solution.py:61
  192.5 13.4 %fc2_grad.1 = (bf16[8,32,2048]{2,1,0:T(8,128)(2,1)}, bf16[8,32,2048]{2,1,0:T(8,128)(2,1)}, bf16[8,32,2048]{2,1,0:T(8,128)(2,1)}, bf16[8,32,2048]{2,1,0:T(8,128)(2,1)}) custom-call(s32[2]{0:T(128)} %pad_add_fusion.refs_0_, bf16[2,680,1024]{2,1,0:T(8,128)(2,1)} %get-tuple-element.120.refs_0_.refs_1_, bf16[2,680,1024]{2,1,0:T(8,128)(2,1)} %copy-done.16, ...), custom_call_target="tpu_custom_call" | custom-call | flops 299999985664 | bytes 1048576 | tf_op jit(solution)/shard_map/fc2_grad/pallas_call | solution.py:61
  208.0 13.8 %fc1_grad.1 = (bf16[8,32,2048]{2,1,0:T(8,128)(2,1)}, bf16[8,32,2048]{2,1,0:T(8,128)(2,1)}, bf16[8,32,2048]{2,1,0:T(8,128)(2,1)}, bf16[8,32,2048]{2,1,0:T(8,128)(2,1)}) custom-call(s32[2]{0:T(128)} %pad_add_fusion.refs_0_, bf16[2,680,1024]{2,1,0:T(8,128)(2,1)} %get-tuple-element.120.refs_0_.refs_1_, bf16[2,680,1024]{2,1,0:T(8,128)(2,1)} %copy-done.16, ...), custom_call_target="tpu_custom_call" | custom-call | flops 299999985664 | bytes 1048576 | tf_op jit(solution)/shard_map/fc1_grad/pallas_call | solution.py:61
  223.8 16.7 %first_back.1 = (f32[680,1024]{1,0:T(8,128)}, bf16[680,1024]{1,0:T(8,128)(2,1)}, bf16[680,1024]{1,0:T(8,128)(2,1)}, f32[8,1024]{1,0:T(8,128)}) custom-call(s32[2]{0:T(128)} %pad_add_fusion.refs_0_, bf16[680,4096]{1,0:T(8,128)(2,1)} %get-tuple-element.126.refs_5_.refs_3_.refs_1_, bf16[16,2,64,4096]{3,2,1,0:T(8,128)(2,1)} %bitcast.93, ...), custom_call_target="tpu_custom_call" | custom-call | flops 499999997952 | bytes 1048576 | tf_op jit(solution)/shard_map/first_back/pallas_call | solution.py:61
  246.1 19.7 %attend_back.2 = (bf16[3,680,512]{2,1,0:T(8,128)(2,1)}, f32[8,512]{1,0:T(8,128)}) custom-call(bf16[680,1024]{1,0:T(8,128)(2,1)} %get-tuple-element.114.refs_0_, bf16[680,1024]{1,0:T(8,128)(2,1)} %get-tuple-element.115.refs_1_, bf16[680,1024]{1,0:T(8,128)(2,1)} %get-tuple-element.116.refs_2_, bf16[680,1024]{1,0:T(8,128)(2,1)} %get-tuple-element.130.refs_3_, ...), custom_call_target="tpu_custom_call" | custom-call | flops 399999991808 | bytes 1048576 | tf_op jit(solution)/shard_map/attend_back/pallas_call | solution.py:61
  274.1 19.5 %attend_back.3 = (bf16[3,680,512]{2,1,0:T(8,128)(2,1)}, f32[8,512]{1,0:T(8,128)}) custom-call(bf16[680,1024]{1,0:T(8,128)(2,1)} %get-tuple-element.114.refs_0_, bf16[680,1024]{1,0:T(8,128)(2,1)} %get-tuple-element.115.refs_1_, bf16[680,1024]{1,0:T(8,128)(2,1)} %get-tuple-element.116.refs_2_, bf16[680,1024]{1,0:T(8,128)(2,1)} %get-tuple-element.130.refs_3_, ...), custom_call_target="tpu_custom_call" | custom-call | flops 399999991808 | bytes 1048576 | tf_op jit(solution)/shard_map/attend_back/pallas_call | solution.py:61
  302.0 9.4 %qkv_grad.2 = (bf16[8,32,1280]{2,1,0:T(8,128)(2,1)}, bf16[8,32,1280]{2,1,0:T(8,128)(2,1)}, bf16[8,32,1280]{2,1,0:T(8,128)(2,1)}, bf16[8,32,1280]{2,1,0:T(8,128)(2,1)}) custom-call(s32[2]{0:T(128)} %pad_add_fusion.refs_0_, bf16[680,1024]{1,0:T(8,128)(2,1)} %get-tuple-element.119.refs_1_, bf16[680,1024]{1,0:T(8,128)(2,1)} %copy-done.18, ...), custom_call_target="tpu_custom_call" | custom-call | flops 199999995904 | bytes 1048576 | tf_op jit(solution)/shard_map/qkv_grad/pallas_call | solution.py:61
  313.4 7.3 %qkv_grad.3 = (bf16[8,32,768]{2,1,0:T(8,128)(2,1)}, bf16[8,32,768]{2,1,0:T(8,128)(2,1)}, bf16[8,32,768]{2,1,0:T(8,128)(2,1)}, bf16[8,32,768]{2,1,0:T(8,128)(2,1)}) custom-call(s32[2]{0:T(128)} %pad_add_fusion.refs_0_, bf16[680,1024]{1,0:T(8,128)(2,1)} %get-tuple-element.119.refs_1_, bf16[680,1024]{1,0:T(8,128)(2,1)} %copy-done.18, ...), custom_call_target="tpu_custom_call" | custom-call | flops 199999995904 | bytes 1048576 | tf_op jit(solution)/shard_map/qkv_grad/pallas_call | solution.py:61
  326.2 11.5 %output.1 = (bf16[680,1024]{1,0:T(8,128)(2,1)}, f32[1,1024]{1,0:T(1,128)}) custom-call(bf16[680,4096]{1,0:T(8,128)(2,1)} %get-tuple-element.123.refs_3_.refs_0_, bf16[16,2,64,4096]{3,2,1,0:T(8,128)(2,1)} %bitcast.94, bf16[680,1024]{1,0:T(8,128)(2,1)} %refs_2_.4, f32[680,1024]{1,0:T(8,128)} %get-tuple-element.124.refs_3_, ...), custom_call_target="tpu_custom_call" | custom-call | flops 399999991808 | bytes 1048576 | tf_op jit(solution)/shard_map/output/pallas_call | solution.py:61
  343.6 13.0 %last.1 = (bf16[680,1024]{1,0:T(8,128)(2,1)}, f32[8,1024]{1,0:T(8,128)}) custom-call(s32[2]{0:T(128)} %pad_add_fusion.refs_0_, f32[8,1024]{1,0:T(8,128)} %get-tuple-element.118.refs_4_.refs_6_.refs_1_, bf16[680,1024]{1,0:T(8,128)(2,1)} %refs_2_.5, f32[680,1024]{1,0:T(8,128)} %get-tuple-element.176.refs_3_, ...), custom_call_target="tpu_custom_call" | custom-call | flops 399999991808 | bytes 1048576 | tf_op jit(solution)/shard_map/last/pallas_call | solution.py:61
  372.9 6.9 %all-to-all-done.2 = bf16[32,2,3712]{2,1,0:T(2,128)(2,1)S(1)} async-done(((bf16[32,2,3712]{2,1,0:T(2,128)(2,1)}), bf16[32,2,3712]{2,1,0:T(2,128)(2,1)S(1)}, u32[]{:S(2)}, u32[]{:S(2)}) %all-to-all-start.2) | async-done | bytes 475168 | tf_op jit(solution)/shard_map/all_to_all | solution.py:831
  381.3 6.6 %collective-permute-done.36.refs_1_.refs_3_ = bf16[2,64,2048]{2,1,0:T(8,128)(2,1)S(1)} collective-permute-done((bf16[2,64,2048]{2,1,0:T(8,128)(2,1)}, bf16[2,64,2048]{2,1,0:T(8,128)(2,1)S(1)}, u32[]{:S(2)}, u32[]{:S(2)}) %collective-permute-start.36) | collective-permute-done | bytes 524320 | tf_op jit(solution)/shard_map/ppermute | solution.py:86
  400.3 6.4 %all-to-all-done.3 = f32[32,1,64]{2,1,0:T(1,128)S(1)} async-done(((f32[32,1,64]{2,1,0:T(1,128)}), f32[32,1,64]{2,1,0:T(1,128)S(1)}, u32[]{:S(2)}, u32[]{:S(2)}) %all-to-all-start.3) | async-done | bytes 8224 | tf_op jit(solution)/shard_map/all_to_all | solution.py:831
  (215 shorter events, 127.0 us)
Async XLA Ops:
  21.5 141.1 %all-gather.2.cloned.1.call-start = ((), (), s32[]{:S(2)}) async-start(), calls=%async_computation.4 | async-start | bytes 17301504 | tf_op jit(solution)/shard_map/all_gather | solution.py:866
  28.9 19.7 %collective-permute-start.2 = (bf16[2,32,2048]{2,1,0:T(8,128)(2,1)S(1)}, bf16[2,32,2048]{2,1,0:T(8,128)(2,1)S(1)}, u32[]{:S(2)}, u32[]{:S(2)}) collective-permute-start(bf16[2,32,2048]{2,1,0:T(8,128)(2,1)S(1)} %pad_maximum_fusion.6), channel_id=1, source_target_pairs={{0,8},{2,10},{4,12},{6,14},{8,0},{10,2},{12,4},{14,6},{16,24},{18,... | collective-permute-start | bytes 786440 | tf_op jit(solution)/shard_map/ppermute | solution.py:86
  38.4 19.0 %collective-permute-start.6 = (bf16[4,32,2048]{2,1,0:T(8,128)(2,1)}, bf16[4,32,2048]{2,1,0:T(8,128)(2,1)S(1)}, u32[]{:S(2)}, u32[]{:S(2)}) collective-permute-start(bf16[4,32,2048]{2,1,0:T(8,128)(2,1)} %pad_maximum_fusion.3), channel_id=1, source_target_pairs={{0,1},{1,0},{2,3},{3,2},{4,5},{5,4},{6,7},{7,6},{8,9},{9,8},{10,11... | collective-permute-start | bytes 1572872 | tf_op jit(solution)/shard_map/ppermute | solution.py:86
  50.1 30.8 %all-to-all-start.1 = ((f32[32,1,3456]{2,1,0:T(1,128)}), f32[32,1,3456]{2,1,0:T(1,128)S(1)}, u32[]{:S(2)}, u32[]{:S(2)}) async-start(f32[32,1,3456]{2,1,0:T(1,128)} %copy.89), calls=%async_computation.1 | async-start | bytes 884736 | tf_op jit(solution)/shard_map/all_to_all | solution.py:831
  58.5 36.9 %collective-permute-start.7 = (bf16[8,32,2048]{2,1,0:T(8,128)(2,1)}, bf16[8,32,2048]{2,1,0:T(8,128)(2,1)}, u32[]{:S(2)}, u32[]{:S(2)}) collective-permute-start(bf16[8,32,2048]{2,1,0:T(8,128)(2,1)} %pad_maximum_fusion.1), channel_id=1, source_target_pairs={{0,4},{2,6},{4,0},{6,2},{8,12},{10,14},{12,8},{14,10},{16,20},{18,... | collective-permute-start | bytes 3145736 | tf_op jit(solution)/shard_map/ppermute | solution.py:86
  61.4 41.0 %collective-permute-start.4 = (bf16[8,32,2048]{2,1,0:T(8,128)(2,1)}, bf16[8,32,2048]{2,1,0:T(8,128)(2,1)}, u32[]{:S(2)}, u32[]{:S(2)}) collective-permute-start(bf16[8,32,2048]{2,1,0:T(8,128)(2,1)} %pad_maximum_fusion), channel_id=1, source_target_pairs={{0,1},{1,0},{2,3},{3,2},{4,5},{5,4},{6,7},{7,6},{8,9},{9,8},{10,11... | collective-permute-start | bytes 3145736 | tf_op jit(solution)/shard_map/ppermute | solution.py:86
  153.4 25.0 %collective-permute-start.12 = (bf16[2,680,1024]{2,1,0:T(8,128)(2,1)}, bf16[2,680,1024]{2,1,0:T(8,128)(2,1)S(1)}, u32[]{:S(2)}, u32[]{:S(2)}) collective-permute-start(bf16[2,680,1024]{2,1,0:T(8,128)(2,1)} %get-tuple-element.120.refs_0_.refs_1_), channel_id=1, source_target_pairs={{0,2},{2,0},{4,6},{6,4},{8,10},{10,8},{12,14},{14,12},{16,18},{18,... | collective-permute-start | bytes 8355848 | tf_op jit(solution)/shard_map/ppermute | solution.py:86
  205.9 34.7 %collective-permute-start.15 = (bf16[8,32,2048]{2,1,0:T(8,128)(2,1)}, bf16[8,32,2048]{2,1,0:T(8,128)(2,1)}, u32[]{:S(2)}, u32[]{:S(2)}) collective-permute-start(bf16[8,32,2048]{2,1,0:T(8,128)(2,1)} %get-tuple-element.135), channel_id=1, source_target_pairs={{0,1},{1,0},{2,3},{3,2},{4,5},{5,4},{6,7},{7,6},{8,9},{9,8},{10,11... | collective-permute-start | bytes 3145736 | tf_op jit(solution)/shard_map/ppermute | solution.py:86
  207.2 33.4 %collective-permute-start.16 = (bf16[8,32,2048]{2,1,0:T(8,128)(2,1)}, bf16[8,32,2048]{2,1,0:T(8,128)(2,1)}, u32[]{:S(2)}, u32[]{:S(2)}) collective-permute-start(bf16[8,32,2048]{2,1,0:T(8,128)(2,1)} %get-tuple-element.136), channel_id=1, source_target_pairs={{0,4},{2,6},{4,0},{6,2},{8,12},{10,14},{12,8},{14,10},{16,20},{18,... | collective-permute-start | bytes 3145736 | tf_op jit(solution)/shard_map/ppermute | solution.py:86
  221.9 43.9 %collective-permute-start.19 = (bf16[8,32,2048]{2,1,0:T(8,128)(2,1)}, bf16[8,32,2048]{2,1,0:T(8,128)(2,1)}, u32[]{:S(2)}, u32[]{:S(2)}) collective-permute-start(bf16[8,32,2048]{2,1,0:T(8,128)(2,1)} %get-tuple-element.151), channel_id=1, source_target_pairs={{0,1},{1,0},{2,3},{3,2},{4,5},{5,4},{6,7},{7,6},{8,9},{9,8},{10,11... | collective-permute-start | bytes 3145736 | tf_op jit(solution)/shard_map/ppermute | solution.py:86
  223.3 42.5 %collective-permute-start.20 = (bf16[8,32,2048]{2,1,0:T(8,128)(2,1)}, bf16[8,32,2048]{2,1,0:T(8,128)(2,1)}, u32[]{:S(2)}, u32[]{:S(2)}) collective-permute-start(bf16[8,32,2048]{2,1,0:T(8,128)(2,1)} %get-tuple-element.152), channel_id=1, source_target_pairs={{0,4},{2,6},{4,0},{6,2},{8,12},{10,14},{12,8},{14,10},{16,20},{18,... | collective-permute-start | bytes 3145736 | tf_op jit(solution)/shard_map/ppermute | solution.py:86
  240.5 33.6 %collective-permute-start.21 = (bf16[680,1024]{1,0:T(8,128)(2,1)}, bf16[680,1024]{1,0:T(8,128)(2,1)}, u32[]{:S(2)}, u32[]{:S(2)}) collective-permute-start(bf16[680,1024]{1,0:T(8,128)(2,1)} %get-tuple-element.160.refs_5_), channel_id=1, source_target_pairs={{0,2},{2,0},{4,6},{6,4},{8,10},{10,8},{12,14},{14,12},{16,18},{18,... | collective-permute-start | bytes 4177928 | tf_op jit(solution)/shard_map/ppermute | solution.py:86
  243.9 27.2 %collective-permute-start.17 = (bf16[4,32,2048]{2,1,0:T(8,128)(2,1)}, bf16[4,32,2048]{2,1,0:T(8,128)(2,1)}, u32[]{:S(2)}, u32[]{:S(2)}) collective-permute-start(bf16[4,32,2048]{2,1,0:T(8,128)(2,1)} %get-tuple-element.142.refs_11_), channel_id=1, source_target_pairs={{0,4},{2,6},{4,0},{6,2},{8,12},{10,14},{12,8},{14,10},{16,20},{18,... | collective-permute-start | bytes 1572872 | tf_op jit(solution)/shard_map/ppermute | solution.py:86
  245.5 25.6 %collective-permute-start.18 = (bf16[4,32,2048]{2,1,0:T(8,128)(2,1)}, bf16[4,32,2048]{2,1,0:T(8,128)(2,1)}, u32[]{:S(2)}, u32[]{:S(2)}) collective-permute-start(bf16[4,32,2048]{2,1,0:T(8,128)(2,1)} %get-tuple-element.144.refs_13_), channel_id=1, source_target_pairs={{0,1},{1,0},{2,3},{3,2},{4,5},{5,4},{6,7},{7,6},{8,9},{9,8},{10,11... | collective-permute-start | bytes 1572872 | tf_op jit(solution)/shard_map/ppermute | solution.py:86
  269.1 24.5 %collective-permute-start.25 = (bf16[4,32,2048]{2,1,0:T(8,128)(2,1)}, bf16[4,32,2048]{2,1,0:T(8,128)(2,1)}, u32[]{:S(2)}, u32[]{:S(2)}) collective-permute-start(bf16[4,32,2048]{2,1,0:T(8,128)(2,1)} %get-tuple-element.157.refs_14_), channel_id=1, source_target_pairs={{0,4},{2,6},{4,0},{6,2},{8,12},{10,14},{12,8},{14,10},{16,20},{18,... | collective-permute-start | bytes 1572872 | tf_op jit(solution)/shard_map/ppermute | solution.py:86
  270.4 23.2 %collective-permute-start.26 = (bf16[4,32,2048]{2,1,0:T(8,128)(2,1)}, bf16[4,32,2048]{2,1,0:T(8,128)(2,1)}, u32[]{:S(2)}, u32[]{:S(2)}) collective-permute-start(bf16[4,32,2048]{2,1,0:T(8,128)(2,1)} %get-tuple-element.159.refs_16_), channel_id=1, source_target_pairs={{0,1},{1,0},{2,3},{3,2},{4,5},{5,4},{6,7},{7,6},{8,9},{9,8},{10,11... | collective-permute-start | bytes 1572872 | tf_op jit(solution)/shard_map/ppermute | solution.py:86
  271.1 30.9 %collective-permute-start.23 = (bf16[3,680,512]{2,1,0:T(8,128)(2,1)}, bf16[3,680,512]{2,1,0:T(8,128)(2,1)}, u32[]{:S(2)}, u32[]{:S(2)}) collective-permute-start(bf16[3,680,512]{2,1,0:T(8,128)(2,1)} %get-tuple-element.145.refs_10_.refs_3_.refs_8_), channel_id=1, source_target_pairs={{0,2},{2,0},{4,6},{6,4},{8,10},{10,8},{12,14},{14,12},{16,18},{18,... | collective-permute-start | bytes 6266888 | tf_op jit(solution)/shard_map/ppermute | solution.py:86
  273.6 24.6 %collective-permute-start.24 = (bf16[2,64,2048]{2,1,0:T(8,128)(2,1)}, bf16[2,64,2048]{2,1,0:T(8,128)(2,1)}, u32[]{:S(2)}, u32[]{:S(2)}) collective-permute-start(bf16[2,64,2048]{2,1,0:T(8,128)(2,1)} %get-tuple-element.150.refs_12_), channel_id=1, source_target_pairs={{0,8},{2,10},{4,12},{6,14},{8,0},{10,2},{12,4},{14,6},{16,24},{18,... | collective-permute-start | bytes 1572872 | tf_op jit(solution)/shard_map/ppermute | solution.py:86
  293.7 19.8 %collective-permute-start.22 = (bf16[3,680,512]{2,1,0:T(8,128)(2,1)}, bf16[3,680,512]{2,1,0:T(8,128)(2,1)}, u32[]{:S(2)}, u32[]{:S(2)}) collective-permute-start(bf16[3,680,512]{2,1,0:T(8,128)(2,1)} %get-tuple-element.161.refs_9_.refs_3_), channel_id=1, source_target_pairs={{0,2},{2,0},{4,6},{6,4},{8,10},{10,8},{12,14},{14,12},{16,18},{18,... | collective-permute-start | bytes 6266888 | tf_op jit(solution)/shard_map/ppermute | solution.py:86
  296.6 24.1 %collective-permute-start.27 = (bf16[2,64,2048]{2,1,0:T(8,128)(2,1)}, bf16[2,64,2048]{2,1,0:T(8,128)(2,1)}, u32[]{:S(2)}, u32[]{:S(2)}) collective-permute-start(bf16[2,64,2048]{2,1,0:T(8,128)(2,1)} %get-tuple-element.169.refs_13_), channel_id=1, source_target_pairs={{0,8},{2,10},{4,12},{6,14},{8,0},{10,2},{12,4},{14,6},{16,24},{18,... | collective-permute-start | bytes 1572872 | tf_op jit(solution)/shard_map/ppermute | solution.py:86
  300.3 24.6 %collective-permute-start.28 = (bf16[1,64,2048]{2,1,0:T(8,128)(2,1)}, bf16[1,64,2048]{2,1,0:T(8,128)(2,1)}, u32[]{:S(2)}, u32[]{:S(2)}) collective-permute-start(bf16[1,64,2048]{2,1,0:T(8,128)(2,1)} %get-tuple-element.165.refs_11_), channel_id=1, source_target_pairs={{0,16},{2,18},{4,20},{6,22},{8,24},{10,26},{12,28},{14,30},{16,0},... | collective-permute-start | bytes 786440 | tf_op jit(solution)/shard_map/ppermute | solution.py:86
  311.3 26.4 %collective-permute-start.29 = (bf16[8,32,1280]{2,1,0:T(8,128)(2,1)}, bf16[8,32,1280]{2,1,0:T(8,128)(2,1)}, u32[]{:S(2)}, u32[]{:S(2)}) collective-permute-start(bf16[8,32,1280]{2,1,0:T(8,128)(2,1)} %get-tuple-element.177), channel_id=1, source_target_pairs={{0,1},{1,0},{2,3},{3,2},{4,5},{5,4},{6,7},{7,6},{8,9},{9,8},{10,11... | collective-permute-start | bytes 1966088 | tf_op jit(solution)/shard_map/ppermute | solution.py:86
  312.6 25.1 %collective-permute-start.30 = (bf16[8,32,1280]{2,1,0:T(8,128)(2,1)}, bf16[8,32,1280]{2,1,0:T(8,128)(2,1)}, u32[]{:S(2)}, u32[]{:S(2)}) collective-permute-start(bf16[8,32,1280]{2,1,0:T(8,128)(2,1)} %get-tuple-element.178), channel_id=1, source_target_pairs={{0,4},{2,6},{4,0},{6,2},{8,12},{10,14},{12,8},{14,10},{16,20},{18,... | collective-permute-start | bytes 1966088 | tf_op jit(solution)/shard_map/ppermute | solution.py:86
  324.9 18.7 %collective-permute-start.33 = (bf16[1,64,2048]{2,1,0:T(8,128)(2,1)}, bf16[1,64,2048]{2,1,0:T(8,128)(2,1)}, u32[]{:S(2)}, u32[]{:S(2)}) collective-permute-start(bf16[1,64,2048]{2,1,0:T(8,128)(2,1)} %get-tuple-element.174.refs_8_), channel_id=1, source_target_pairs={{0,16},{2,18},{4,20},{6,22},{8,24},{10,26},{12,28},{14,30},{16,0},... | collective-permute-start | bytes 786440 | tf_op jit(solution)/shard_map/ppermute | solution.py:86
  (40 other events, 629.1 us)
Sparse Core Ops, SparseCore 0:
  28.1 134.4 all-gather.1

commit v2 on v1

--- a/solution.py
+++ b/solution.py
@@ -38,9 +38,25 @@
     return [(first, min(size, rows - first)) for first in range(0, rows, size)]
 
 
-def call(kernel, out_shape, in_specs, out_specs, scratch, cost, name, grid=None, after=()):
-    extra = {} if grid is None else {"grid": grid}
-    count = len(in_specs)
+def call(
+    kernel, out_shape, in_specs, out_specs, scratch, cost, name, grid=None, after=(), scalars=0
+):
+    count = len(in_specs) + scalars
+    in_specs = list(in_specs) + [ANY] * len(after)
+    if scalars:
+        extra = {
+            "grid_spec": pltpu.PrefetchScalarGridSpec(
+                num_scalar_prefetch=scalars,
+                grid=grid,
+                in_specs=in_specs,
+                out_specs=out_specs,
+                scratch_shapes=scratch,
+            )
+        }
+    else:
+        extra = {"in_specs": in_specs, "out_specs": out_specs, "scratch_shapes": scratch}
+        if grid is not None:
+            extra["grid"] = grid
 
     def body(*refs):
         kernel(*refs[:count], *refs[count + len(after) :])
@@ -48,9 +64,6 @@
     run = pl.pallas_call(
         body,
         out_shape=out_shape,
-        in_specs=list(in_specs) + [ANY] * len(after),
-        out_specs=out_specs,
-        scratch_shapes=scratch,
         cost_estimate=pl.CostEstimate(
             flops=int(cost * 1e9), bytes_accessed=1 << 20, transcendentals=0
         ),
@@ -132,10 +145,14 @@
         self.held = [jnp.concatenate(pair, axis=0) for pair in zip(self.held, self.received)]
         self.launch()
 
-    def sides(self):
-        while self.step < self.cube.hops - 1:
-            self.advance()
-        return [self.held[0], self.received[0], self.held[1], self.received[1]]
+    def sides(self, others=None):
+        crossed = [self.cube.hop(held, self.cube.core) for held in self.held]
+        if others is not None:
+            self.received = behind(self.received, others)
+        got = []
+        for held, received, other in zip(self.held, self.received, crossed):
+            got += [held, received, other, self.cube.hop(received, self.cube.core)]
+        return got
 
 
 class Scatter:
@@ -187,14 +204,14 @@
 def make_pieces(cube, place, held, columns, target, sem):
     dp_at, tensor_at = place[0], place[1]
     first, count = columns
-    half = cube.devices // 2
+    quarter = cube.devices // 4
     copies = []
     for part, order in enumerate(cube.orders):
-        for side in range(2):
-            source = held[2 * part + side]
+        for side in range(4):
+            source = held[4 * part + side]
             rows = source.shape[1]
-            for item in range(half):
-                dp_mask, tensor_mask = cube.masks(order, side * half + item)
+            for item in range(quarter):
+                dp_mask, tensor_mask = cube.masks(order, side * quarter + item)
                 owner = jnp.bitwise_xor(dp_at, dp_mask)
                 tensor_owner = jnp.bitwise_xor(tensor_at, tensor_mask)
                 row = pl.multiple_of(owner * (2 * rows) + part * rows, 16)
@@ -228,11 +245,11 @@
 
 
 def front_kernel(
-    cube, pieces, place, tokens, parts, h0, h1, h2, h3,
+    cube, pieces, place, tokens, parts, h0, h1, h2, h3, h4, h5, h6, h7,
     mixed, query, key, value, r_query, r_key, modul, fc1_bias, head_scale,
     weight, sem, qv_bias,
 ):
-    copies = start_pieces(cube, place, (h0, h1, h2, h3), (0, weight.shape[2]), weight, sem)
+    copies = start_pieces(cube, place, (h0, h1, h2, h3, h4, h5, h6, h7), (0, weight.shape[2]), weight, sem)
     rows, width = tokens.shape
     local = width // cube.tensor_size
     wide = fc1_bias.shape[1] // cube.tensor_size
@@ -313,12 +330,12 @@
 
 
 def middle_kernel(
-    cube, place, heads, tokens, cotangent, modul, proj_bias, h0, h1, h2, h3,
+    cube, place, heads, tokens, cotangent, modul, proj_bias, h0, h1, h2, h3, h4, h5, h6, h7,
     branch, middle, mixed, gated_sum, weight, sem,
 ):
     rows, width = tokens.shape
     local = width // cube.tensor_size
-    copies = start_pieces(cube, place, (h0, h1, h2, h3), (3 * local, local), weight, sem)
+    copies = start_pieces(cube, place, (h0, h1, h2, h3, h4, h5, h6, h7), (3 * local, local), weight, sem)
     for copy in copies:
         copy.wait()
     gain = 1.0 + modul[3:4, :]
@@ -415,7 +432,7 @@
 
 
 def first_back_kernel(
-    cube, steps, place, grad_pre, matrix, middle, branch, cotangent, modul, h0, h1, h2, h3,
+    cube, steps, place, grad_pre, matrix, middle, branch, cotangent, modul, h0, h1, h2, h3, h4, h5, h6, h7,
     g_middle, gated, g_heads, sums,
     total, middle_here, branch_here, cotangent_here, gated_here, small, sem, small_sem,
 ):
@@ -428,7 +445,7 @@
         pltpu.make_async_copy(cotangent, cotangent_here, sem.at[2]),
     ]
     small_copies = make_pieces(
-        cube, place, (h0, h1, h2, h3), (3 * narrow, narrow), small, small_sem
+        cube, place, (h0, h1, h2, h3, h4, h5, h6, h7), (3 * narrow, narrow), small, small_sem
     )
     outs = [
         pltpu.make_async_copy(total, g_middle, sem.at[0]),
@@ -495,40 +512,28 @@
             )
 
 
-def pieces_out(cube, place, item, table, outs, sem, first, count):
-    dp_at, tensor_at = place[0], place[1]
-    tensor_rel = jnp.bitwise_xor(tensor_at, item)
+def piece_copies(cube, place, relative, table, outs, sem, first, count):
+    dp_at = place[0]
+    item = jnp.bitwise_xor(place[1], relative)
     piece = table.shape[1] * 2 // cube.dp_size
-    for pair in range(cube.dp_size // 2):
-        dp_rel = jnp.bitwise_xor(dp_at - dp_at % 2, 2 * pair)
-        for part, order in enumerate(cube.sum_orders):
-            keep, send = outs[2 * part], outs[2 * part + 1]
-            half, rows = keep.shape[0], keep.shape[1]
-            index = cube.index(order, dp_rel, tensor_rel)
-            source = table.at[item, pl.ds(pair * piece + part * rows, rows), :]
-            away = index >= half
-
-            @pl.when(away)
-            def _():
+    copies = []
+    for part, order in enumerate(cube.sum_orders):
+        half, rows = outs[2 * part].shape[0], outs[2 * part].shape[1]
+        for index in range(2 * half):
+            dp_mask, tensor_mask = cube.masks(order, index)
+            if tensor_mask != relative:
+                continue
+            pair = jnp.bitwise_xor(dp_at, dp_mask) // 2
+            row = pl.multiple_of(pair * piece + part * rows, 16)
+            out = outs[2 * part + index // half]
+            copies.append(
                 pltpu.make_async_copy(
-                    source, send.at[index - half, :, pl.ds(first, count)], sem
-                ).start()
-
-            @pl.when(jnp.logical_not(away))
-            def _():
-                pltpu.make_async_copy(
-                    source, keep.at[index, :, pl.ds(first, count)], sem
-                ).start()
-
-
-def wait_pieces(cube, item, table, outs, sem, first, count):
-    for pair in range(cube.dp_size // 2):
-        for part in range(2):
-            keep = outs[2 * part]
-            rows = keep.shape[1]
-            pltpu.make_async_copy(
-                table.at[item, pl.ds(0, rows), :], keep.at[0, :, pl.ds(first, count)], sem
-            ).wait()
+                    table.at[item, pl.ds(row, rows), :],
+                    out.at[index % half, :, pl.ds(first, count)],
+                    sem,
+                )
+            )
+    return copies
 
 
 def wide_grad_kernel(cube, per, place, left, left_far, right, right_far, *refs):
@@ -542,19 +547,20 @@
         core_rows(cube, place, flip.at[1], left_far)
 
     got = (dot(flip[0], right[...]) + dot(flip[1], right_far[...])).astype(BF16)
-    for item in range(cube.tensor_size):
-        for part in range(per):
-
-            @pl.when(step == item * per + part)
-            def _():
-                table[item, :, part * block : (part + 1) * block] = got
-                if part == per - 1:
-                    pieces_out(cube, place, item, table, outs, sem, 0, local)
-
-    @pl.when(step == cube.tensor_size * per - 1)
-    def _():
-        for item in range(cube.tensor_size):
-            wait_pieces(cube, item, table, outs, sem, 0, local)
+    item = jnp.bitwise_xor(place[1], step // per)
+    table[item, :, pl.ds(pl.multiple_of((step % per) * block, LANES), block)] = got
+    for relative in range(cube.tensor_size):
+        copies = piece_copies(cube, place, relative, table, outs, sem, 0, local)
+
+        @pl.when(step == relative * per + per - 1)
+        def _():
+            for copy in copies:
+                copy.start()
+
+        @pl.when(step == cube.tensor_size * per - 1)
+        def _():
+            for copy in copies:
+                copy.wait()
 
 
 def qkv_grad_kernel(cube, with_proj, place, mixed, mixed_far, grads, grads_far, *refs):
@@ -592,29 +598,36 @@
             copy.start()
     for copy in copies[2:4]:
         copy.wait()
-    for item in range(cube.tensor_size):
-        cols = slice(item * local, (item + 1) * local)
+    started = []
+    for relative in range(cube.tensor_size):
+        item = jnp.bitwise_xor(place[1], relative)
+        cols = pl.ds(pl.multiple_of(item * local, LANES), local)
         for kind in range(3):
             table[item, :, kind * local : (kind + 1) * local] = (
                 dot(flip[0], own[kind, :, cols]) + dot(flip[1], far[kind, :, cols])
             ).astype(BF16)
-        pieces_out(cube, place, item, table, outs, sem, 0, 3 * local)
+        group = piece_copies(cube, place, relative, table, outs, sem, 0, 3 * local)
+        for copy in group:
+            copy.start()
+        started += group
     if with_proj:
         narrow = small.shape[2]
         for copy in late + copies[4:]:
             copy.wait()
         core_rows(cube, place, flip.at[0], mat)
         core_rows(cube, place, flip.at[1], mat_far)
-        for item in range(cube.tensor_size):
-            cols = slice(item * narrow, (item + 1) * narrow)
+        for relative in range(cube.tensor_size):
+            item = jnp.bitwise_xor(place[1], relative)
+            cols = pl.ds(pl.multiple_of(item * narrow, LANES), narrow)
             small[item] = (dot(flip[0], sides[:, cols]) + dot(flip[1], sides_far[:, cols])).astype(
                 BF16
             )
-            pieces_out(cube, place, item, small, outs, sem, 3 * local, narrow)
-        for item in range(cube.tensor_size):
-            wait_pieces(cube, item, small, outs, sem, 3 * local, narrow)
-    for item in range(cube.tensor_size):
-        wait_pieces(cube, item, table, outs, sem, 0, 3 * local)
+            group = piece_copies(cube, place, relative, small, outs, sem, 3 * local, narrow)
+            for copy in group:
+                copy.start()
+            started += group
+    for copy in started:
+        copy.wait()
 
 
 def split_into(base, lanes, start, values):
@@ -684,7 +697,8 @@
     sums[1:2, :] = jnp.sum(d_value.astype(F32), axis=0, keepdims=True)
 
 
-def last_kernel(cube, splits, place, modul, tokens, g_middle, h0, h1, h2, h3, *refs):
+def last_kernel(cube, splits, place, modul, tokens, g_middle, *refs):
+    held, refs = refs[:8], refs[8:]
     grads, refs = refs[: len(splits)], refs[len(splits) :]
     grad_tokens, sums, weight, left, tokens_here, middle_here, sem, in_sem = refs[:8]
     grads_here = refs[8:]
@@ -698,7 +712,7 @@
     ]
     for copy in copies:
         copy.start()
-    pieces = make_pieces(cube, place, (h0, h1, h2, h3), (0, weight.shape[2]), weight, sem)
+    pieces = make_pieces(cube, place, held, (0, weight.shape[2]), weight, sem)
     for copy in pieces:
         copy.start()
     for which, (start, size) in enumerate(splits):
@@ -860,8 +874,6 @@
         jnp.concatenate([qkv_weight.reshape(piece_rows, 3 * narrow), proj_weight.T], axis=1),
     )
     narrow_gather.advance(cond_own)
-    while narrow_gather.step < cube.hops - 4:
-        narrow_gather.advance()
     wide_shard = jnp.concatenate([fc1_weight, fc2_weight.T], axis=1)
     wide_all = lax.all_gather(
         behind(wide_shard, narrow_gather.held), AXES, axis=0, tiled=True
@@ -886,8 +898,7 @@
             [modul_part + bias_part, jnp.broadcast_to(rest, (devices, rest.shape[1]))], axis=1
         )
     ).reshape(dp_size, tensor_size, -1)
-    narrow_gather.advance(parts)
-    held = narrow_gather.sides()
+    held = narrow_gather.sides(parts)
     rest = parts[:, 0, 6 * narrow :]
     proj_bias_full = rest[:, :piece_rows].reshape(1, width)
     fc2_bias_full = rest[:, piece_rows : 2 * piece_rows].reshape(1, width)
@@ -905,7 +916,7 @@
         [half_shape(rows, width)] * 4
         + [shape(rows, width)] * 2
         + [shape(8, width), shape(1, hidden_width), shape(1, width)],
-        [SMEM, VMEM, VMEM] + [ANY] * 4,
+        [SMEM, VMEM, VMEM] + [ANY] * 8,
         [VMEM] * 9,
         [
             pltpu.VMEM((tensor_size, width, 3 * narrow), BF16),
@@ -931,7 +942,7 @@
     branch, middle, mixed_two, gated_sum = call(
         functools.partial(middle_kernel, cube),
         [shape(rows, width)] * 2 + [half_shape(2, rows, width), shape(1, width)],
-        [SMEM] + [VMEM] * 5 + [ANY] * 4,
+        [SMEM] + [VMEM] * 5 + [ANY] * 8,
         [VMEM] * 4,
         [pltpu.VMEM((tensor_size, width, narrow), BF16), dma],
         10, "middle", after=[mixed_one_far],
@@ -982,14 +993,21 @@
     flip_scratch = pltpu.VMEM((2, width // 2, rows), BF16)
     grad_scratch = [flip_scratch, pltpu.VMEM((tensor_size, width // 2, wide), BF16), dma]
 
+    def mixed_far_part(which):
+        return pl.BlockSpec((None, rows, width), lambda i, at: (which, 0, 0))
+
+    side_relative = pl.BlockSpec(
+        (rows, block), lambda i, at: (0, jnp.bitwise_xor(at[1], i // per) * per + i % per)
+    )
+
     def wide_grad(which, right, right_far, name, after):
         return call(
             functools.partial(wide_grad_kernel, cube, per),
             piece_shapes(wide),
-            [SMEM] + [mixed_part(which)] * 2 + [side] * 2,
+            [mixed_far_part(which)] * 2 + [side_relative] * 2,
             [ANY] * 4,
             grad_scratch,
-            300, name, grid=(wide_steps,), after=after,
+            300, name, grid=(wide_steps,), after=after, scalars=1,
         )(place, mixed_two, mixed_two_far, right, right_far)
 
     outs = wide_grad(1, hidden, hidden_far, "fc2_grad", [grad_pre])
@@ -1010,7 +1028,7 @@
             half_shape(rows, width),
             shape(8, width),
         ],
-        [SMEM, side, wide_block(0)] + [ANY] * 3 + [eight_rows] + [ANY] * 4,
+        [SMEM, side, wide_block(0)] + [ANY] * 3 + [eight_rows] + [ANY] * 8,
         [ANY, ANY, whole_half, eight_rows],
         [
             full, full, full, full_half, full_half,
@@ -1101,7 +1119,7 @@
     grad_tokens, sums_zero = call(
         functools.partial(last_kernel, cube, splits),
         [half_shape(rows, width), shape(8, width)],
-        [SMEM, VMEM] + [ANY] * (6 + len(splits)),
+        [SMEM, VMEM] + [ANY] * (10 + len(splits)),
         [VMEM] * 2,
         [
             pltpu.VMEM((tensor_size, width, 3 * narrow), BF16),
@@ -1112,10 +1130,7 @@
         400, "last", after=after,
     )(place, modul, tokens, g_middle, *held, *qkv_grads)
 
-    landed = qkv_sum.received
-    qkv_sum.advance(sums_zero)
-    fc2_own = fc2_sum.finish(sums_zero)
-    fc1_own = fc1_sum.finish(sums_zero)
+    near_out = qkv_sum.advance(sums_zero)
 
     late = call(
         functools.partial(pack_kernel, splits),
@@ -1124,8 +1139,11 @@
         VMEM,
         [pltpu.VMEM((dp_size, 2 * LANES), F32)],
         1, "pack",
-    )(sums_one, gamma_sum, sums_zero, fc1_bias_sum, gated_sum, *all_sums)
-    late = to_all(behind(late, landed), BACK_AXES)
+    )(sums_one, gamma_sum, behind(sums_zero, near_out), fc1_bias_sum, gated_sum, *all_sums)
+    far_out = qkv_sum.advance(late)
+    late = behind(to_all(late, BACK_AXES), far_out)
+    fc2_own = fc2_sum.finish(far_out)
+    fc1_own = fc1_sum.finish(far_out)
     grad_modul_all = late[:, : 6 * narrow]
     late_sum = jnp.sum(late.astype(F32), axis=0)
     grad_ada_bias = late_sum[: 6 * narrow].reshape(6, narrow)
@@ -1141,8 +1159,8 @@
         cond_back, grad_modul_all, (((0,), (0,)), ((), ())), preferred_element_type=F32
     ).reshape(piece_rows, 6, narrow)
     cond_part = dot_nt(grad_modul_all, ada_flat)
-    qkv_sum.advance(cond_part)
-    own = qkv_sum.finish()
+    cond_all = to_all(cond_part, BACK_AXES).reshape(tensor_size, dp_size, piece_rows)
+    own = qkv_sum.finish(cond_part)
     parts_own, first = [], 0
     for which, (start, size) in enumerate(splits):
         parts_own.append(own[:, first : first + 3 * size].reshape(piece_rows, 3, size))
@@ -1152,7 +1170,6 @@
             first += narrow
     qkv_own = jnp.concatenate(parts_own, axis=2)
 
-    cond_all = to_all(cond_part, BACK_AXES).reshape(tensor_size, dp_size, piece_rows)
     cond_image = lax.dynamic_slice_in_dim(cond_float, tensor_at, 1, axis=0)
     unused, silu_back = jax.vjp(jax.nn.silu, cond_image)
     grad_condition = silu_back(jnp.sum(cond_all, axis=0).reshape(1, width))[0]

time: 421 us -> 418 us (level)
  waiting for transfers between devices: 82.6 us -> 91.5 us
  local copies, waits for them, and re-layouts: 26.1 us -> 17.6 us
  other arithmetic: 17.5 us -> 13 us
    all_to_all x3, waiting for transfers between devices: 29 us -> 42.1 us  [to_all(): return lax.all_to_all(values, axes, split_axis=0, concat_axis=0, tiled=True)]
    ppermute x38 -> x40, waiting for transfers between devices: 42.1 us -> 34.4 us  [hop(): return lax.ppermute(values, axis, [(i, i ^ mask) for i in range(size)])]
    concatenate x2 -> x0, local copies, waits for them, and re-layouts: 4.61 us -> none  [advance(): jnp.concatenate(pair, axis=0)]
    ppermute x38 -> x40, starting transfers between devices: 36.1 us -> 34.6 us  [hop(): return lax.ppermute(values, axis, [(i, i ^ mask) for i in range(size)])]
  transfers between devices with their start and end apart: 43 -> 45, of which waited for: 11 -> 14; matrix products, arithmetic and copies ran while one was open for 8% -> 6% of each run, Pallas kernels for 52% -> 52%
where the time goes in v2:
time: 418 us; the launch traced here: 414 us
  Pallas kernels  219 us (52%)
  waiting for transfers between devices  91.5 us (22%)
  starting transfers between devices  55.4 us (13%)
  local copies, waits for them, and re-layouts  17.6 us (4%)
  between operations  15.3 us (4%)
  other arithmetic  13 us (3%)
    pallas_call x15, Pallas kernels, call(): return lambda *operands: run(*operands, *after)  195 us
    all_to_all x3, waiting for transfers between devices, to_all(): return lax.all_to_all(values, axes, split_axis=0, concat_axis=0, tiled=True)  42.1 us
    ppermute x40, starting transfers between devices, hop(): return lax.ppermute(values, axis, [(i, i ^ mask) for i in range(size)])  34.6 us
    ppermute x40, waiting for transfers between devices, hop(): return lax.ppermute(values, axis, [(i, i ^ mask) for i in range(size)])  34.4 us
    pallas_call x9, Pallas kernels, add_pieces(): pl.pallas_call(functools.partial(add_kernel, parts, groups, merge), out_s...  23.7 us
    all_to_all x3, starting transfers between devices, to_all(): return lax.all_to_all(values, axes, split_axis=0, concat_axis=0, tiled=True)  14.6 us
    all_gather x1, waiting for transfers between devices, local(): lax.all_gather(behind(wide_shard, narrow_gather.held), AXES, axis=0, tile...  10.6 us
  transfers between devices with their start and end apart: 45, of which 14 were waited for; matrix products, arithmetic and copies ran while one was open for 6% of the time, Pallas kernels for 52%

profile of v2, /device:TPU:0, one launch (start us, length us, event | category | flops | bytes accessed | tf_op | source)
XLA Modules:
  0.0 413.5 jit_solution(3553986857266621371)
XLA Ops:
  9.0 4.1 collective-permute-start
  14.6 6.2 %all-to-all-start = ((bf16[16,2,64]{2,1,0:T(2,128)(2,1)}), bf16[16,2,64]{2,1,0:T(2,128)(2,1)S(1)}, u32[]{:S(2)}, u32[]{:S(2)}) async-start(bf16[16,2,64]{2,1,0:T(2,128)(2,1)} %bitcast.68), calls=%async_computation | async-start | bytes 16384 | tf_op jit(solution)/shard_map/all_to_all | solution.py:866
  22.7 4.4 %all-to-all-done = bf16[16,2,64]{2,1,0:T(2,128)(2,1)S(1)} async-done(((bf16[16,2,64]{2,1,0:T(2,128)(2,1)}), bf16[16,2,64]{2,1,0:T(2,128)(2,1)S(1)}, u32[]{:S(2)}, u32[]{:S(2)}) %all-to-all-start) | async-done | bytes 4128 | tf_op jit(solution)/shard_map/all_to_all | solution.py:866
  29.8 7.0 %collective-permute-done.5 = bf16[2,32,2048]{2,1,0:T(8,128)(2,1)S(1)} collective-permute-done((bf16[2,32,2048]{2,1,0:T(8,128)(2,1)S(1)}, bf16[2,32,2048]{2,1,0:T(8,128)(2,1)S(1)}, u32[]{:S(2)}, u32[]{:S(2)}) %collective-permute-start.5) | collective-permute-done | bytes 262176 | tf_op jit(solution)/shard_map/ppermute | solution.py:99
  38.4 8.9 %collective-permute-done.2 = bf16[2,32,2048]{2,1,0:T(8,128)(2,1)S(1)} collective-permute-done((bf16[2,32,2048]{2,1,0:T(8,128)(2,1)S(1)}, bf16[2,32,2048]{2,1,0:T(8,128)(2,1)S(1)}, u32[]{:S(2)}, u32[]{:S(2)}) %collective-permute-start.2) | collective-permute-done | bytes 262176 | tf_op jit(solution)/shard_map/ppermute | solution.py:99
  54.1 6.2 %collective-permute-done.3 = bf16[4,32,2048]{2,1,0:T(8,128)(2,1)} collective-permute-done((bf16[4,32,2048]{2,1,0:T(8,128)(2,1)S(1)}, bf16[4,32,2048]{2,1,0:T(8,128)(2,1)}, u32[]{:S(2)}, u32[]{:S(2)}) %collective-permute-start.3) | collective-permute-done | bytes 524320 | tf_op jit(solution)/shard_map/ppermute | solution.py:99
  64.2 7.1 %all-to-all-start.1 = ((f32[32,1,3456]{2,1,0:T(1,128)}), f32[32,1,3456]{2,1,0:T(1,128)S(1)}, u32[]{:S(2)}, u32[]{:S(2)}) async-start(f32[32,1,3456]{2,1,0:T(1,128)} %copy.89), calls=%async_computation.1 | async-start | bytes 884736 | tf_op jit(solution)/shard_map/all_to_all | solution.py:845
  71.3 27.6 %all-to-all-done.1 = f32[32,1,3456]{2,1,0:T(1,128)S(1)} async-done(((f32[32,1,3456]{2,1,0:T(1,128)}), f32[32,1,3456]{2,1,0:T(1,128)S(1)}, u32[]{:S(2)}, u32[]{:S(2)}) %all-to-all-start.1) | async-done | bytes 442400 | tf_op jit(solution)/shard_map/all_to_all | solution.py:845
  107.9 15.9 %front.1 = (bf16[680,1024]{1,0:T(8,128)(2,1)}, bf16[680,1024]{1,0:T(8,128)(2,1)}, bf16[680,1024]{1,0:T(8,128)(2,1)}, bf16[680,1024]{1,0:T(8,128)(2,1)}, f32[680,...) custom-call(s32[2]{0:T(128)} %pad_add_fusion.refs_0_, ...), custom_call_target="tpu_custom_call" | custom-call | flops 16000000000 | bytes 1048576 | tf_op jit(solution)/shard_map/front/pallas_call | solution.py:74
  124.0 14.8 %attend.1 = (bf16[680,1024]{1,0:T(8,128)(2,1)}, f32[680,1024]{1,0:T(8,128)}) custom-call(bf16[680,1024]{1,0:T(8,128)(2,1)} %get-tuple-element.116.refs_0_, bf16[680,1024]{1,0:T(8,128)(2,1)} %get-tuple-element.117.refs_1_, bf16[680,1024]{1,0:T(8,128)(2,1)} %get-tuple-element.118.refs_2_, bf16[680,128]{1,0:T(8,128)(2,1)} %copy.91.refs_3_.refs_8_, ...), custom_call_target="tpu_custom_call" | custom-call | flops 20000000000 | bytes 1048576 | tf_op jit(solution)/shard_map/attend/pallas_call | solution.py:74
  140.4 10.2 %middle.1 = (f32[680,1024]{1,0:T(8,128)}, f32[680,1024]{1,0:T(8,128)}, bf16[2,680,1024]{2,1,0:T(8,128)(2,1)}, f32[1,1024]{1,0:T(1,128)}) custom-call(s32[2]{0:T(128)} %pad_add_fusion.refs_0_, bf16[680,1024]{1,0:T(8,128)(2,1)} %get-tuple-element.119.refs_1_.refs_7_, bf16[680,1024]{1,0:T(8,128)(2,1)} %refs_2_.5, bf16[680,1024]{1,0:T(8,128)(2,1)} %refs_2_.4, ...), custom_call_target="tpu_custom_call" | custom-call | flops 10000000000 | bytes 1048576 | tf_op jit(solution)/shard_map/middle/pallas_call | solution.py:74
  151.6 10.6 %all-gather.2.cloned.1.call-done = bf16[2048,4096]{1,0:T(8,128)(2,1)} async-done(((bf16[64,4096]{1,0:T(8,128)(2,1)}), bf16[2048,4096]{1,0:T(8,128)(2,1)}) %all-gather.2.cloned.1.call-update) | async-done | bytes 16777232 | tf_op jit(solution)/shard_map/all_gather | solution.py:878
  162.2 15.6 %hidden.1 = (bf16[680,4096]{1,0:T(8,128)(2,1)}, f32[680,4096]{1,0:T(8,128)}) custom-call(bf16[2,680,1024]{2,1,0:T(8,128)(2,1)} %get-tuple-element.122.refs_0_.refs_1_, f32[1,4096]{1,0:T(1,128)} %get-tuple-element.123.refs_1_, bf16[16,2,64,4096]{3,2,1,0:T(8,128)(2,1)} %bitcast.92, bf16[680,1024]{1,0:T(8,128)(2,1)} %collective-permute-done.13.refs_3_.refs_8_), custom_call_target="tpu_custom_call" | custom-call | flops 20000000000 | bytes 1048576 | tf_op jit(solution)/shard_map/hidden/pallas_call | solution.py:74
  179.6 12.4 %pre_back.1 = (bf16[680,4096]{1,0:T(8,128)(2,1)}, f32[1,4096]{1,0:T(1,128)}) custom-call(f32[680,4096]{1,0:T(8,128)} %get-tuple-element.127.refs_0_, bf16[2,680,1024]{2,1,0:T(8,128)(2,1)} %get-tuple-element.122.refs_0_.refs_1_, bf16[16,2,64,4096]{3,2,1,0:T(8,128)(2,1)} %bitcast.93, bf16[2,680,1024]{2,1,0:T(8,128)(2,1)} %copy-done.19), custom_call_target="tpu_custom_call" | custom-call | flops 299999985664 | bytes 1048576 | tf_op jit(solution)/shard_map/pre_back/pallas_call | solution.py:74
  192.2 13.6 %fc2_grad.1 = (bf16[8,32,2048]{2,1,0:T(8,128)(2,1)}, bf16[8,32,2048]{2,1,0:T(8,128)(2,1)}, bf16[8,32,2048]{2,1,0:T(8,128)(2,1)}, bf16[8,32,2048]{2,1,0:T(8,128)(2,1)}) custom-call(s32[2]{0:T(128)} %pad_add_fusion.refs_0_, bf16[2,680,1024]{2,1,0:T(8,128)(2,1)} %get-tuple-element.122.refs_0_.refs_1_, bf16[2,680,1024]{2,1,0:T(8,128)(2,1)} %copy-done.19, ...), custom_call_target="tpu_custom_call" | custom-call | flops 299999985664 | bytes 1048576 | tf_op jit(solution)/shard_map/fc2_grad/pallas_call | solution.py:74
  207.9 13.6 %fc1_grad.1 = (bf16[8,32,2048]{2,1,0:T(8,128)(2,1)}, bf16[8,32,2048]{2,1,0:T(8,128)(2,1)}, bf16[8,32,2048]{2,1,0:T(8,128)(2,1)}, bf16[8,32,2048]{2,1,0:T(8,128)(2,1)}) custom-call(s32[2]{0:T(128)} %pad_add_fusion.refs_0_, bf16[2,680,1024]{2,1,0:T(8,128)(2,1)} %get-tuple-element.122.refs_0_.refs_1_, bf16[2,680,1024]{2,1,0:T(8,128)(2,1)} %copy-done.19, ...), custom_call_target="tpu_custom_call" | custom-call | flops 299999985664 | bytes 1048576 | tf_op jit(solution)/shard_map/fc1_grad/pallas_call | solution.py:74
  223.6 16.8 %first_back.1 = (f32[680,1024]{1,0:T(8,128)}, bf16[680,1024]{1,0:T(8,128)(2,1)}, bf16[680,1024]{1,0:T(8,128)(2,1)}, f32[8,1024]{1,0:T(8,128)}) custom-call(s32[2]{0:T(128)} %pad_add_fusion.refs_0_, bf16[680,4096]{1,0:T(8,128)(2,1)} %get-tuple-element.128.refs_5_.refs_3_.refs_1_, bf16[16,2,64,4096]{3,2,1,0:T(8,128)(2,1)} %bitcast.94, ...), custom_call_target="tpu_custom_call" | custom-call | flops 499999997952 | bytes 1048576 | tf_op jit(solution)/shard_map/first_back/pallas_call | solution.py:74
  246.0 19.5 %attend_back.2 = (bf16[3,680,512]{2,1,0:T(8,128)(2,1)}, f32[8,512]{1,0:T(8,128)}) custom-call(bf16[680,1024]{1,0:T(8,128)(2,1)} %get-tuple-element.116.refs_0_, bf16[680,1024]{1,0:T(8,128)(2,1)} %get-tuple-element.117.refs_1_, bf16[680,1024]{1,0:T(8,128)(2,1)} %get-tuple-element.118.refs_2_, bf16[680,1024]{1,0:T(8,128)(2,1)} %get-tuple-element.132.refs_3_, ...), custom_call_target="tpu_custom_call" | custom-call | flops 399999991808 | bytes 1048576 | tf_op jit(solution)/shard_map/attend_back/pallas_call | solution.py:74
  273.9 19.7 %attend_back.3 = (bf16[3,680,512]{2,1,0:T(8,128)(2,1)}, f32[8,512]{1,0:T(8,128)}) custom-call(bf16[680,1024]{1,0:T(8,128)(2,1)} %get-tuple-element.116.refs_0_, bf16[680,1024]{1,0:T(8,128)(2,1)} %get-tuple-element.117.refs_1_, bf16[680,1024]{1,0:T(8,128)(2,1)} %get-tuple-element.118.refs_2_, bf16[680,1024]{1,0:T(8,128)(2,1)} %get-tuple-element.132.refs_3_, ...), custom_call_target="tpu_custom_call" | custom-call | flops 399999991808 | bytes 1048576 | tf_op jit(solution)/shard_map/attend_back/pallas_call | solution.py:74
  301.6 9.1 %qkv_grad.2 = (bf16[8,32,1280]{2,1,0:T(8,128)(2,1)}, bf16[8,32,1280]{2,1,0:T(8,128)(2,1)}, bf16[8,32,1280]{2,1,0:T(8,128)(2,1)}, bf16[8,32,1280]{2,1,0:T(8,128)(2,1)}) custom-call(s32[2]{0:T(128)} %pad_add_fusion.refs_0_, bf16[680,1024]{1,0:T(8,128)(2,1)} %get-tuple-element.121.refs_1_, bf16[680,1024]{1,0:T(8,128)(2,1)} %copy-done.20, ...), custom_call_target="tpu_custom_call" | custom-call | flops 199999995904 | bytes 1048576 | tf_op jit(solution)/shard_map/qkv_grad/pallas_call | solution.py:74
  312.8 7.3 %qkv_grad.3 = (bf16[8,32,768]{2,1,0:T(8,128)(2,1)}, bf16[8,32,768]{2,1,0:T(8,128)(2,1)}, bf16[8,32,768]{2,1,0:T(8,128)(2,1)}, bf16[8,32,768]{2,1,0:T(8,128)(2,1)}) custom-call(s32[2]{0:T(128)} %pad_add_fusion.refs_0_, bf16[680,1024]{1,0:T(8,128)(2,1)} %get-tuple-element.121.refs_1_, bf16[680,1024]{1,0:T(8,128)(2,1)} %copy-done.20, ...), custom_call_target="tpu_custom_call" | custom-call | flops 199999995904 | bytes 1048576 | tf_op jit(solution)/shard_map/qkv_grad/pallas_call | solution.py:74
  325.7 11.7 %output.1 = (bf16[680,1024]{1,0:T(8,128)(2,1)}, f32[1,1024]{1,0:T(1,128)}) custom-call(bf16[680,4096]{1,0:T(8,128)(2,1)} %get-tuple-element.125.refs_3_.refs_0_, bf16[16,2,64,4096]{3,2,1,0:T(8,128)(2,1)} %bitcast.95, bf16[680,1024]{1,0:T(8,128)(2,1)} %refs_2_.4, f32[680,1024]{1,0:T(8,128)} %get-tuple-element.126.refs_3_, ...), custom_call_target="tpu_custom_call" | custom-call | flops 399999991808 | bytes 1048576 | tf_op jit(solution)/shard_map/output/pallas_call | solution.py:74
  343.0 13.0 %last.1 = (bf16[680,1024]{1,0:T(8,128)(2,1)}, f32[8,1024]{1,0:T(8,128)}) custom-call(s32[2]{0:T(128)} %pad_add_fusion.refs_0_, f32[8,1024]{1,0:T(8,128)} %get-tuple-element.120.refs_4_.refs_6_.refs_1_, bf16[680,1024]{1,0:T(8,128)(2,1)} %refs_2_.5, f32[680,1024]{1,0:T(8,128)} %get-tuple-element.178.refs_3_, bf16[8,32,2048]{2,1,0:T(8,128)(2,1)} %copy-done.6, ...), custom_call_target="tpu_custom_call" | custom-call | flops 399999991808 | bytes 1048576 | tf_op jit(solution)/shard_map/last/pallas_call | solution.py:74
  376.8 12.0 %all-to-all-done.2 = bf16[32,2,3712]{2,1,0:T(2,128)(2,1)S(1)} async-done(((bf16[32,2,3712]{2,1,0:T(2,128)(2,1)}), bf16[32,2,3712]{2,1,0:T(2,128)(2,1)S(1)}, u32[]{:S(2)}, u32[]{:S(2)}) %all-to-all-start.2) | async-done | bytes 475168 | tf_op jit(solution)/shard_map/all_to_all | solution.py:845
  (216 shorter events, 110.9 us)
Async XLA Ops:
  20.8 141.4 %all-gather.2.cloned.1.call-start = ((), (), s32[]{:S(2)}) async-start(), calls=%async_computation.4 | async-start | bytes 17301504 | tf_op jit(solution)/shard_map/all_gather | solution.py:878
  28.1 19.2 %collective-permute-start.2 = (bf16[2,32,2048]{2,1,0:T(8,128)(2,1)S(1)}, bf16[2,32,2048]{2,1,0:T(8,128)(2,1)S(1)}, u32[]{:S(2)}, u32[]{:S(2)}) collective-permute-start(bf16[2,32,2048]{2,1,0:T(8,128)(2,1)S(1)} %pad_maximum_fusion.6), channel_id=1, source_target_pairs={{0,8},{2,10},{4,12},{6,14},{8,0},{10,2},{12,4},{14,6},{16,24},{18,... | collective-permute-start | bytes 786440 | tf_op jit(solution)/shard_map/ppermute | solution.py:99
  53.4 47.5 %collective-permute-start.7 = (bf16[8,32,2048]{2,1,0:T(8,128)(2,1)S(1)}, bf16[8,32,2048]{2,1,0:T(8,128)(2,1)}, u32[]{:S(2)}, u32[]{:S(2)}) collective-permute-start(bf16[8,32,2048]{2,1,0:T(8,128)(2,1)S(1)} %pad_maximum_fusion.1.refs_7_.refs_10_.refs_11_.refs_8_), channel_id=1, source_target_pairs={{0,4},{2,6},{4,0},{6,2},{8,12},{10,14},{12,8},{14,10},{16,20},{18,... | collective-permute-start | bytes 3145736 | tf_op jit(solution)/shard_map/ppermute | solution.py:99
  61.5 39.4 %collective-permute-start.4 = (bf16[8,32,2048]{2,1,0:T(8,128)(2,1)S(1)}, bf16[8,32,2048]{2,1,0:T(8,128)(2,1)}, u32[]{:S(2)}, u32[]{:S(2)}) collective-permute-start(bf16[8,32,2048]{2,1,0:T(8,128)(2,1)S(1)} %pad_maximum_fusion.refs_3_.refs_6_.refs_7_.refs_4_), channel_id=1, source_target_pairs={{0,1},{1,0},{2,3},{3,2},{4,5},{5,4},{6,7},{7,6},{8,9},{9,8},{10,11... | collective-permute-start | bytes 3145736 | tf_op jit(solution)/shard_map/ppermute | solution.py:99
  64.2 34.8 %all-to-all-start.1 = ((f32[32,1,3456]{2,1,0:T(1,128)}), f32[32,1,3456]{2,1,0:T(1,128)S(1)}, u32[]{:S(2)}, u32[]{:S(2)}) async-start(f32[32,1,3456]{2,1,0:T(1,128)} %copy.89), calls=%async_computation.1 | async-start | bytes 884736 | tf_op jit(solution)/shard_map/all_to_all | solution.py:845
  150.6 27.4 %collective-permute-start.14 = (bf16[2,680,1024]{2,1,0:T(8,128)(2,1)}, bf16[2,680,1024]{2,1,0:T(8,128)(2,1)S(1)}, u32[]{:S(2)}, u32[]{:S(2)}) collective-permute-start(bf16[2,680,1024]{2,1,0:T(8,128)(2,1)} %get-tuple-element.122.refs_0_.refs_1_), channel_id=1, source_target_pairs={{0,2},{2,0},{4,6},{6,4},{8,10},{10,8},{12,14},{14,12},{16,18},{18,... | collective-permute-start | bytes 8355848 | tf_op jit(solution)/shard_map/ppermute | solution.py:99
  205.8 34.8 %collective-permute-start.17 = (bf16[8,32,2048]{2,1,0:T(8,128)(2,1)}, bf16[8,32,2048]{2,1,0:T(8,128)(2,1)}, u32[]{:S(2)}, u32[]{:S(2)}) collective-permute-start(bf16[8,32,2048]{2,1,0:T(8,128)(2,1)} %get-tuple-element.137), channel_id=1, source_target_pairs={{0,1},{1,0},{2,3},{3,2},{4,5},{5,4},{6,7},{7,6},{8,9},{9,8},{10,11... | collective-permute-start | bytes 3145736 | tf_op jit(solution)/shard_map/ppermute | solution.py:99
  207.1 33.4 %collective-permute-start.18 = (bf16[8,32,2048]{2,1,0:T(8,128)(2,1)}, bf16[8,32,2048]{2,1,0:T(8,128)(2,1)}, u32[]{:S(2)}, u32[]{:S(2)}) collective-permute-start(bf16[8,32,2048]{2,1,0:T(8,128)(2,1)} %get-tuple-element.138), channel_id=1, source_target_pairs={{0,4},{2,6},{4,0},{6,2},{8,12},{10,14},{12,8},{14,10},{16,20},{18,... | collective-permute-start | bytes 3145736 | tf_op jit(solution)/shard_map/ppermute | solution.py:99
  221.5 44.0 %collective-permute-start.21 = (bf16[8,32,2048]{2,1,0:T(8,128)(2,1)}, bf16[8,32,2048]{2,1,0:T(8,128)(2,1)}, u32[]{:S(2)}, u32[]{:S(2)}) collective-permute-start(bf16[8,32,2048]{2,1,0:T(8,128)(2,1)} %get-tuple-element.153), channel_id=1, source_target_pairs={{0,1},{1,0},{2,3},{3,2},{4,5},{5,4},{6,7},{7,6},{8,9},{9,8},{10,11... | collective-permute-start | bytes 3145736 | tf_op jit(solution)/shard_map/ppermute | solution.py:99
  223.1 42.4 %collective-permute-start.22 = (bf16[8,32,2048]{2,1,0:T(8,128)(2,1)}, bf16[8,32,2048]{2,1,0:T(8,128)(2,1)}, u32[]{:S(2)}, u32[]{:S(2)}) collective-permute-start(bf16[8,32,2048]{2,1,0:T(8,128)(2,1)} %get-tuple-element.154), channel_id=1, source_target_pairs={{0,4},{2,6},{4,0},{6,2},{8,12},{10,14},{12,8},{14,10},{16,20},{18,... | collective-permute-start | bytes 3145736 | tf_op jit(solution)/shard_map/ppermute | solution.py:99
  240.5 33.4 %collective-permute-start.23 = (bf16[680,1024]{1,0:T(8,128)(2,1)}, bf16[680,1024]{1,0:T(8,128)(2,1)}, u32[]{:S(2)}, u32[]{:S(2)}) collective-permute-start(bf16[680,1024]{1,0:T(8,128)(2,1)} %get-tuple-element.162.refs_5_), channel_id=1, source_target_pairs={{0,2},{2,0},{4,6},{6,4},{8,10},{10,8},{12,14},{14,12},{16,18},{18,... | collective-permute-start | bytes 4177928 | tf_op jit(solution)/shard_map/ppermute | solution.py:99
  243.9 27.0 %collective-permute-start.19 = (bf16[4,32,2048]{2,1,0:T(8,128)(2,1)}, bf16[4,32,2048]{2,1,0:T(8,128)(2,1)}, u32[]{:S(2)}, u32[]{:S(2)}) collective-permute-start(bf16[4,32,2048]{2,1,0:T(8,128)(2,1)} %get-tuple-element.144.refs_11_), channel_id=1, source_target_pairs={{0,4},{2,6},{4,0},{6,2},{8,12},{10,14},{12,8},{14,10},{16,20},{18,... | collective-permute-start | bytes 1572872 | tf_op jit(solution)/shard_map/ppermute | solution.py:99
  245.4 25.5 %collective-permute-start.20 = (bf16[4,32,2048]{2,1,0:T(8,128)(2,1)}, bf16[4,32,2048]{2,1,0:T(8,128)(2,1)}, u32[]{:S(2)}, u32[]{:S(2)}) collective-permute-start(bf16[4,32,2048]{2,1,0:T(8,128)(2,1)} %get-tuple-element.146.refs_13_), channel_id=1, source_target_pairs={{0,1},{1,0},{2,3},{3,2},{4,5},{5,4},{6,7},{7,6},{8,9},{9,8},{10,11... | collective-permute-start | bytes 1572872 | tf_op jit(solution)/shard_map/ppermute | solution.py:99
  268.8 24.8 %collective-permute-start.27 = (bf16[4,32,2048]{2,1,0:T(8,128)(2,1)}, bf16[4,32,2048]{2,1,0:T(8,128)(2,1)}, u32[]{:S(2)}, u32[]{:S(2)}) collective-permute-start(bf16[4,32,2048]{2,1,0:T(8,128)(2,1)} %get-tuple-element.159.refs_14_), channel_id=1, source_target_pairs={{0,4},{2,6},{4,0},{6,2},{8,12},{10,14},{12,8},{14,10},{16,20},{18,... | collective-permute-start | bytes 1572872 | tf_op jit(solution)/shard_map/ppermute | solution.py:99
  270.1 23.5 %collective-permute-start.28 = (bf16[4,32,2048]{2,1,0:T(8,128)(2,1)}, bf16[4,32,2048]{2,1,0:T(8,128)(2,1)}, u32[]{:S(2)}, u32[]{:S(2)}) collective-permute-start(bf16[4,32,2048]{2,1,0:T(8,128)(2,1)} %get-tuple-element.161.refs_16_), channel_id=1, source_target_pairs={{0,1},{1,0},{2,3},{3,2},{4,5},{5,4},{6,7},{7,6},{8,9},{9,8},{10,11... | collective-permute-start | bytes 1572872 | tf_op jit(solution)/shard_map/ppermute | solution.py:99
  270.9 30.7 %collective-permute-start.25 = (bf16[3,680,512]{2,1,0:T(8,128)(2,1)}, bf16[3,680,512]{2,1,0:T(8,128)(2,1)}, u32[]{:S(2)}, u32[]{:S(2)}) collective-permute-start(bf16[3,680,512]{2,1,0:T(8,128)(2,1)} %get-tuple-element.147.refs_10_.refs_3_.refs_12_), channel_id=1, source_target_pairs={{0,2},{2,0},{4,6},{6,4},{8,10},{10,8},{12,14},{14,12},{16,18},{18,... | collective-permute-start | bytes 6266888 | tf_op jit(solution)/shard_map/ppermute | solution.py:99
  273.4 24.6 %collective-permute-start.26 = (bf16[2,64,2048]{2,1,0:T(8,128)(2,1)}, bf16[2,64,2048]{2,1,0:T(8,128)(2,1)}, u32[]{:S(2)}, u32[]{:S(2)}) collective-permute-start(bf16[2,64,2048]{2,1,0:T(8,128)(2,1)} %get-tuple-element.152.refs_12_), channel_id=1, source_target_pairs={{0,8},{2,10},{4,12},{6,14},{8,0},{10,2},{12,4},{14,6},{16,24},{18,... | collective-permute-start | bytes 1572872 | tf_op jit(solution)/shard_map/ppermute | solution.py:99
  293.6 19.2 %collective-permute-start.24 = (bf16[3,680,512]{2,1,0:T(8,128)(2,1)}, bf16[3,680,512]{2,1,0:T(8,128)(2,1)}, u32[]{:S(2)}, u32[]{:S(2)}) collective-permute-start(bf16[3,680,512]{2,1,0:T(8,128)(2,1)} %get-tuple-element.163.refs_9_.refs_3_.refs_13_), channel_id=1, source_target_pairs={{0,2},{2,0},{4,6},{6,4},{8,10},{10,8},{12,14},{14,12},{16,18},{18,... | collective-permute-start | bytes 6266888 | tf_op jit(solution)/shard_map/ppermute | solution.py:99
  296.4 23.7 %collective-permute-start.29 = (bf16[2,64,2048]{2,1,0:T(8,128)(2,1)}, bf16[2,64,2048]{2,1,0:T(8,128)(2,1)}, u32[]{:S(2)}, u32[]{:S(2)}) collective-permute-start(bf16[2,64,2048]{2,1,0:T(8,128)(2,1)} %get-tuple-element.171.refs_13_), channel_id=1, source_target_pairs={{0,8},{2,10},{4,12},{6,14},{8,0},{10,2},{12,4},{14,6},{16,24},{18,... | collective-permute-start | bytes 1572872 | tf_op jit(solution)/shard_map/ppermute | solution.py:99
  300.1 24.2 %collective-permute-start.30 = (bf16[1,64,2048]{2,1,0:T(8,128)(2,1)}, bf16[1,64,2048]{2,1,0:T(8,128)(2,1)}, u32[]{:S(2)}, u32[]{:S(2)}) collective-permute-start(bf16[1,64,2048]{2,1,0:T(8,128)(2,1)} %get-tuple-element.167.refs_11_), channel_id=1, source_target_pairs={{0,16},{2,18},{4,20},{6,22},{8,24},{10,26},{12,28},{14,30},{16,0},... | collective-permute-start | bytes 786440 | tf_op jit(solution)/shard_map/ppermute | solution.py:99
  310.7 26.7 %collective-permute-start.31 = (bf16[8,32,1280]{2,1,0:T(8,128)(2,1)}, bf16[8,32,1280]{2,1,0:T(8,128)(2,1)}, u32[]{:S(2)}, u32[]{:S(2)}) collective-permute-start(bf16[8,32,1280]{2,1,0:T(8,128)(2,1)} %get-tuple-element.179), channel_id=1, source_target_pairs={{0,1},{1,0},{2,3},{3,2},{4,5},{5,4},{6,7},{7,6},{8,9},{9,8},{10,11... | collective-permute-start | bytes 1966088 | tf_op jit(solution)/shard_map/ppermute | solution.py:99
  312.0 25.4 %collective-permute-start.32 = (bf16[8,32,1280]{2,1,0:T(8,128)(2,1)}, bf16[8,32,1280]{2,1,0:T(8,128)(2,1)}, u32[]{:S(2)}, u32[]{:S(2)}) collective-permute-start(bf16[8,32,1280]{2,1,0:T(8,128)(2,1)} %get-tuple-element.180), channel_id=1, source_target_pairs={{0,4},{2,6},{4,0},{6,2},{8,12},{10,14},{12,8},{14,10},{16,20},{18,... | collective-permute-start | bytes 1966088 | tf_op jit(solution)/shard_map/ppermute | solution.py:99
  364.0 24.8 %all-to-all-start.2 = ((bf16[32,2,3712]{2,1,0:T(2,128)(2,1)}), bf16[32,2,3712]{2,1,0:T(2,128)(2,1)S(1)}, u32[]{:S(2)}, u32[]{:S(2)}) async-start(bf16[32,2,3712]{2,1,0:T(2,128)(2,1)} %reshape.258), calls=%async_computation.2 | async-start | bytes 950272 | tf_op jit(solution)/shard_map/all_to_all | solution.py:845
  373.2 19.8 %collective-permute-start.39 = (bf16[1,64,2048]{2,1,0:T(8,128)(2,1)}, bf16[1,64,2048]{2,1,0:T(8,128)(2,1)S(1)}, u32[]{:S(2)}, u32[]{:S(2)}) collective-permute-start(bf16[1,64,2048]{2,1,0:T(8,128)(2,1)} %get-tuple-element.205), channel_id=1, source_target_pairs={{0,16},{2,18},{4,20},{6,22},{8,24},{10,26},{12,28},{14,30},{16,0},... | collective-permute-start | bytes 786440 | tf_op jit(solution)/shard_map/ppermute | solution.py:99
  (44 other events, 708.2 us)
Sparse Core Ops, SparseCore 0:
  27.4 134.7 all-gather.1

commit v3 on v2

--- a/solution.py
+++ b/solution.py
@@ -232,9 +232,9 @@
     return centred, lax.rsqrt(variance + NORM_EPS)
 
 
-def head_ones():
-    row = lax.broadcasted_iota(jnp.int32, (LANES, LANES), 0) // HEAD
-    col = lax.broadcasted_iota(jnp.int32, (LANES, LANES), 1) // HEAD
+def head_ones(lanes=LANES):
+    row = lax.broadcasted_iota(jnp.int32, (lanes, lanes), 0) // HEAD
+    col = lax.broadcasted_iota(jnp.int32, (lanes, lanes), 1) // HEAD
     return (row == col).astype(BF16)
 
 
@@ -647,7 +647,7 @@
     low = lanes < HEAD
     inner = lanes % HEAD
     q, k, v, g = query[...], key[...], value[...], grad[...]
-    ones = head_ones()
+    ones = head_ones(2 * LANES)
     spare = 16
     zero = jnp.zeros((rows, LANES), BF16)
     one = jnp.ones((rows, LANES), BF16)
@@ -684,14 +684,14 @@
     d_key = dot(pairs[step : step + rows, :], sides[1])
     d_query = flat_query[...].T
     scale = head_scale[0:1, :]
-    unit = q.astype(F32) / scale
-    along = head_sums(unit * d_query, ones)
+    unit = q.astype(F32) * (1.0 / scale)
+    unit_key = k.astype(F32)
+    both = head_sums(jnp.concatenate([unit * d_query, unit_key * d_key], axis=1), ones)
+    along, along_key = both[:, :LANES], both[:, LANES:]
     out = (r_query[...] * scale * (d_query - unit * along)).astype(BF16)
     grads[0] = out
     sums[0:1, :] = jnp.sum(out.astype(F32), axis=0, keepdims=True)
     sums[2:3, :] = jnp.sum(along, axis=0, keepdims=True)
-    unit_key = k.astype(F32)
-    along_key = head_sums(unit_key * d_key, ones)
     grads[1] = (r_key[...] * (d_key - unit_key * along_key)).astype(BF16)
     grads[2] = d_value
     sums[1:2, :] = jnp.sum(d_value.astype(F32), axis=0, keepdims=True)

time: 418 us -> 419 us (level)
  no operation moved by 1% of the time
where the time goes in v3:
time: 419 us; the launch traced here: 414 us
  Pallas kernels  220 us (53%)
  waiting for transfers between devices  91.5 us (22%)
  starting transfers between devices  55.3 us (13%)
  local copies, waits for them, and re-layouts  17.6 us (4%)
  between operations  15.3 us (4%)
  other arithmetic  13 us (3%)
    pallas_call x15, Pallas kernels, call(): return lambda *operands: run(*operands, *after)  195 us
    all_to_all x3, waiting for transfers between devices, to_all(): return lax.all_to_all(values, axes, split_axis=0, concat_axis=0, tiled=True)  42.1 us
    ppermute x40, starting transfers between devices, hop(): return lax.ppermute(values, axis, [(i, i ^ mask) for i in range(size)])  34.5 us
    ppermute x40, waiting for transfers between devices, hop(): return lax.ppermute(values, axis, [(i, i ^ mask) for i in range(size)])  34.4 us
    pallas_call x9, Pallas kernels, add_pieces(): pl.pallas_call(functools.partial(add_kernel, parts, groups, merge), out_s...  24.1 us
    all_to_all x3, starting transfers between devices, to_all(): return lax.all_to_all(values, axes, split_axis=0, concat_axis=0, tiled=True)  14.6 us
    all_gather x1, waiting for transfers between devices, local(): lax.all_gather(behind(wide_shard, narrow_gather.held), AXES, axis=0, tile...  10.6 us
  transfers between devices with their start and end apart: 45, of which 14 were waited for; matrix products, arithmetic and copies ran while one was open for 6% of the time, Pallas kernels for 52%

profile of v3, /device:TPU:0, one launch (start us, length us, event | category | flops | bytes accessed | tf_op | source)
XLA Modules:
  0.0 414.5 jit_solution(5338788281806216699)
XLA Ops:
  9.0 4.1 collective-permute-start
  14.6 6.2 %all-to-all-start = ((bf16[16,2,64]{2,1,0:T(2,128)(2,1)}), bf16[16,2,64]{2,1,0:T(2,128)(2,1)S(1)}, u32[]{:S(2)}, u32[]{:S(2)}) async-start(bf16[16,2,64]{2,1,0:T(2,128)(2,1)} %bitcast.68), calls=%async_computation | async-start | bytes 16384 | tf_op jit(solution)/shard_map/all_to_all | solution.py:866
  22.7 4.4 %all-to-all-done = bf16[16,2,64]{2,1,0:T(2,128)(2,1)S(1)} async-done(((bf16[16,2,64]{2,1,0:T(2,128)(2,1)}), bf16[16,2,64]{2,1,0:T(2,128)(2,1)S(1)}, u32[]{:S(2)}, u32[]{:S(2)}) %all-to-all-start) | async-done | bytes 4128 | tf_op jit(solution)/shard_map/all_to_all | solution.py:866
  29.8 7.0 %collective-permute-done.5 = bf16[2,32,2048]{2,1,0:T(8,128)(2,1)S(1)} collective-permute-done((bf16[2,32,2048]{2,1,0:T(8,128)(2,1)S(1)}, bf16[2,32,2048]{2,1,0:T(8,128)(2,1)S(1)}, u32[]{:S(2)}, u32[]{:S(2)}) %collective-permute-start.5) | collective-permute-done | bytes 262176 | tf_op jit(solution)/shard_map/ppermute | solution.py:99
  38.4 8.9 %collective-permute-done.2 = bf16[2,32,2048]{2,1,0:T(8,128)(2,1)S(1)} collective-permute-done((bf16[2,32,2048]{2,1,0:T(8,128)(2,1)S(1)}, bf16[2,32,2048]{2,1,0:T(8,128)(2,1)S(1)}, u32[]{:S(2)}, u32[]{:S(2)}) %collective-permute-start.2) | collective-permute-done | bytes 262176 | tf_op jit(solution)/shard_map/ppermute | solution.py:99
  54.1 6.2 %collective-permute-done.3 = bf16[4,32,2048]{2,1,0:T(8,128)(2,1)} collective-permute-done((bf16[4,32,2048]{2,1,0:T(8,128)(2,1)S(1)}, bf16[4,32,2048]{2,1,0:T(8,128)(2,1)}, u32[]{:S(2)}, u32[]{:S(2)}) %collective-permute-start.3) | collective-permute-done | bytes 524320 | tf_op jit(solution)/shard_map/ppermute | solution.py:99
  64.2 7.1 %all-to-all-start.1 = ((f32[32,1,3456]{2,1,0:T(1,128)}), f32[32,1,3456]{2,1,0:T(1,128)S(1)}, u32[]{:S(2)}, u32[]{:S(2)}) async-start(f32[32,1,3456]{2,1,0:T(1,128)} %copy.89), calls=%async_computation.1 | async-start | bytes 884736 | tf_op jit(solution)/shard_map/all_to_all | solution.py:845
  71.3 27.6 %all-to-all-done.1 = f32[32,1,3456]{2,1,0:T(1,128)S(1)} async-done(((f32[32,1,3456]{2,1,0:T(1,128)}), f32[32,1,3456]{2,1,0:T(1,128)S(1)}, u32[]{:S(2)}, u32[]{:S(2)}) %all-to-all-start.1) | async-done | bytes 442400 | tf_op jit(solution)/shard_map/all_to_all | solution.py:845
  107.9 15.9 %front.1 = (bf16[680,1024]{1,0:T(8,128)(2,1)}, bf16[680,1024]{1,0:T(8,128)(2,1)}, bf16[680,1024]{1,0:T(8,128)(2,1)}, bf16[680,1024]{1,0:T(8,128)(2,1)}, f32[680,...) custom-call(s32[2]{0:T(128)} %pad_add_fusion.refs_0_, ...), custom_call_target="tpu_custom_call" | custom-call | flops 16000000000 | bytes 1048576 | tf_op jit(solution)/shard_map/front/pallas_call | solution.py:74
  124.0 14.8 %attend.1 = (bf16[680,1024]{1,0:T(8,128)(2,1)}, f32[680,1024]{1,0:T(8,128)}) custom-call(bf16[680,1024]{1,0:T(8,128)(2,1)} %get-tuple-element.116.refs_0_, bf16[680,1024]{1,0:T(8,128)(2,1)} %get-tuple-element.117.refs_1_, bf16[680,1024]{1,0:T(8,128)(2,1)} %get-tuple-element.118.refs_2_, bf16[680,128]{1,0:T(8,128)(2,1)} %copy.91.refs_3_.refs_8_, ...), custom_call_target="tpu_custom_call" | custom-call | flops 20000000000 | bytes 1048576 | tf_op jit(solution)/shard_map/attend/pallas_call | solution.py:74
  140.4 10.2 %middle.1 = (f32[680,1024]{1,0:T(8,128)}, f32[680,1024]{1,0:T(8,128)}, bf16[2,680,1024]{2,1,0:T(8,128)(2,1)}, f32[1,1024]{1,0:T(1,128)}) custom-call(s32[2]{0:T(128)} %pad_add_fusion.refs_0_, bf16[680,1024]{1,0:T(8,128)(2,1)} %get-tuple-element.119.refs_1_.refs_7_, bf16[680,1024]{1,0:T(8,128)(2,1)} %refs_2_.5, bf16[680,1024]{1,0:T(8,128)(2,1)} %refs_2_.4, ...), custom_call_target="tpu_custom_call" | custom-call | flops 10000000000 | bytes 1048576 | tf_op jit(solution)/shard_map/middle/pallas_call | solution.py:74
  151.6 10.6 %all-gather.2.cloned.1.call-done = bf16[2048,4096]{1,0:T(8,128)(2,1)} async-done(((bf16[64,4096]{1,0:T(8,128)(2,1)}), bf16[2048,4096]{1,0:T(8,128)(2,1)}) %all-gather.2.cloned.1.call-update) | async-done | bytes 16777232 | tf_op jit(solution)/shard_map/all_gather | solution.py:878
  162.2 15.6 %hidden.1 = (bf16[680,4096]{1,0:T(8,128)(2,1)}, f32[680,4096]{1,0:T(8,128)}) custom-call(bf16[2,680,1024]{2,1,0:T(8,128)(2,1)} %get-tuple-element.122.refs_0_.refs_1_, f32[1,4096]{1,0:T(1,128)} %get-tuple-element.123.refs_1_, bf16[16,2,64,4096]{3,2,1,0:T(8,128)(2,1)} %bitcast.92, bf16[680,1024]{1,0:T(8,128)(2,1)} %collective-permute-done.13.refs_3_.refs_8_), custom_call_target="tpu_custom_call" | custom-call | flops 20000000000 | bytes 1048576 | tf_op jit(solution)/shard_map/hidden/pallas_call | solution.py:74
  179.6 12.4 %pre_back.1 = (bf16[680,4096]{1,0:T(8,128)(2,1)}, f32[1,4096]{1,0:T(1,128)}) custom-call(f32[680,4096]{1,0:T(8,128)} %get-tuple-element.127.refs_0_, bf16[2,680,1024]{2,1,0:T(8,128)(2,1)} %get-tuple-element.122.refs_0_.refs_1_, bf16[16,2,64,4096]{3,2,1,0:T(8,128)(2,1)} %bitcast.93, bf16[2,680,1024]{2,1,0:T(8,128)(2,1)} %copy-done.19), custom_call_target="tpu_custom_call" | custom-call | flops 299999985664 | bytes 1048576 | tf_op jit(solution)/shard_map/pre_back/pallas_call | solution.py:74
  192.2 13.6 %fc2_grad.1 = (bf16[8,32,2048]{2,1,0:T(8,128)(2,1)}, bf16[8,32,2048]{2,1,0:T(8,128)(2,1)}, bf16[8,32,2048]{2,1,0:T(8,128)(2,1)}, bf16[8,32,2048]{2,1,0:T(8,128)(2,1)}) custom-call(s32[2]{0:T(128)} %pad_add_fusion.refs_0_, bf16[2,680,1024]{2,1,0:T(8,128)(2,1)} %get-tuple-element.122.refs_0_.refs_1_, bf16[2,680,1024]{2,1,0:T(8,128)(2,1)} %copy-done.19, ...), custom_call_target="tpu_custom_call" | custom-call | flops 299999985664 | bytes 1048576 | tf_op jit(solution)/shard_map/fc2_grad/pallas_call | solution.py:74
  207.9 13.6 %fc1_grad.1 = (bf16[8,32,2048]{2,1,0:T(8,128)(2,1)}, bf16[8,32,2048]{2,1,0:T(8,128)(2,1)}, bf16[8,32,2048]{2,1,0:T(8,128)(2,1)}, bf16[8,32,2048]{2,1,0:T(8,128)(2,1)}) custom-call(s32[2]{0:T(128)} %pad_add_fusion.refs_0_, bf16[2,680,1024]{2,1,0:T(8,128)(2,1)} %get-tuple-element.122.refs_0_.refs_1_, bf16[2,680,1024]{2,1,0:T(8,128)(2,1)} %copy-done.19, ...), custom_call_target="tpu_custom_call" | custom-call | flops 299999985664 | bytes 1048576 | tf_op jit(solution)/shard_map/fc1_grad/pallas_call | solution.py:74
  223.6 16.8 %first_back.1 = (f32[680,1024]{1,0:T(8,128)}, bf16[680,1024]{1,0:T(8,128)(2,1)}, bf16[680,1024]{1,0:T(8,128)(2,1)}, f32[8,1024]{1,0:T(8,128)}) custom-call(s32[2]{0:T(128)} %pad_add_fusion.refs_0_, bf16[680,4096]{1,0:T(8,128)(2,1)} %get-tuple-element.128.refs_5_.refs_3_.refs_1_, bf16[16,2,64,4096]{3,2,1,0:T(8,128)(2,1)} %bitcast.94, ...), custom_call_target="tpu_custom_call" | custom-call | flops 499999997952 | bytes 1048576 | tf_op jit(solution)/shard_map/first_back/pallas_call | solution.py:74
  246.0 20.0 %attend_back.2 = (bf16[3,680,512]{2,1,0:T(8,128)(2,1)}, f32[8,512]{1,0:T(8,128)}) custom-call(bf16[680,1024]{1,0:T(8,128)(2,1)} %get-tuple-element.116.refs_0_, bf16[680,1024]{1,0:T(8,128)(2,1)} %get-tuple-element.117.refs_1_, bf16[680,1024]{1,0:T(8,128)(2,1)} %get-tuple-element.118.refs_2_, bf16[680,1024]{1,0:T(8,128)(2,1)} %get-tuple-element.132.refs_3_, ...), custom_call_target="tpu_custom_call" | custom-call | flops 399999991808 | bytes 1048576 | tf_op jit(solution)/shard_map/attend_back/pallas_call | solution.py:74
  274.5 20.0 %attend_back.3 = (bf16[3,680,512]{2,1,0:T(8,128)(2,1)}, f32[8,512]{1,0:T(8,128)}) custom-call(bf16[680,1024]{1,0:T(8,128)(2,1)} %get-tuple-element.116.refs_0_, bf16[680,1024]{1,0:T(8,128)(2,1)} %get-tuple-element.117.refs_1_, bf16[680,1024]{1,0:T(8,128)(2,1)} %get-tuple-element.118.refs_2_, bf16[680,1024]{1,0:T(8,128)(2,1)} %get-tuple-element.132.refs_3_, ...), custom_call_target="tpu_custom_call" | custom-call | flops 399999991808 | bytes 1048576 | tf_op jit(solution)/shard_map/attend_back/pallas_call | solution.py:74
  302.5 9.1 %qkv_grad.2 = (bf16[8,32,1280]{2,1,0:T(8,128)(2,1)}, bf16[8,32,1280]{2,1,0:T(8,128)(2,1)}, bf16[8,32,1280]{2,1,0:T(8,128)(2,1)}, bf16[8,32,1280]{2,1,0:T(8,128)(2,1)}) custom-call(s32[2]{0:T(128)} %pad_add_fusion.refs_0_, bf16[680,1024]{1,0:T(8,128)(2,1)} %get-tuple-element.121.refs_1_, bf16[680,1024]{1,0:T(8,128)(2,1)} %copy-done.20, ...), custom_call_target="tpu_custom_call" | custom-call | flops 199999995904 | bytes 1048576 | tf_op jit(solution)/shard_map/qkv_grad/pallas_call | solution.py:74
  313.8 7.3 %qkv_grad.3 = (bf16[8,32,768]{2,1,0:T(8,128)(2,1)}, bf16[8,32,768]{2,1,0:T(8,128)(2,1)}, bf16[8,32,768]{2,1,0:T(8,128)(2,1)}, bf16[8,32,768]{2,1,0:T(8,128)(2,1)}) custom-call(s32[2]{0:T(128)} %pad_add_fusion.refs_0_, bf16[680,1024]{1,0:T(8,128)(2,1)} %get-tuple-element.121.refs_1_, bf16[680,1024]{1,0:T(8,128)(2,1)} %copy-done.20, ...), custom_call_target="tpu_custom_call" | custom-call | flops 199999995904 | bytes 1048576 | tf_op jit(solution)/shard_map/qkv_grad/pallas_call | solution.py:74
  326.6 11.5 %output.1 = (bf16[680,1024]{1,0:T(8,128)(2,1)}, f32[1,1024]{1,0:T(1,128)}) custom-call(bf16[680,4096]{1,0:T(8,128)(2,1)} %get-tuple-element.125.refs_3_.refs_0_, bf16[16,2,64,4096]{3,2,1,0:T(8,128)(2,1)} %bitcast.95, bf16[680,1024]{1,0:T(8,128)(2,1)} %refs_2_.4, f32[680,1024]{1,0:T(8,128)} %get-tuple-element.126.refs_3_, ...), custom_call_target="tpu_custom_call" | custom-call | flops 399999991808 | bytes 1048576 | tf_op jit(solution)/shard_map/output/pallas_call | solution.py:74
  343.9 13.0 %last.1 = (bf16[680,1024]{1,0:T(8,128)(2,1)}, f32[8,1024]{1,0:T(8,128)}) custom-call(s32[2]{0:T(128)} %pad_add_fusion.refs_0_, f32[8,1024]{1,0:T(8,128)} %get-tuple-element.120.refs_4_.refs_6_.refs_1_, bf16[680,1024]{1,0:T(8,128)(2,1)} %refs_2_.5, f32[680,1024]{1,0:T(8,128)} %get-tuple-element.178.refs_3_, bf16[8,32,2048]{2,1,0:T(8,128)(2,1)} %copy-done.6, ...), custom_call_target="tpu_custom_call" | custom-call | flops 399999991808 | bytes 1048576 | tf_op jit(solution)/shard_map/last/pallas_call | solution.py:74
  377.8 12.0 %all-to-all-done.2 = bf16[32,2,3712]{2,1,0:T(2,128)(2,1)S(1)} async-done(((bf16[32,2,3712]{2,1,0:T(2,128)(2,1)}), bf16[32,2,3712]{2,1,0:T(2,128)(2,1)S(1)}, u32[]{:S(2)}, u32[]{:S(2)}) %all-to-all-start.2) | async-done | bytes 475168 | tf_op jit(solution)/shard_map/all_to_all | solution.py:845
  (216 shorter events, 111.4 us)
Async XLA Ops:
  20.8 141.4 %all-gather.2.cloned.1.call-start = ((), (), s32[]{:S(2)}) async-start(), calls=%async_computation.4 | async-start | bytes 17301504 | tf_op jit(solution)/shard_map/all_gather | solution.py:878
  28.1 19.2 %collective-permute-start.2 = (bf16[2,32,2048]{2,1,0:T(8,128)(2,1)S(1)}, bf16[2,32,2048]{2,1,0:T(8,128)(2,1)S(1)}, u32[]{:S(2)}, u32[]{:S(2)}) collective-permute-start(bf16[2,32,2048]{2,1,0:T(8,128)(2,1)S(1)} %pad_maximum_fusion.6), channel_id=1, source_target_pairs={{0,8},{2,10},{4,12},{6,14},{8,0},{10,2},{12,4},{14,6},{16,24},{18,... | collective-permute-start | bytes 786440 | tf_op jit(solution)/shard_map/ppermute | solution.py:99
  53.4 47.5 %collective-permute-start.7 = (bf16[8,32,2048]{2,1,0:T(8,128)(2,1)S(1)}, bf16[8,32,2048]{2,1,0:T(8,128)(2,1)}, u32[]{:S(2)}, u32[]{:S(2)}) collective-permute-start(bf16[8,32,2048]{2,1,0:T(8,128)(2,1)S(1)} %pad_maximum_fusion.1.refs_7_.refs_10_.refs_11_.refs_8_), channel_id=1, source_target_pairs={{0,4},{2,6},{4,0},{6,2},{8,12},{10,14},{12,8},{14,10},{16,20},{18,... | collective-permute-start | bytes 3145736 | tf_op jit(solution)/shard_map/ppermute | solution.py:99
  61.5 39.4 %collective-permute-start.4 = (bf16[8,32,2048]{2,1,0:T(8,128)(2,1)S(1)}, bf16[8,32,2048]{2,1,0:T(8,128)(2,1)}, u32[]{:S(2)}, u32[]{:S(2)}) collective-permute-start(bf16[8,32,2048]{2,1,0:T(8,128)(2,1)S(1)} %pad_maximum_fusion.refs_3_.refs_6_.refs_7_.refs_4_), channel_id=1, source_target_pairs={{0,1},{1,0},{2,3},{3,2},{4,5},{5,4},{6,7},{7,6},{8,9},{9,8},{10,11... | collective-permute-start | bytes 3145736 | tf_op jit(solution)/shard_map/ppermute | solution.py:99
  64.2 34.8 %all-to-all-start.1 = ((f32[32,1,3456]{2,1,0:T(1,128)}), f32[32,1,3456]{2,1,0:T(1,128)S(1)}, u32[]{:S(2)}, u32[]{:S(2)}) async-start(f32[32,1,3456]{2,1,0:T(1,128)} %copy.89), calls=%async_computation.1 | async-start | bytes 884736 | tf_op jit(solution)/shard_map/all_to_all | solution.py:845
  150.6 27.4 %collective-permute-start.14 = (bf16[2,680,1024]{2,1,0:T(8,128)(2,1)}, bf16[2,680,1024]{2,1,0:T(8,128)(2,1)S(1)}, u32[]{:S(2)}, u32[]{:S(2)}) collective-permute-start(bf16[2,680,1024]{2,1,0:T(8,128)(2,1)} %get-tuple-element.122.refs_0_.refs_1_), channel_id=1, source_target_pairs={{0,2},{2,0},{4,6},{6,4},{8,10},{10,8},{12,14},{14,12},{16,18},{18,... | collective-permute-start | bytes 8355848 | tf_op jit(solution)/shard_map/ppermute | solution.py:99
  205.8 34.8 %collective-permute-start.17 = (bf16[8,32,2048]{2,1,0:T(8,128)(2,1)}, bf16[8,32,2048]{2,1,0:T(8,128)(2,1)}, u32[]{:S(2)}, u32[]{:S(2)}) collective-permute-start(bf16[8,32,2048]{2,1,0:T(8,128)(2,1)} %get-tuple-element.137), channel_id=1, source_target_pairs={{0,1},{1,0},{2,3},{3,2},{4,5},{5,4},{6,7},{7,6},{8,9},{9,8},{10,11... | collective-permute-start | bytes 3145736 | tf_op jit(solution)/shard_map/ppermute | solution.py:99
  207.1 33.4 %collective-permute-start.18 = (bf16[8,32,2048]{2,1,0:T(8,128)(2,1)}, bf16[8,32,2048]{2,1,0:T(8,128)(2,1)}, u32[]{:S(2)}, u32[]{:S(2)}) collective-permute-start(bf16[8,32,2048]{2,1,0:T(8,128)(2,1)} %get-tuple-element.138), channel_id=1, source_target_pairs={{0,4},{2,6},{4,0},{6,2},{8,12},{10,14},{12,8},{14,10},{16,20},{18,... | collective-permute-start | bytes 3145736 | tf_op jit(solution)/shard_map/ppermute | solution.py:99
  221.5 44.4 %collective-permute-start.21 = (bf16[8,32,2048]{2,1,0:T(8,128)(2,1)}, bf16[8,32,2048]{2,1,0:T(8,128)(2,1)}, u32[]{:S(2)}, u32[]{:S(2)}) collective-permute-start(bf16[8,32,2048]{2,1,0:T(8,128)(2,1)} %get-tuple-element.153), channel_id=1, source_target_pairs={{0,1},{1,0},{2,3},{3,2},{4,5},{5,4},{6,7},{7,6},{8,9},{9,8},{10,11... | collective-permute-start | bytes 3145736 | tf_op jit(solution)/shard_map/ppermute | solution.py:99
  223.1 42.9 %collective-permute-start.22 = (bf16[8,32,2048]{2,1,0:T(8,128)(2,1)}, bf16[8,32,2048]{2,1,0:T(8,128)(2,1)}, u32[]{:S(2)}, u32[]{:S(2)}) collective-permute-start(bf16[8,32,2048]{2,1,0:T(8,128)(2,1)} %get-tuple-element.154), channel_id=1, source_target_pairs={{0,4},{2,6},{4,0},{6,2},{8,12},{10,14},{12,8},{14,10},{16,20},{18,... | collective-permute-start | bytes 3145736 | tf_op jit(solution)/shard_map/ppermute | solution.py:99
  240.5 34.1 %collective-permute-start.23 = (bf16[680,1024]{1,0:T(8,128)(2,1)}, bf16[680,1024]{1,0:T(8,128)(2,1)}, u32[]{:S(2)}, u32[]{:S(2)}) collective-permute-start(bf16[680,1024]{1,0:T(8,128)(2,1)} %get-tuple-element.162.refs_5_), channel_id=1, source_target_pairs={{0,2},{2,0},{4,6},{6,4},{8,10},{10,8},{12,14},{14,12},{16,18},{18,... | collective-permute-start | bytes 4177928 | tf_op jit(solution)/shard_map/ppermute | solution.py:99
  243.9 27.5 %collective-permute-start.19 = (bf16[4,32,2048]{2,1,0:T(8,128)(2,1)}, bf16[4,32,2048]{2,1,0:T(8,128)(2,1)}, u32[]{:S(2)}, u32[]{:S(2)}) collective-permute-start(bf16[4,32,2048]{2,1,0:T(8,128)(2,1)} %get-tuple-element.144.refs_11_), channel_id=1, source_target_pairs={{0,4},{2,6},{4,0},{6,2},{8,12},{10,14},{12,8},{14,10},{16,20},{18,... | collective-permute-start | bytes 1572872 | tf_op jit(solution)/shard_map/ppermute | solution.py:99
  245.4 26.0 %collective-permute-start.20 = (bf16[4,32,2048]{2,1,0:T(8,128)(2,1)}, bf16[4,32,2048]{2,1,0:T(8,128)(2,1)}, u32[]{:S(2)}, u32[]{:S(2)}) collective-permute-start(bf16[4,32,2048]{2,1,0:T(8,128)(2,1)} %get-tuple-element.146.refs_13_), channel_id=1, source_target_pairs={{0,1},{1,0},{2,3},{3,2},{4,5},{5,4},{6,7},{7,6},{8,9},{9,8},{10,11... | collective-permute-start | bytes 1572872 | tf_op jit(solution)/shard_map/ppermute | solution.py:99
  269.3 25.2 %collective-permute-start.27 = (bf16[4,32,2048]{2,1,0:T(8,128)(2,1)}, bf16[4,32,2048]{2,1,0:T(8,128)(2,1)}, u32[]{:S(2)}, u32[]{:S(2)}) collective-permute-start(bf16[4,32,2048]{2,1,0:T(8,128)(2,1)} %get-tuple-element.159.refs_14_), channel_id=1, source_target_pairs={{0,4},{2,6},{4,0},{6,2},{8,12},{10,14},{12,8},{14,10},{16,20},{18,... | collective-permute-start | bytes 1572872 | tf_op jit(solution)/shard_map/ppermute | solution.py:99
  270.6 23.9 %collective-permute-start.28 = (bf16[4,32,2048]{2,1,0:T(8,128)(2,1)}, bf16[4,32,2048]{2,1,0:T(8,128)(2,1)}, u32[]{:S(2)}, u32[]{:S(2)}) collective-permute-start(bf16[4,32,2048]{2,1,0:T(8,128)(2,1)} %get-tuple-element.161.refs_16_), channel_id=1, source_target_pairs={{0,1},{1,0},{2,3},{3,2},{4,5},{5,4},{6,7},{7,6},{8,9},{9,8},{10,11... | collective-permute-start | bytes 1572872 | tf_op jit(solution)/shard_map/ppermute | solution.py:99
  271.4 31.1 %collective-permute-start.25 = (bf16[3,680,512]{2,1,0:T(8,128)(2,1)}, bf16[3,680,512]{2,1,0:T(8,128)(2,1)}, u32[]{:S(2)}, u32[]{:S(2)}) collective-permute-start(bf16[3,680,512]{2,1,0:T(8,128)(2,1)} %get-tuple-element.147.refs_10_.refs_3_.refs_12_), channel_id=1, source_target_pairs={{0,2},{2,0},{4,6},{6,4},{8,10},{10,8},{12,14},{14,12},{16,18},{18,... | collective-permute-start | bytes 6266888 | tf_op jit(solution)/shard_map/ppermute | solution.py:99
  274.1 24.8 %collective-permute-start.26 = (bf16[2,64,2048]{2,1,0:T(8,128)(2,1)}, bf16[2,64,2048]{2,1,0:T(8,128)(2,1)}, u32[]{:S(2)}, u32[]{:S(2)}) collective-permute-start(bf16[2,64,2048]{2,1,0:T(8,128)(2,1)} %get-tuple-element.152.refs_12_), channel_id=1, source_target_pairs={{0,8},{2,10},{4,12},{6,14},{8,0},{10,2},{12,4},{14,6},{16,24},{18,... | collective-permute-start | bytes 1572872 | tf_op jit(solution)/shard_map/ppermute | solution.py:99
  294.5 19.2 %collective-permute-start.24 = (bf16[3,680,512]{2,1,0:T(8,128)(2,1)}, bf16[3,680,512]{2,1,0:T(8,128)(2,1)}, u32[]{:S(2)}, u32[]{:S(2)}) collective-permute-start(bf16[3,680,512]{2,1,0:T(8,128)(2,1)} %get-tuple-element.163.refs_9_.refs_3_.refs_13_), channel_id=1, source_target_pairs={{0,2},{2,0},{4,6},{6,4},{8,10},{10,8},{12,14},{14,12},{16,18},{18,... | collective-permute-start | bytes 6266888 | tf_op jit(solution)/shard_map/ppermute | solution.py:99
  297.3 23.7 %collective-permute-start.29 = (bf16[2,64,2048]{2,1,0:T(8,128)(2,1)}, bf16[2,64,2048]{2,1,0:T(8,128)(2,1)}, u32[]{:S(2)}, u32[]{:S(2)}) collective-permute-start(bf16[2,64,2048]{2,1,0:T(8,128)(2,1)} %get-tuple-element.171.refs_13_), channel_id=1, source_target_pairs={{0,8},{2,10},{4,12},{6,14},{8,0},{10,2},{12,4},{14,6},{16,24},{18,... | collective-permute-start | bytes 1572872 | tf_op jit(solution)/shard_map/ppermute | solution.py:99
  301.0 24.2 %collective-permute-start.30 = (bf16[1,64,2048]{2,1,0:T(8,128)(2,1)}, bf16[1,64,2048]{2,1,0:T(8,128)(2,1)}, u32[]{:S(2)}, u32[]{:S(2)}) collective-permute-start(bf16[1,64,2048]{2,1,0:T(8,128)(2,1)} %get-tuple-element.167.refs_11_), channel_id=1, source_target_pairs={{0,16},{2,18},{4,20},{6,22},{8,24},{10,26},{12,28},{14,30},{16,0},... | collective-permute-start | bytes 786440 | tf_op jit(solution)/shard_map/ppermute | solution.py:99
  311.7 26.4 %collective-permute-start.31 = (bf16[8,32,1280]{2,1,0:T(8,128)(2,1)}, bf16[8,32,1280]{2,1,0:T(8,128)(2,1)}, u32[]{:S(2)}, u32[]{:S(2)}) collective-permute-start(bf16[8,32,1280]{2,1,0:T(8,128)(2,1)} %get-tuple-element.179), channel_id=1, source_target_pairs={{0,1},{1,0},{2,3},{3,2},{4,5},{5,4},{6,7},{7,6},{8,9},{9,8},{10,11... | collective-permute-start | bytes 1966088 | tf_op jit(solution)/shard_map/ppermute | solution.py:99
  313.0 25.1 %collective-permute-start.32 = (bf16[8,32,1280]{2,1,0:T(8,128)(2,1)}, bf16[8,32,1280]{2,1,0:T(8,128)(2,1)}, u32[]{:S(2)}, u32[]{:S(2)}) collective-permute-start(bf16[8,32,1280]{2,1,0:T(8,128)(2,1)} %get-tuple-element.180), channel_id=1, source_target_pairs={{0,4},{2,6},{4,0},{6,2},{8,12},{10,14},{12,8},{14,10},{16,20},{18,... | collective-permute-start | bytes 1966088 | tf_op jit(solution)/shard_map/ppermute | solution.py:99
  365.0 24.8 %all-to-all-start.2 = ((bf16[32,2,3712]{2,1,0:T(2,128)(2,1)}), bf16[32,2,3712]{2,1,0:T(2,128)(2,1)S(1)}, u32[]{:S(2)}, u32[]{:S(2)}) async-start(bf16[32,2,3712]{2,1,0:T(2,128)(2,1)} %reshape.258), calls=%async_computation.2 | async-start | bytes 950272 | tf_op jit(solution)/shard_map/all_to_all | solution.py:845
  374.2 19.8 %collective-permute-start.39 = (bf16[1,64,2048]{2,1,0:T(8,128)(2,1)}, bf16[1,64,2048]{2,1,0:T(8,128)(2,1)S(1)}, u32[]{:S(2)}, u32[]{:S(2)}) collective-permute-start(bf16[1,64,2048]{2,1,0:T(8,128)(2,1)} %get-tuple-element.205), channel_id=1, source_target_pairs={{0,16},{2,18},{4,20},{6,22},{8,24},{10,26},{12,28},{14,30},{16,0},... | collective-permute-start | bytes 786440 | tf_op jit(solution)/shard_map/ppermute | solution.py:99
  (44 other events, 707.7 us)
Sparse Core Ops, SparseCore 0:
  27.4 134.7 all-gather.1
